TPU v7x, 128 devices: a whole 4x4x4 slice. The times are simulated.
128 devices in a mesh: slab: 32 (over z_lo, x, y), energy: 4 (over z_hi, core).
Axes of the slice: x: 4, y: 4, z: 4 (z_hi: 2, z_lo: 2; z = z_hi * 2 + z_lo), core: 2. Of those that a mesh axis runs over, the one named last changes fastest.
Arguments:
- onsite: float32 [32, 256, 256], P('slab'), may hold values from -1.4 to 0.3, as said below
- coupling: float32 [32, 256, 256], P('slab'), may hold values from -0.25 to 1.6
- pattern: int32 [32, 4, 4], P('slab'), may hold values 0 or 1
- contact_rates: float32 [2, 256], replicated, may hold values from 1 to 3
- energy_index: int32 [16], P('energy'), parts along dimension 0, may hold values from 0 to 31
Outputs:
- spectral: float32 [32, 16, 256], P('slab', 'energy'), parts along dimension 1
- transmission: float32 [16], P('energy'), parts along dimension 0
There are 4 independent parts, one for each index of `energy`. A program takes and returns all parts, laid end to end along the dimension named above; an argument that names none is the same for every part. Nothing has to cross between parts.
Inputs may be any that keep to these rules, and one draw needn't show every extreme that they name: Every onsite block is symmetric.
All inputs are finite; a program needn't handle non-finite values. No bound on the sum of `pattern` on one device may be relied on, other than what follows from the above.
Results may differ from a plain program's by a relative error of at most 0.00012.
Values sent between devices are 32-bit elements; how exact they have to be, the bound alone decides.
No kernel may reach another device: no remote copies, remote signals or barrier semaphores. Data moves between devices by JAX's collectives and lax.ppermute only.
A program may use at most 64 MiB of HBM per device.

v0:
```python
import jax
import jax.numpy as jnp
from jax import lax
from jax.sharding import PartitionSpec as P

energy_floor = -0.2
energy_spacing = 0.0125
broadening = 0.3
highest = lax.Precision.HIGHEST


def passed_along(value, axis, steps):
    count = lax.axis_size(axis)
    initial, last = (max(0, -steps), min(count, count - steps))
    return lax.ppermute(value, axis, [(source, source + steps) for source in range(initial, last)])


def product(left_factor, right_factor):
    return jnp.dot(left_factor, right_factor, preferred_element_type=jnp.float32, precision=highest)


def complex_product(left_factor, right_factor):
    real_real = product(left_factor[0], right_factor[0])
    imag_imag = product(left_factor[1], right_factor[1])
    summed = product(left_factor[0] + left_factor[1], right_factor[0] + right_factor[1])
    return jnp.stack([real_real - imag_imag, summed - real_real - imag_imag])


def schur_after(coupling_block, greens):
    halfway = jnp.stack([product(greens[0], coupling_block), product(greens[1], coupling_block)])
    transposed = coupling_block.T
    return jnp.stack([product(transposed, halfway[0]), product(transposed, halfway[1])])


def schur_before(coupling_block, greens):
    transposed = coupling_block.T
    halfway = jnp.stack([product(greens[0], transposed), product(greens[1], transposed)])
    return jnp.stack([product(coupling_block, halfway[0]), product(coupling_block, halfway[1])])


def invert(matrix):
    orbitals = matrix.shape[1]
    diag_real = jnp.diagonal(matrix[0])
    diag_imag = jnp.diagonal(matrix[1])
    modulus = diag_real * diag_real + diag_imag * diag_imag
    start_real = diag_real / modulus
    start_imag = -diag_imag / modulus
    identity = jnp.eye(orbitals, dtype=jnp.float32)
    applied_real = matrix[0] * start_real[None, :] - matrix[1] * start_imag[None, :]
    applied_imag = matrix[0] * start_imag[None, :] + matrix[1] * start_real[None, :]
    scaled_real = start_real[:, None] * applied_real - start_imag[:, None] * applied_imag
    scaled_imag = start_real[:, None] * applied_imag + start_imag[:, None] * applied_real
    approx = jnp.stack(
        [
            2.0 * identity * start_real[None, :] - scaled_real,
            2.0 * identity * start_imag[None, :] - scaled_imag,
        ]
    )
    applied = complex_product(matrix, approx)
    approx = 2.0 * approx - complex_product(approx, applied)
    return approx


def green_block(energy, onsite_block, self_energy):
    identity = jnp.eye(onsite_block.shape[0], dtype=jnp.float32)
    real_part = energy * identity - onsite_block - self_energy[0]
    imag_part = broadening * identity - self_energy[1]
    return invert(jnp.stack([real_part, imag_part]))


def spectral_row(greens):
    return -2.0 * jnp.diagonal(greens[1])


def transmitted(left_energy, right_energy, greens):
    gamma_left = -2.0 * left_energy[1]
    gamma_right = -2.0 * right_energy[1]
    forward_real = product(gamma_left, greens[0])
    forward_imag = product(gamma_left, greens[1])
    backward_real = product(gamma_right, greens[0].T)
    backward_imag = -product(gamma_right, greens[1].T)
    return jnp.sum(forward_real * backward_real.T) - jnp.sum(forward_imag * backward_imag.T)


def contact_energy(rates):
    identity = jnp.eye(rates.shape[0], dtype=jnp.float32)
    return jnp.stack([jnp.zeros_like(identity), identity * (-0.5 * rates)[None, :]])


def mask_coupling(coupling, pattern):
    slab_count = coupling.shape[0]
    orbitals = coupling.shape[1]
    tile_count = pattern.shape[1]
    tile_size = orbitals // tile_count
    blocks = coupling.reshape(slab_count, tile_count, tile_size, tile_count, tile_size)
    blocks = blocks * pattern.astype(jnp.float32)[:, :, None, :, None]
    return blocks.reshape(slab_count, orbitals, orbitals)


def on_device(onsite, coupling, pattern, contact_rates, energy_index):
    slab_count = onsite.shape[0]
    orbitals = onsite.shape[1]
    masked = mask_coupling(coupling, pattern)
    sections = lax.axis_size("slab")
    device = lax.axis_index("slab")
    energy_count = energy_index.shape[0]
    batch_size = 1
    rounds = energy_count // batch_size
    energy_flat = energy_floor + energy_spacing * energy_index.astype(jnp.float32)
    energies = energy_flat.reshape(rounds, batch_size)
    left_contact = contact_energy(contact_rates[0])
    right_contact = contact_energy(contact_rates[1])
    lower_onsite = onsite[1:][::-1]
    lower_coupling = masked[: slab_count - 1][::-1]
    last_coupling = masked[slab_count - 1]

    def left_work(energy, incoming):
        start_energy = jnp.where(device == 0, left_contact, incoming)

        def left_step(carried, pieces):
            greens = green_block(energy, pieces[0], carried)
            return (schur_after(pieces[1], greens), carried)

        return lax.scan(left_step, start_energy, (onsite, masked))

    def right_work(energy, incoming):
        start_energy = jnp.where(
            device == sections - 1, right_contact, schur_before(last_coupling, incoming)
        )

        def right_step(carried, pieces):
            greens = green_block(energy, pieces[0], carried)
            return (schur_before(pieces[1], greens), carried)

        lowest_energy, uppers = lax.scan(right_step, start_energy, (lower_onsite, lower_coupling))
        entering = jnp.concatenate([lowest_energy[None], uppers[::-1]], axis=0)
        return (green_block(energy, onsite[0], lowest_energy), entering)

    def handle(position, work, incoming, outgoing, store):
        active = (position >= 0) & (position < rounds)
        clipped = jnp.clip(position, 0, rounds - 1)
        energy_now = lax.dynamic_index_in_dim(energies, clipped, 0, keepdims=False)

        def working(unused):
            return jax.vmap(work)(energy_now, incoming)

        def resting(unused):
            return (
                jnp.zeros_like(outgoing),
                jnp.zeros((batch_size, slab_count, 2, orbitals, orbitals), jnp.float32),
            )

        sending, entering = lax.cond(active, working, resting, None)
        previous = lax.dynamic_index_in_dim(store, clipped, 0, keepdims=False)
        store = lax.dynamic_update_index_in_dim(
            store, jnp.where(active, entering, previous), clipped, 0
        )
        return (sending, store)

    def advance(step_index, carry):
        out_left, out_right, left_store, right_store = carry
        from_left = passed_along(out_left, "slab", 1)
        from_right = passed_along(out_right, "slab", -1)
        out_left, left_store = handle(
            step_index - device, left_work, from_left, out_left, left_store
        )
        out_right, right_store = handle(
            step_index - (sections - 1 - device), right_work, from_right, out_right, right_store
        )
        return (out_left, out_right, left_store, right_store)

    boundary = jnp.zeros((batch_size, 2, orbitals, orbitals), jnp.float32)
    store = jnp.zeros((rounds, batch_size, slab_count, 2, orbitals, orbitals), jnp.float32)
    results = lax.fori_loop(0, sections - 1 + rounds, advance, (boundary, boundary, store, store))
    lefts = results[2].reshape(energy_count, slab_count, 2, orbitals, orbitals)
    rights = results[3].reshape(energy_count, slab_count, 2, orbitals, orbitals)

    def finish(pieces):
        energy, left_part, right_part = pieces

        def slab_greens(onsite_block, self_energy):
            return green_block(energy, onsite_block, self_energy)

        greens = jax.vmap(slab_greens)(onsite, left_part + right_part)
        spectra = jax.vmap(spectral_row)(greens)
        crossing = transmitted(left_part[0], right_part[0], greens[0])
        return (spectra, crossing)

    spectra, crossing = lax.map(finish, (energy_flat, lefts, rights))
    crossing = jnp.where(device == sections // 2, crossing, jnp.zeros_like(crossing))
    crossing = lax.psum(crossing, "slab")
    return (jnp.transpose(spectra, (1, 0, 2)), crossing)


def solution(mesh):
    return jax.shard_map(
        on_device,
        mesh=mesh,
        in_specs=(
            P("slab", None, None),
            P("slab", None, None),
            P("slab", None, None),
            P(),
            P("energy"),
        ),
        out_specs=(P("slab", "energy", None), P("energy")),
        check_vma=False,
    )
```

profile of v0, /device:TPU:64, one launch (start us, length us, event | category | flops | bytes accessed | tf_op | source)
XLA Modules:
  0.0 1378.6 jit_solution(396930352567652758)
XLA Ops:
  10.6 1150.8 %while.39 = (s32[]{:T(128)}, f32[1,2,256,256]{2,3,1,0:T(8,128)}, f32[1,2,256,256]{2,3,1,0:T(8,128)}, f32[4,1,1,2,256,256]{5,4,3,2,1,0:T(8,128)}, f32[4,1,1,2,256...) while((s32[]{:T(128)}, f32[1,2,256,256]{2,3,1,0:T(8,128)}, ...), condition=%wide.region_5.6_spmd.clone, body=%wide.region_0.5_spmd.sunk.clone | while | flops 4034008064 | bytes 57708160 | solution.py:174
  30.9 11.8 conditional.6
  62.8 11.8 conditional.6
  95.2 11.8 conditional.6
  126.7 11.8 conditional.6
  163.6 17.8 %collective-permute-start = (f32[1,2,256,256]{3,2,1,0:T(8,128)}, f32[1,2,256,256]{3,2,1,0:T(8,128)}, u32[]{:S(2)}, u32[]{:S(2)}) collective-permute-start(f32[1,2,256,256]{3,2,1,0:T(8,128)} %copy.53), channel_id=1, source_target_pairs={{0,4},{4,8},{8,12},{12,16},{16,20},{20,24},{24,28},{28,32},{32,36}... | collective-permute-start | bytes 1572872 | tf_op jit(solution)/shard_map/while/body/eval_jaxpr/ppermute | solution.py:15
  212.4 17.4 %collective-permute-start = (f32[1,2,256,256]{3,2,1,0:T(8,128)}, f32[1,2,256,256]{3,2,1,0:T(8,128)}, u32[]{:S(2)}, u32[]{:S(2)}) collective-permute-start(f32[1,2,256,256]{3,2,1,0:T(8,128)} %copy.53), channel_id=1, source_target_pairs={{0,4},{4,8},{8,12},{12,16},{16,20},{20,24},{24,28},{28,32},{32,36}... | collective-permute-start | bytes 1572872 | tf_op jit(solution)/shard_map/while/body/eval_jaxpr/ppermute | solution.py:15
  262.8 19.9 %collective-permute-start = (f32[1,2,256,256]{3,2,1,0:T(8,128)}, f32[1,2,256,256]{3,2,1,0:T(8,128)}, u32[]{:S(2)}, u32[]{:S(2)}) collective-permute-start(f32[1,2,256,256]{3,2,1,0:T(8,128)} %copy.53), channel_id=1, source_target_pairs={{0,4},{4,8},{8,12},{12,16},{16,20},{20,24},{24,28},{28,32},{32,36}... | collective-permute-start | bytes 1572872 | tf_op jit(solution)/shard_map/while/body/eval_jaxpr/ppermute | solution.py:15
  315.7 19.9 %collective-permute-start = (f32[1,2,256,256]{3,2,1,0:T(8,128)}, f32[1,2,256,256]{3,2,1,0:T(8,128)}, u32[]{:S(2)}, u32[]{:S(2)}) collective-permute-start(f32[1,2,256,256]{3,2,1,0:T(8,128)} %copy.53), channel_id=1, source_target_pairs={{0,4},{4,8},{8,12},{12,16},{16,20},{20,24},{24,28},{28,32},{32,36}... | collective-permute-start | bytes 1572872 | tf_op jit(solution)/shard_map/while/body/eval_jaxpr/ppermute | solution.py:15
  368.7 17.1 %collective-permute-start = (f32[1,2,256,256]{3,2,1,0:T(8,128)}, f32[1,2,256,256]{3,2,1,0:T(8,128)}, u32[]{:S(2)}, u32[]{:S(2)}) collective-permute-start(f32[1,2,256,256]{3,2,1,0:T(8,128)} %copy.53), channel_id=1, source_target_pairs={{0,4},{4,8},{8,12},{12,16},{16,20},{20,24},{24,28},{28,32},{32,36}... | collective-permute-start | bytes 1572872 | tf_op jit(solution)/shard_map/while/body/eval_jaxpr/ppermute | solution.py:15
  418.5 30.6 %collective-permute-start = (f32[1,2,256,256]{3,2,1,0:T(8,128)}, f32[1,2,256,256]{3,2,1,0:T(8,128)}, u32[]{:S(2)}, u32[]{:S(2)}) collective-permute-start(f32[1,2,256,256]{3,2,1,0:T(8,128)} %copy.53), channel_id=1, source_target_pairs={{0,4},{4,8},{8,12},{12,16},{16,20},{20,24},{24,28},{28,32},{32,36}... | collective-permute-start | bytes 1572872 | tf_op jit(solution)/shard_map/while/body/eval_jaxpr/ppermute | solution.py:15
  538.8 21.6 %collective-permute-start = (f32[1,2,256,256]{3,2,1,0:T(8,128)}, f32[1,2,256,256]{3,2,1,0:T(8,128)}, u32[]{:S(2)}, u32[]{:S(2)}) collective-permute-start(f32[1,2,256,256]{3,2,1,0:T(8,128)} %copy.53), channel_id=1, source_target_pairs={{0,4},{4,8},{8,12},{12,16},{16,20},{20,24},{24,28},{28,32},{32,36}... | collective-permute-start | bytes 1572872 | tf_op jit(solution)/shard_map/while/body/eval_jaxpr/ppermute | solution.py:15
  655.8 25.7 %collective-permute-start = (f32[1,2,256,256]{3,2,1,0:T(8,128)}, f32[1,2,256,256]{3,2,1,0:T(8,128)}, u32[]{:S(2)}, u32[]{:S(2)}) collective-permute-start(f32[1,2,256,256]{3,2,1,0:T(8,128)} %copy.53), channel_id=1, source_target_pairs={{0,4},{4,8},{8,12},{12,16},{16,20},{20,24},{24,28},{28,32},{32,36}... | collective-permute-start | bytes 1572872 | tf_op jit(solution)/shard_map/while/body/eval_jaxpr/ppermute | solution.py:15
  714.5 20.9 %collective-permute-start = (f32[1,2,256,256]{3,2,1,0:T(8,128)}, f32[1,2,256,256]{3,2,1,0:T(8,128)}, u32[]{:S(2)}, u32[]{:S(2)}) collective-permute-start(f32[1,2,256,256]{3,2,1,0:T(8,128)} %copy.53), channel_id=1, source_target_pairs={{0,4},{4,8},{8,12},{12,16},{16,20},{20,24},{24,28},{28,32},{32,36}... | collective-permute-start | bytes 1572872 | tf_op jit(solution)/shard_map/while/body/eval_jaxpr/ppermute | solution.py:15
  768.5 10.2 collective-permute-start
  791.2 7.9 collective-permute-start
  832.2 187.0 %collective-permute-start = (f32[1,2,256,256]{3,2,1,0:T(8,128)}, f32[1,2,256,256]{3,2,1,0:T(8,128)}, u32[]{:S(2)}, u32[]{:S(2)}) collective-permute-start(f32[1,2,256,256]{3,2,1,0:T(8,128)} %copy.53), channel_id=1, source_target_pairs={{0,4},{4,8},{8,12},{12,16},{16,20},{20,24},{24,28},{28,32},{32,36}... | collective-permute-start | bytes 1572872 | tf_op jit(solution)/shard_map/while/body/eval_jaxpr/ppermute | solution.py:15
  1026.2 14.1 %conditional.7 = (f32[1,2,256,256]{2,3,1,0:T(8,128)}, f32[1,1,2,256,256]{3,4,2,1,0:T(8,128)S(1)}) conditional(s32[]{:T(128)} %convert_element_type.44, () %tuple.108, (f32[4,1]{0,1:T(1,128)S(1)}, s32[]{:T(128)}, f32[1,256,256]{1,2,0:T(8,128)}, s32[]{:T(128)}, f32[1,2,256,256]{3,2,1,0:T(8,128)S(1)}, /*index=5*/f32[256,256]{1,0:T(8,128)S(1)}, ...), branch_computations={%region_3.3_spmd, %region_4.4_spmd} | conditional | flops 2016872960 | bytes 17318954 | solution.py:153
  1062.4 14.1 %conditional.7 = (f32[1,2,256,256]{2,3,1,0:T(8,128)}, f32[1,1,2,256,256]{3,4,2,1,0:T(8,128)S(1)}) conditional(s32[]{:T(128)} %convert_element_type.44, () %tuple.108, (f32[4,1]{0,1:T(1,128)S(1)}, s32[]{:T(128)}, f32[1,256,256]{1,2,0:T(8,128)}, s32[]{:T(128)}, f32[1,2,256,256]{3,2,1,0:T(8,128)S(1)}, /*index=5*/f32[256,256]{1,0:T(8,128)S(1)}, ...), branch_computations={%region_3.3_spmd, %region_4.4_spmd} | conditional | flops 2016872960 | bytes 17318954 | solution.py:153
  1084.0 25.5 %collective-permute-start = (f32[1,2,256,256]{3,2,1,0:T(8,128)}, f32[1,2,256,256]{3,2,1,0:T(8,128)}, u32[]{:S(2)}, u32[]{:S(2)}) collective-permute-start(f32[1,2,256,256]{3,2,1,0:T(8,128)} %copy.53), channel_id=1, source_target_pairs={{0,4},{4,8},{8,12},{12,16},{16,20},{20,24},{24,28},{28,32},{32,36}... | collective-permute-start | bytes 1572872 | tf_op jit(solution)/shard_map/while/body/eval_jaxpr/ppermute | solution.py:15
  1115.0 14.1 %conditional.7 = (f32[1,2,256,256]{2,3,1,0:T(8,128)}, f32[1,1,2,256,256]{3,4,2,1,0:T(8,128)S(1)}) conditional(s32[]{:T(128)} %convert_element_type.44, () %tuple.108, (f32[4,1]{0,1:T(1,128)S(1)}, s32[]{:T(128)}, f32[1,256,256]{1,2,0:T(8,128)}, s32[]{:T(128)}, f32[1,2,256,256]{3,2,1,0:T(8,128)S(1)}, /*index=5*/f32[256,256]{1,0:T(8,128)S(1)}, ...), branch_computations={%region_3.3_spmd, %region_4.4_spmd} | conditional | flops 2016872960 | bytes 17318954 | solution.py:153
  1144.4 14.1 %conditional.7 = (f32[1,2,256,256]{2,3,1,0:T(8,128)}, f32[1,1,2,256,256]{3,4,2,1,0:T(8,128)S(1)}) conditional(s32[]{:T(128)} %convert_element_type.44, () %tuple.108, (f32[4,1]{0,1:T(1,128)S(1)}, s32[]{:T(128)}, f32[1,256,256]{1,2,0:T(8,128)}, s32[]{:T(128)}, f32[1,2,256,256]{3,2,1,0:T(8,128)S(1)}, /*index=5*/f32[256,256]{1,0:T(8,128)S(1)}, ...), branch_computations={%region_3.3_spmd, %region_4.4_spmd} | conditional | flops 2016872960 | bytes 17318954 | solution.py:153
  1161.4 89.4 %while.40 = (s32[]{:T(128)}, f32[4,1,256]{2,0,1:T(4,128)S(1)}, f32[4]{0:T(128)S(1)}, f32[4]{0:T(128)S(1)}, f32[1,256,256]{2,1,0:T(8,128)S(1)}, /*index=5*/f32[4,1,2,256,256]{4,3,2,1,0:T(8,128)}, f32[4,1,2,256,256]{4,3,2,1,0:T(8,128)}) while((s32[]{:T(128)}, f32[4,1,256]{2,0,1:T(4,128)S(1)}, f32[4]{0:T(128)S(1)}, f32[4]{0:T(128)S(1)}, ...), condition=%wide.region_9.10_spmd.clone, body=%wide.region_6.9_spmd.sunk.clone | while | flops 2020936448 | bytes 21011624 | solution.py:189
  1250.9 127.7 %psum.7 = f32[4]{0:T(128)} all-reduce(f32[4]{0:T(128)S(1)} %broadcast_select_fusion), channel_id=1, replica_groups=mesh['slab'=32,'energy'=4] {'slab'}, use_global_device_ids=true, to_apply=%region_10.11 | all-reduce | flops 4 | bytes 32 | tf_op jit(solution)/shard_map/psum | solution.py:191
  (1089 shorter events, 871.7 us)
Async XLA Ops:
  160.3 23.6 %collective-permute-start.1 = (f32[1,2,256,256]{3,2,1,0:T(8,128)S(1)}, f32[1,2,256,256]{3,2,1,0:T(8,128)S(1)}, u32[]{:S(2)}, u32[]{:S(2)}) collective-permute-start(f32[1,2,256,256]{3,2,1,0:T(8,128)S(1)} %copy.54), channel_id=1, source_target_pairs={{4,0},{8,4},{12,8},{16,12},{20,16},{24,20},{28,24},{32,28},{36,32}... | collective-permute-start | bytes 1572872 | tf_op jit(solution)/shard_map/while/body/eval_jaxpr/ppermute | solution.py:15
  163.6 24.0 %collective-permute-start = (f32[1,2,256,256]{3,2,1,0:T(8,128)}, f32[1,2,256,256]{3,2,1,0:T(8,128)}, u32[]{:S(2)}, u32[]{:S(2)}) collective-permute-start(f32[1,2,256,256]{3,2,1,0:T(8,128)} %copy.53), channel_id=1, source_target_pairs={{0,4},{4,8},{8,12},{12,16},{16,20},{20,24},{24,28},{28,32},{32,36}... | collective-permute-start | bytes 1572872 | tf_op jit(solution)/shard_map/while/body/eval_jaxpr/ppermute | solution.py:15
  209.0 23.1 %collective-permute-start.1 = (f32[1,2,256,256]{3,2,1,0:T(8,128)S(1)}, f32[1,2,256,256]{3,2,1,0:T(8,128)S(1)}, u32[]{:S(2)}, u32[]{:S(2)}) collective-permute-start(f32[1,2,256,256]{3,2,1,0:T(8,128)S(1)} %copy.54), channel_id=1, source_target_pairs={{4,0},{8,4},{12,8},{16,12},{20,16},{24,20},{28,24},{32,28},{36,32}... | collective-permute-start | bytes 1572872 | tf_op jit(solution)/shard_map/while/body/eval_jaxpr/ppermute | solution.py:15
  212.4 23.6 %collective-permute-start = (f32[1,2,256,256]{3,2,1,0:T(8,128)}, f32[1,2,256,256]{3,2,1,0:T(8,128)}, u32[]{:S(2)}, u32[]{:S(2)}) collective-permute-start(f32[1,2,256,256]{3,2,1,0:T(8,128)} %copy.53), channel_id=1, source_target_pairs={{0,4},{4,8},{8,12},{12,16},{16,20},{20,24},{24,28},{28,32},{32,36}... | collective-permute-start | bytes 1572872 | tf_op jit(solution)/shard_map/while/body/eval_jaxpr/ppermute | solution.py:15
  259.4 25.6 %collective-permute-start.1 = (f32[1,2,256,256]{3,2,1,0:T(8,128)S(1)}, f32[1,2,256,256]{3,2,1,0:T(8,128)S(1)}, u32[]{:S(2)}, u32[]{:S(2)}) collective-permute-start(f32[1,2,256,256]{3,2,1,0:T(8,128)S(1)} %copy.54), channel_id=1, source_target_pairs={{4,0},{8,4},{12,8},{16,12},{20,16},{24,20},{28,24},{32,28},{36,32}... | collective-permute-start | bytes 1572872 | tf_op jit(solution)/shard_map/while/body/eval_jaxpr/ppermute | solution.py:15
  262.8 26.1 %collective-permute-start = (f32[1,2,256,256]{3,2,1,0:T(8,128)}, f32[1,2,256,256]{3,2,1,0:T(8,128)}, u32[]{:S(2)}, u32[]{:S(2)}) collective-permute-start(f32[1,2,256,256]{3,2,1,0:T(8,128)} %copy.53), channel_id=1, source_target_pairs={{0,4},{4,8},{8,12},{12,16},{16,20},{20,24},{24,28},{28,32},{32,36}... | collective-permute-start | bytes 1572872 | tf_op jit(solution)/shard_map/while/body/eval_jaxpr/ppermute | solution.py:15
  312.4 25.7 %collective-permute-start.1 = (f32[1,2,256,256]{3,2,1,0:T(8,128)S(1)}, f32[1,2,256,256]{3,2,1,0:T(8,128)S(1)}, u32[]{:S(2)}, u32[]{:S(2)}) collective-permute-start(f32[1,2,256,256]{3,2,1,0:T(8,128)S(1)} %copy.54), channel_id=1, source_target_pairs={{4,0},{8,4},{12,8},{16,12},{20,16},{24,20},{28,24},{32,28},{36,32}... | collective-permute-start | bytes 1572872 | tf_op jit(solution)/shard_map/while/body/eval_jaxpr/ppermute | solution.py:15
  315.7 26.1 %collective-permute-start = (f32[1,2,256,256]{3,2,1,0:T(8,128)}, f32[1,2,256,256]{3,2,1,0:T(8,128)}, u32[]{:S(2)}, u32[]{:S(2)}) collective-permute-start(f32[1,2,256,256]{3,2,1,0:T(8,128)} %copy.53), channel_id=1, source_target_pairs={{0,4},{4,8},{8,12},{12,16},{16,20},{20,24},{24,28},{28,32},{32,36}... | collective-permute-start | bytes 1572872 | tf_op jit(solution)/shard_map/while/body/eval_jaxpr/ppermute | solution.py:15
  365.3 24.4 %collective-permute-start.1 = (f32[1,2,256,256]{3,2,1,0:T(8,128)S(1)}, f32[1,2,256,256]{3,2,1,0:T(8,128)S(1)}, u32[]{:S(2)}, u32[]{:S(2)}) collective-permute-start(f32[1,2,256,256]{3,2,1,0:T(8,128)S(1)} %copy.54), channel_id=1, source_target_pairs={{4,0},{8,4},{12,8},{16,12},{20,16},{24,20},{28,24},{32,28},{36,32}... | collective-permute-start | bytes 1572872 | tf_op jit(solution)/shard_map/while/body/eval_jaxpr/ppermute | solution.py:15
  368.7 25.1 %collective-permute-start = (f32[1,2,256,256]{3,2,1,0:T(8,128)}, f32[1,2,256,256]{3,2,1,0:T(8,128)}, u32[]{:S(2)}, u32[]{:S(2)}) collective-permute-start(f32[1,2,256,256]{3,2,1,0:T(8,128)} %copy.53), channel_id=1, source_target_pairs={{0,4},{4,8},{8,12},{12,16},{16,20},{20,24},{24,28},{28,32},{32,36}... | collective-permute-start | bytes 1572872 | tf_op jit(solution)/shard_map/while/body/eval_jaxpr/ppermute | solution.py:15
  415.2 41.9 %collective-permute-start.1 = (f32[1,2,256,256]{3,2,1,0:T(8,128)S(1)}, f32[1,2,256,256]{3,2,1,0:T(8,128)S(1)}, u32[]{:S(2)}, u32[]{:S(2)}) collective-permute-start(f32[1,2,256,256]{3,2,1,0:T(8,128)S(1)} %copy.54), channel_id=1, source_target_pairs={{4,0},{8,4},{12,8},{16,12},{20,16},{24,20},{28,24},{32,28},{36,32}... | collective-permute-start | bytes 1572872 | tf_op jit(solution)/shard_map/while/body/eval_jaxpr/ppermute | solution.py:15
  418.5 42.1 %collective-permute-start = (f32[1,2,256,256]{3,2,1,0:T(8,128)}, f32[1,2,256,256]{3,2,1,0:T(8,128)}, u32[]{:S(2)}, u32[]{:S(2)}) collective-permute-start(f32[1,2,256,256]{3,2,1,0:T(8,128)} %copy.53), channel_id=1, source_target_pairs={{0,4},{4,8},{8,12},{12,16},{16,20},{20,24},{24,28},{28,32},{32,36}... | collective-permute-start | bytes 1572872 | tf_op jit(solution)/shard_map/while/body/eval_jaxpr/ppermute | solution.py:15
  535.4 31.0 %collective-permute-start.1 = (f32[1,2,256,256]{3,2,1,0:T(8,128)S(1)}, f32[1,2,256,256]{3,2,1,0:T(8,128)S(1)}, u32[]{:S(2)}, u32[]{:S(2)}) collective-permute-start(f32[1,2,256,256]{3,2,1,0:T(8,128)S(1)} %copy.54), channel_id=1, source_target_pairs={{4,0},{8,4},{12,8},{16,12},{20,16},{24,20},{28,24},{32,28},{36,32}... | collective-permute-start | bytes 1572872 | tf_op jit(solution)/shard_map/while/body/eval_jaxpr/ppermute | solution.py:15
  538.8 31.2 %collective-permute-start = (f32[1,2,256,256]{3,2,1,0:T(8,128)}, f32[1,2,256,256]{3,2,1,0:T(8,128)}, u32[]{:S(2)}, u32[]{:S(2)}) collective-permute-start(f32[1,2,256,256]{3,2,1,0:T(8,128)} %copy.53), channel_id=1, source_target_pairs={{0,4},{4,8},{8,12},{12,16},{16,20},{20,24},{24,28},{28,32},{32,36}... | collective-permute-start | bytes 1572872 | tf_op jit(solution)/shard_map/while/body/eval_jaxpr/ppermute | solution.py:15
  652.5 31.4 %collective-permute-start.1 = (f32[1,2,256,256]{3,2,1,0:T(8,128)S(1)}, f32[1,2,256,256]{3,2,1,0:T(8,128)S(1)}, u32[]{:S(2)}, u32[]{:S(2)}) collective-permute-start(f32[1,2,256,256]{3,2,1,0:T(8,128)S(1)} %copy.54), channel_id=1, source_target_pairs={{4,0},{8,4},{12,8},{16,12},{20,16},{24,20},{28,24},{32,28},{36,32}... | collective-permute-start | bytes 1572872 | tf_op jit(solution)/shard_map/while/body/eval_jaxpr/ppermute | solution.py:15
  655.8 31.8 %collective-permute-start = (f32[1,2,256,256]{3,2,1,0:T(8,128)}, f32[1,2,256,256]{3,2,1,0:T(8,128)}, u32[]{:S(2)}, u32[]{:S(2)}) collective-permute-start(f32[1,2,256,256]{3,2,1,0:T(8,128)} %copy.53), channel_id=1, source_target_pairs={{0,4},{4,8},{8,12},{12,16},{16,20},{20,24},{24,28},{28,32},{32,36}... | collective-permute-start | bytes 1572872 | tf_op jit(solution)/shard_map/while/body/eval_jaxpr/ppermute | solution.py:15
  711.2 26.7 %collective-permute-start.1 = (f32[1,2,256,256]{3,2,1,0:T(8,128)S(1)}, f32[1,2,256,256]{3,2,1,0:T(8,128)S(1)}, u32[]{:S(2)}, u32[]{:S(2)}) collective-permute-start(f32[1,2,256,256]{3,2,1,0:T(8,128)S(1)} %copy.54), channel_id=1, source_target_pairs={{4,0},{8,4},{12,8},{16,12},{20,16},{24,20},{28,24},{32,28},{36,32}... | collective-permute-start | bytes 1572872 | tf_op jit(solution)/shard_map/while/body/eval_jaxpr/ppermute | solution.py:15
  714.5 27.1 %collective-permute-start = (f32[1,2,256,256]{3,2,1,0:T(8,128)}, f32[1,2,256,256]{3,2,1,0:T(8,128)}, u32[]{:S(2)}, u32[]{:S(2)}) collective-permute-start(f32[1,2,256,256]{3,2,1,0:T(8,128)} %copy.53), channel_id=1, source_target_pairs={{0,4},{4,8},{8,12},{12,16},{16,20},{20,24},{24,28},{28,32},{32,36}... | collective-permute-start | bytes 1572872 | tf_op jit(solution)/shard_map/while/body/eval_jaxpr/ppermute | solution.py:15
  828.8 197.4 %collective-permute-start.1 = (f32[1,2,256,256]{3,2,1,0:T(8,128)S(1)}, f32[1,2,256,256]{3,2,1,0:T(8,128)S(1)}, u32[]{:S(2)}, u32[]{:S(2)}) collective-permute-start(f32[1,2,256,256]{3,2,1,0:T(8,128)S(1)} %copy.54), channel_id=1, source_target_pairs={{4,0},{8,4},{12,8},{16,12},{20,16},{24,20},{28,24},{32,28},{36,32}... | collective-permute-start | bytes 1572872 | tf_op jit(solution)/shard_map/while/body/eval_jaxpr/ppermute | solution.py:15
  832.2 209.2 %collective-permute-start = (f32[1,2,256,256]{3,2,1,0:T(8,128)}, f32[1,2,256,256]{3,2,1,0:T(8,128)}, u32[]{:S(2)}, u32[]{:S(2)}) collective-permute-start(f32[1,2,256,256]{3,2,1,0:T(8,128)} %copy.53), channel_id=1, source_target_pairs={{0,4},{4,8},{8,12},{12,16},{16,20},{20,24},{24,28},{28,32},{32,36}... | collective-permute-start | bytes 1572872 | tf_op jit(solution)/shard_map/while/body/eval_jaxpr/ppermute | solution.py:15
  1047.8 29.9 %collective-permute-start = (f32[1,2,256,256]{3,2,1,0:T(8,128)}, f32[1,2,256,256]{3,2,1,0:T(8,128)}, u32[]{:S(2)}, u32[]{:S(2)}) collective-permute-start(f32[1,2,256,256]{3,2,1,0:T(8,128)} %copy.53), channel_id=1, source_target_pairs={{0,4},{4,8},{8,12},{12,16},{16,20},{20,24},{24,28},{28,32},{32,36}... | collective-permute-start | bytes 1572872 | tf_op jit(solution)/shard_map/while/body/eval_jaxpr/ppermute | solution.py:15
  1080.7 34.3 %collective-permute-start.1 = (f32[1,2,256,256]{3,2,1,0:T(8,128)S(1)}, f32[1,2,256,256]{3,2,1,0:T(8,128)S(1)}, u32[]{:S(2)}, u32[]{:S(2)}) collective-permute-start(f32[1,2,256,256]{3,2,1,0:T(8,128)S(1)} %copy.54), channel_id=1, source_target_pairs={{4,0},{8,4},{12,8},{16,12},{20,16},{24,20},{28,24},{32,28},{36,32}... | collective-permute-start | bytes 1572872 | tf_op jit(solution)/shard_map/while/body/eval_jaxpr/ppermute | solution.py:15
  1084.0 46.2 %collective-permute-start = (f32[1,2,256,256]{3,2,1,0:T(8,128)}, f32[1,2,256,256]{3,2,1,0:T(8,128)}, u32[]{:S(2)}, u32[]{:S(2)}) collective-permute-start(f32[1,2,256,256]{3,2,1,0:T(8,128)} %copy.53), channel_id=1, source_target_pairs={{0,4},{4,8},{8,12},{12,16},{16,20},{20,24},{24,28},{28,32},{32,36}... | collective-permute-start | bytes 1572872 | tf_op jit(solution)/shard_map/while/body/eval_jaxpr/ppermute | solution.py:15
  1136.6 23.0 %collective-permute-start = (f32[1,2,256,256]{3,2,1,0:T(8,128)}, f32[1,2,256,256]{3,2,1,0:T(8,128)}, u32[]{:S(2)}, u32[]{:S(2)}) collective-permute-start(f32[1,2,256,256]{3,2,1,0:T(8,128)} %copy.53), channel_id=1, source_target_pairs={{0,4},{4,8},{8,12},{12,16},{16,20},{20,24},{24,28},{28,32},{32,36}... | collective-permute-start | bytes 1572872 | tf_op jit(solution)/shard_map/while/body/eval_jaxpr/ppermute | solution.py:15
  (128 other events, 1015.1 us)
where the time goes:
time: 1390 us; the launch traced here: 1380 us
  starting transfers between devices  615 us (44%)
  local copies, waits for them, and re-layouts  370 us (27%)
  blocking collectives  128 us (9%)
  waiting for transfers between devices  106 us (8%)
  matrix products  76.7 us (6%)
  other arithmetic  70.3 us (5%)
    ppermute x70, starting transfers between devices, passed_along(): lax.ppermute(value, axis, [(source, source + steps) for source in range(i...  615 us
    another operation x200, local copies, waits for them, and re-layouts  171 us
    psum x1, blocking collectives, on_device(): crossing = lax.psum(crossing, 'slab')  128 us
    ppermute x70, waiting for transfers between devices, passed_along(): lax.ppermute(value, axis, [(source, source + steps) for source in range(i...  106 us
    dynamic_slice x105, local copies, waits for them, and re-layouts, handle(): previous = lax.dynamic_index_in_dim(store, clipped, 0, keepdims=False)  82.4 us
    dot_general x120, matrix products, product(): jnp.dot(left_factor, right_factor, preferred_element_type=jnp.float32, pr...  76.7 us
    dynamic_update_slice x70, local copies, waits for them, and re-layouts, handle(): lax.dynamic_update_index_in_dim(store, jnp.where(active, entering, previo...  36.1 us
    dynamic_update_slice x35, other arithmetic, handle(): lax.dynamic_update_index_in_dim(store, jnp.where(active, entering, previo...  31.3 us
  transfers between devices with their start and end apart: 70, of which 48 were waited for; matrix products, arithmetic and copies ran while one was open for 20% of the time, Pallas kernels for 0%

commit v1 on v0

v1 whole, which is shorter than its diff:
```python
import functools
import jax
import jax.numpy as jnp
from jax import lax
from jax.experimental import pallas as pl
from jax.experimental.pallas import tpu as pltpu
from jax.sharding import Mesh
from jax.sharding import PartitionSpec as P

energy_floor = -0.2
energy_spacing = 0.0125
broadening = 0.3
W = 256
f32 = jnp.float32
b16 = jnp.bfloat16
VMEM_BYTES = 56 * 2**20


def dot_nt(left, right):
    return lax.dot_general(left, right, (((1,), (1,)), ((), ())), preferred_element_type=f32)


def dot_nn(left, right):
    return lax.dot_general(left, right, (((1,), (0,)), ((), ())), preferred_element_type=f32)


def split(value):
    high = value.astype(b16)
    return high, (value - high.astype(f32)).astype(b16)


def dot3(left, right, dot=dot_nt):
    return dot(left[0], right[0]) + (dot(left[1], right[0]) + dot(left[0], right[1]))


def cdot3(left, right, dot=dot_nt):
    (lr, li), (rr, ri) = left, right
    first = dot3(split(lr), split(rr), dot)
    second = dot3(split(li), split(ri), dot)
    summed = dot3(split(lr + li), split(rr + ri), dot)
    return first - second, summed - first - second


def eye_mask():
    rows = lax.broadcasted_iota(jnp.int32, (W, W), 0)
    columns = lax.broadcasted_iota(jnp.int32, (W, W), 1)
    return rows == columns


def diagonal_row(value):
    return jnp.sum(jnp.where(eye_mask(), value, 0.0), axis=0, keepdims=True)


def diagonal_and_rest(energy, onsite, sr, si):
    br = -(onsite + sr)
    bi = -si
    dr = energy + diagonal_row(br)
    di = broadening + diagonal_row(bi)
    scale = 1.0 / (dr * dr + di * di)
    dr, di = dr * scale, -di * scale
    mask = eye_mask()
    br = jnp.where(mask, 0.0, br)
    bi = jnp.where(mask, 0.0, bi)
    return br, bi, dr, di, br * dr - bi * di, br * di + bi * dr


def chain_step(energy, onsite, lead, sr, si):
    _, _, dr, di, fr, fi = diagonal_and_rest(energy, onsite, sr, si)
    frs, fis, leads = split(fr), split(fi), split(lead)
    pr, pi = dot3(leads, frs), dot3(leads, fis)
    prh, pih = pr.astype(b16), pi.astype(b16)
    qr = dot_nt(prh, frs[0]) - dot_nt(pih, fis[0])
    qi = dot_nt(prh, fis[0]) + dot_nt(pih, frs[0])
    x = lead - pr
    xr, xi = x * dr + pi * di, x * di - pi * dr
    return cdot3((xr, xi), (lead + qr, qi))


def spectral_row(energy, onsite, sr, si):
    br, bi, dr, di, fr, fi = diagonal_and_rest(energy, onsite, sr, si)
    frh, fih, brh, bih = (v.astype(b16) for v in (fr, fi, br, bi))
    yr = br - (dot_nt(frh, brh) - dot_nt(fih, bih))
    yi = bi - (dot_nt(frh, bih) + dot_nt(fih, brh))
    tr = jnp.sum(fr * yr - fi * yi, axis=1, keepdims=True)
    ti = jnp.sum(fr * yi + fi * yr, axis=1, keepdims=True)
    tr = diagonal_row(jnp.broadcast_to(tr, (W, W)))
    ti = diagonal_row(jnp.broadcast_to(ti, (W, W)))
    return -2.0 * (di + (dr * dr - di * di) * ti + 2.0 * dr * di * tr)


def crossing_row(energy, onsite, s0, s1, r0, r1):
    br, bi, dr, di, fr, fi = diagonal_and_rest(energy, onsite, s0 + r0, s1 + r1)
    f2r, f2i = cdot3((fr, fi), (fr, fi), dot_nn)
    f3r, f3i = cdot3((f2r, f2i), (fr, fi), dot_nn)
    one = jnp.where(eye_mask(), 1.0, 0.0)
    kr, ki = one - fr + f2r - f3r, -fi + f2i - f3i
    dcol_r = jnp.where(eye_mask(), dr, 0.0)
    dcol_i = jnp.where(eye_mask(), di, 0.0)
    dcol_r = jnp.sum(dcol_r, axis=1, keepdims=True)
    dcol_i = jnp.sum(dcol_i, axis=1, keepdims=True)
    gr, gi = dcol_r * kr - dcol_i * ki, dcol_r * ki + dcol_i * kr
    left, right = split(-2.0 * s1), split(-2.0 * r1)
    grs, gis = split(gr), split(gi)
    ar, ai = dot3(left, grs, dot_nn), dot3(left, gis, dot_nn)
    cr, ci = dot3(grs, right, dot_nt), dot3(gis, right, dot_nt)
    return jnp.sum(ar * cr + ai * ci, axis=0, keepdims=True)


def first_kernel(steps, place, energy, rates, wire, store, last, hbuf, mbuf, sbuf, in_sem, out_sem):
    flip = place[0]

    def fetch(t):
        slab = jnp.where(flip == 0, t, 15 - t)
        link = jnp.where(flip == 0, t, 14 - t)
        return (
            pltpu.make_async_copy(wire.at[slab, 0], hbuf.at[t], in_sem.at[t, 0]),
            pltpu.make_async_copy(wire.at[link, 1], mbuf.at[t], in_sem.at[t, 1]),
        )

    for t in range(steps):
        for copy in fetch(t):
            copy.start()
    sbuf[0, 0] = jnp.zeros((W, W), f32)
    sbuf[0, 1] = jnp.where(eye_mask(), -0.5 * rates[...], 0.0)

    def body(t, unused):
        for copy in fetch(t):
            copy.wait()
        pltpu.make_async_copy(sbuf.at[t], store.at[t], out_sem.at[t]).start()
        m = mbuf[t]
        lead = jnp.where(flip == 0, m.T, m)
        nr, ni = chain_step(energy[0], hbuf[t], lead, sbuf[t, 0], sbuf[t, 1])
        sbuf[t + 1, 0] = nr
        sbuf[t + 1, 1] = ni
        return 0

    lax.fori_loop(0, steps, body, 0)
    last[...] = sbuf[steps]
    for t in range(steps):
        pltpu.make_async_copy(sbuf.at[t], store.at[t], out_sem.at[t]).wait()


def edge_kernel(place, energy, onsite, link, entering, leaving):
    m = link[...]
    lead = jnp.where(place[0] == 0, m.T, m)
    nr, ni = chain_step(energy[0], onsite[...], lead, entering[0], entering[1])
    leaving[0] = nr
    leaving[1] = ni


def second_kernel(place, energy, wire, store, edge, arrived, spectra, crossing, hbuf, mbuf, sbuf, carried, in_sem):
    flip = place[0]

    def fetch(t):
        slab = jnp.where(flip == 0, 15 - t, t)
        link = jnp.where(flip == 0, jnp.maximum(14 - t, 0), t)
        return (
            pltpu.make_async_copy(wire.at[slab, 0], hbuf.at[t], in_sem.at[t, 0]),
            pltpu.make_async_copy(wire.at[link, 1], mbuf.at[t], in_sem.at[t, 1]),
        )

    def stored(t):
        return pltpu.make_async_copy(store.at[15 - t], sbuf.at[t], in_sem.at[t, 2])

    for t in range(16):
        for copy in fetch(t):
            copy.start()
        if t:
            stored(t).start()
    carried[...] = arrived[...]
    sbuf[0] = edge[...]
    crossing[...] = jnp.zeros((1, W), f32)

    def spectrum(t):
        row = spectral_row(energy[0], hbuf[t], sbuf[t, 0] + carried[0], sbuf[t, 1] + carried[1])
        slab = jnp.where(flip == 0, 15 - t, t)
        spectra[pl.ds(slab, 1)] = row[None]

    def advance(t):
        m = mbuf[t]
        lead = jnp.where(flip == 0, m, m.T)
        nr, ni = chain_step(energy[0], hbuf[t], lead, carried[0], carried[1])
        carried[0] = nr
        carried[1] = ni

    for copy in fetch(0):
        copy.wait()

    @pl.when(flip != 0)
    def _():
        crossing[...] = crossing_row(energy[0], hbuf[0], carried[0], carried[1], sbuf[0, 0], sbuf[0, 1])

    spectrum(0)
    advance(0)

    def body(t, unused):
        for copy in fetch(t):
            copy.wait()
        stored(t).wait()
        spectrum(t)
        advance(t)
        return 0

    lax.fori_loop(1, 15, body, 0)
    for copy in fetch(15):
        copy.wait()
    stored(15).wait()
    spectrum(15)


def vmem():
    return pl.BlockSpec(memory_space=pltpu.VMEM)


def smem():
    return pl.BlockSpec(memory_space=pltpu.SMEM)


def anywhere():
    return pl.BlockSpec(memory_space=pl.ANY)


def params():
    return pltpu.CompilerParams(vmem_limit_bytes=VMEM_BYTES)


def first_sweep(place, energy, rates, wire):
    steps = 15
    return pl.pallas_call(
        functools.partial(first_kernel, steps),
        out_shape=(jax.ShapeDtypeStruct((steps, 2, W, W), f32), jax.ShapeDtypeStruct((2, W, W), f32)),
        in_specs=[smem(), smem(), vmem(), anywhere()],
        out_specs=[anywhere(), vmem()],
        scratch_shapes=[
            pltpu.VMEM((steps, W, W), f32),
            pltpu.VMEM((steps, W, W), f32),
            pltpu.VMEM((steps + 1, 2, W, W), f32),
            pltpu.SemaphoreType.DMA((steps, 2)),
            pltpu.SemaphoreType.DMA((steps,)),
        ],
        name="first_sweep",
        compiler_params=params(),
        cost_estimate=pl.CostEstimate(flops=15 * 20 * 2 * W**3, bytes_accessed=15 * 2**20, transcendentals=0),
    )(place, energy, rates, wire)


def edge_step(place, energy, onsite, link, entering):
    return pl.pallas_call(
        edge_kernel,
        out_shape=jax.ShapeDtypeStruct((2, W, W), f32),
        in_specs=[smem(), smem(), vmem(), vmem(), vmem()],
        out_specs=vmem(),
        name="edge_step",
        compiler_params=params(),
    )(place, energy, onsite, link, entering)


def second_sweep(place, energy, wire, store, edge, arrived):
    return pl.pallas_call(
        second_kernel,
        out_shape=(jax.ShapeDtypeStruct((16, 1, W), f32), jax.ShapeDtypeStruct((1, W), f32)),
        in_specs=[smem(), smem(), anywhere(), anywhere(), vmem(), vmem()],
        out_specs=[vmem(), vmem()],
        scratch_shapes=[
            pltpu.VMEM((16, W, W), f32),
            pltpu.VMEM((16, W, W), f32),
            pltpu.VMEM((16, 2, W, W), f32),
            pltpu.VMEM((2, W, W), f32),
            pltpu.SemaphoreType.DMA((16, 3)),
        ],
        name="second_sweep",
        compiler_params=params(),
    )(place, energy, wire, store, edge, arrived)


def on_device(onsite, coupling, pattern, contact_rates, energy_index):
    half, x, y, core = (lax.axis_index(name) for name in ("half", "x", "y", "core"))
    mask = jnp.repeat(jnp.repeat(pattern[0].astype(f32), 64, axis=0), 64, axis=1)
    masked = coupling[0] * mask
    wire = lax.all_gather(jnp.where(core == 0, onsite[0], masked), ("x", "y", "core"), tiled=False)
    wire = wire.reshape(16, 2, W, W)
    place = half.astype(jnp.int32)[None]
    energies = energy_floor + energy_spacing * energy_index.astype(f32)
    energy = lax.dynamic_slice(energies, (y,), (1,))
    rates = lax.dynamic_slice(contact_rates, (half, 0), (1, W))

    bridge = lax.ppermute(wire[15, 1], "half", [(0, 1)])
    bridge = jnp.where(half == 0, wire[15, 1], bridge)
    inner = lax.dynamic_index_in_dim(wire[:, 0], jnp.where(half == 0, 15, 0), 0, keepdims=False)
    store, edge = first_sweep(place, energy, rates, wire)
    leaving = edge_step(place, energy, inner, bridge, edge)
    arrived = lax.ppermute(leaving, "half", [(0, 1), (1, 0)])
    spectra, crossing = second_sweep(place, energy, wire, store, edge, arrived)

    total = jnp.broadcast_to(jnp.sum(crossing), (1, W))
    mine = jnp.concatenate([lax.dynamic_slice(spectra[:, 0], (4 * x, 0), (4, W)), total], axis=0)

    def sent(shift):
        row = lax.dynamic_slice(mine, (lax.rem(y + shift, 4), 0), (1, W))
        return jnp.concatenate([row, total], axis=0)

    pieces = [sent(0)]
    for shift in (1, 2, 3):
        pieces.append(lax.ppermute(sent(shift), "y", [(a, (a + shift) % 4) for a in range(4)]))
    turned = jnp.stack((pieces[::-1]) * 2)
    gathered = lax.dynamic_slice(turned, (3 - y, 0, 0), (4, 2, W))
    spectral = gathered[:, 0]
    totals = gathered[:, 1]
    totals = jnp.where(half == 0, lax.ppermute(totals, "half", [(1, 0)]), totals)
    return spectral[None], totals[:, 0]


def solution(mesh):
    fine = Mesh(mesh.devices.reshape(2, 4, 4, 2, 2), ("half", "x", "y", "plane", "core"))
    slab = ("half", "x", "y")
    part = ("plane", "core")
    return jax.shard_map(
        on_device,
        mesh=fine,
        in_specs=(P(slab), P(slab), P(slab), P(), P(part)),
        out_specs=(P(slab, part, None), P(part)),
        check_vma=False,
    )
```

time: 1390 us -> 171 us (0.12)
  starting transfers between devices: 615 us -> 9.6 us
  local copies, waits for them, and re-layouts: 370 us -> 14.2 us
  blocking collectives: 128 us -> 0 us
  matrix products: 76.7 us -> 0 us
  other arithmetic: 70.3 us -> 4.98 us
  Pallas kernels: 0 us -> 52.8 us
  waiting for transfers between devices: 106 us -> 73.1 us
    ppermute x70 -> x6, starting transfers between devices: 615 us -> 9.56 us  [the longest x3 5.1 us: on_device(): lax.ppermute(sent(shift), 'y', [(a, (a + shift) % 4) for a in range(4)])]
    another operation x202 -> x5, local copies, waits for them, and re-layouts: 173 us -> 0.05 us  [on_device(): turned = jnp.stack(pieces[::-1] * 2)]
    psum x1 -> x0, blocking collectives: 128 us -> none  [on_device(): crossing = lax.psum(crossing, 'slab')]
    dynamic_slice x117 -> x4, local copies, waits for them, and re-layouts: 89.9 us -> 2.51 us  [the longest x1 0.69 us: on_device(): lax.dynamic_slice(spectra[:, 0], (4 * x, 0), (4, W))]
    ppermute x70 -> x6, waiting for transfers between devices: 106 us -> 20.3 us  [the longest x1 14 us: on_device(): arrived = lax.ppermute(leaving, 'half', [(0, 1), (1, 0)])]
    dot_general x120 -> x0, matrix products: 76.7 us -> none  [product(): jnp.dot(left_factor, right_factor, preferred_element_type=jnp.float32, pr...]
    gather x28 -> x0, local copies, waits for them, and re-layouts: 65.8 us -> none  [the longest x12 28.2 us: invert(): diag_imag = jnp.diagonal(matrix[1])]
    pallas_call x0 -> x3, Pallas kernels: none -> 52.8 us  [the longest x1 27.3 us: second_sweep(): pl.pallas_call(second_kernel, out_shape=(jax.ShapeDtypeStruct((16, 1, W),...]
  transfers between devices with their start and end apart: 70 -> 7, of which waited for: 48 -> 5; matrix products, arithmetic and copies ran while one was open for 20% -> 4% of each run, Pallas kernels for 0% -> 13%
where the time goes in v1:
time: 171 us; the launch traced here: 169 us
  waiting for transfers between devices  73.1 us (43%)
  Pallas kernels  52.8 us (31%)
  local copies, waits for them, and re-layouts  14.2 us (8%)
  between operations  14.2 us (8%)
  starting transfers between devices  9.6 us (6%)
  other arithmetic  4.98 us (3%)
    all_gather x1, waiting for transfers between devices, on_device(): lax.all_gather(jnp.where(core == 0, onsite[0], masked), ('x', 'y', 'core'...  52.7 us
    pallas_call x1, Pallas kernels, second_sweep(): pl.pallas_call(second_kernel, out_shape=(jax.ShapeDtypeStruct((16, 1, W),...  27.3 us
    pallas_call x1, Pallas kernels, first_sweep(): pl.pallas_call(functools.partial(first_kernel, steps), out_shape=(jax.Sha...  21.6 us
    ppermute x1, waiting for transfers between devices, on_device(): arrived = lax.ppermute(leaving, 'half', [(0, 1), (1, 0)])  14 us
    ppermute x3, starting transfers between devices, on_device(): lax.ppermute(sent(shift), 'y', [(a, (a + shift) % 4) for a in range(4)])  5.1 us
    ppermute x1, waiting for transfers between devices, on_device(): lax.ppermute(totals, 'half', [(1, 0)])  4.2 us
    pallas_call x1, Pallas kernels, edge_step(): pl.pallas_call(edge_kernel, out_shape=jax.ShapeDtypeStruct((2, W, W), f32...  3.83 us
  transfers between devices with their start and end apart: 7, of which 5 were waited for; matrix products, arithmetic and copies ran while one was open for 4% of the time, Pallas kernels for 13%

profile of v1, /device:TPU:64, one launch (start us, length us, event | category | flops | bytes accessed | tf_op | source)
XLA Modules:
  0.0 168.8 jit_solution(10985276487037043796)
XLA Ops:
  7.2 0.7 convert_bitcast_fusion
  8.2 1.1 copy.25
  9.3 1.1 copy.24
  10.4 0.9 copy.26
  13.1 52.7 %all-gather.2.cloned.1.call-done = f32[32,256,256]{2,1,0:T(8,128)} async-done(((f32[1,256,256]{2,1,0:T(8,128)}), f32[32,256,256]{2,1,0:T(8,128)}) %all-gather.2.cloned.1.call-update) | async-done | bytes 8388624 | tf_op jit(solution)/shard_map/all_gather | solution.py:280
  65.9 1.0 slice_bitcast_fusion
  66.8 3.2 %collective-permute-start = (f32[256,256]{1,0:T(8,128)S(1)}, f32[256,256]{1,0:T(8,128)S(1)}, u32[]{:S(2)}, u32[]{:S(2)}) collective-permute-start(f32[256,256]{1,0:T(8,128)S(1)} %slice_bitcast_fusion), channel_id=1, source_target_pairs={{0,64},{1,65},{2,66},{3,67},{4,68},{5,69},{6,70},{7,71},{8,72},{9,... | collective-permute-start | bytes 786440 | tf_op jit(solution)/shard_map/ppermute | solution.py:287
  70.0 21.6 %first_sweep.1 = (f32[15,2,256,256]{3,2,1,0:T(8,128)}, f32[2,256,256]{2,1,0:T(8,128)}) custom-call(s32[1]{0:T(128)} %bitcast.place, f32[1]{0:T(128)} %dynamic_slice.30.energy, f32[1,256]{1,0:T(1,128)} %constant_dynamic-slice_fusion.1.rates, f32[16,2,256,256]{3,2,1,0:T(8,128)} %bitcast.27), custom_call_target="tpu_custom_call" | custom-call | flops 10066329600 | bytes 15728640 | tf_op jit(solution)/shard_map/first_sweep/pallas_call | solution.py:229
  91.6 2.6 %slice.21 = f32[16,1,256,256]{3,2,1,0:T(8,128)S(1)} slice(f32[16,2,256,256]{3,2,1,0:T(8,128)} %bitcast.28), slice={[0:16], [0:1], [0:256], [0:256]} | slice | bytes 8388608 | tf_op jit(solution)/shard_map/slice | solution.py:289
  94.3 0.7 dynamic-slice_bitcast_fusion.onsite
  95.0 1.7 %broadcast_select_fusion.link = f32[256,256]{1,0:T(8,128)} fusion(f32[256,256]{1,0:T(8,128)S(1)} %collective-permute-done, pred[]{:T(512)S(6)} %eq.9, f32[16,2,256,256]{3,2,1,0:T(8,128)} %bitcast.29), kind=kLoop, calls=%fused_computation.4 | loop fusion | flops 65536 | bytes 786433 | tf_op jit(solution)/shard_map/jit(_where)/select_n | solution.py:288
  96.7 3.8 %edge_step.1 = f32[2,256,256]{2,1,0:T(8,128)} custom-call(s32[1]{0:T(128)} %bitcast.place, f32[1]{0:T(128)} %dynamic_slice.30.energy, f32[256,256]{1,0:T(8,128)} %dynamic-slice_bitcast_fusion.onsite, f32[256,256]{1,0:T(8,128)} %broadcast_select_fusion.link, f32[2,256,256]{2,1,0:T(8,128)} %get-tuple-element.7.entering.edge), custom_call_target="tpu_custom_call" | custom-call | tf_op jit(solution)/shard_map/edge_step/pallas_call | solution.py:248
  100.5 14.0 %collective-permute-done.1.arrived = f32[2,256,256]{2,1,0:T(8,128)S(1)} collective-permute-done((f32[2,256,256]{2,1,0:T(8,128)}, f32[2,256,256]{2,1,0:T(8,128)S(1)}, u32[]{:S(2)}, u32[]{:S(2)}) %collective-permute-start.1) | collective-permute-done | bytes 524320 | tf_op jit(solution)/shard_map/ppermute | solution.py:292
  114.5 0.8 copy-done.1
  115.3 27.3 %second_sweep.1 = (f32[16,1,256]{2,1,0:T(1,128)}, f32[1,256]{1,0:T(1,128)}) custom-call(s32[1]{0:T(128)} %bitcast.place, f32[1]{0:T(128)} %dynamic_slice.30.energy, f32[16,2,256,256]{3,2,1,0:T(8,128)} %bitcast.30, f32[15,2,256,256]{3,2,1,0:T(8,128)} %get-tuple-element.6.store, f32[2,256,256]{2,1,0:T(8,128)} %get-tuple-element.7.entering.edge, ...), custom_call_target="tpu_custom_call" | custom-call | tf_op jit(solution)/shard_map/second_sweep/pallas_call | solution.py:259
  142.7 0.7 constant_dynamic-slice_fusion
  143.4 1.3 reduce_sum.9
  144.7 0.7 pad_dynamic-slice_fusion
  146.0 2.7 %collective-permute-start.2 = (f32[2,256]{1,0:T(2,128)S(1)}, f32[2,256]{1,0:T(2,128)S(1)}, u32[]{:S(2)}, u32[]{:S(2)}) collective-permute-start(f32[2,256]{1,0:T(2,128)S(1)} %concatenate.16), channel_id=1, source_target_pairs={{0,12},{4,0},{8,4},{12,8},{1,13},{5,1},{9,5},{13,9},{2,14},{6,2},{... | collective-permute-start | bytes 6152 | tf_op jit(solution)/shard_map/ppermute | solution.py:304
  150.0 2.4 %collective-permute-start.3 = (f32[2,256]{1,0:T(2,128)S(1)}, f32[2,256]{1,0:T(2,128)S(1)}, u32[]{:S(2)}, u32[]{:S(2)}) collective-permute-start(f32[2,256]{1,0:T(2,128)S(1)} %concatenate.17), channel_id=1, source_target_pairs={{0,8},{4,12},{8,0},{12,4},{1,9},{5,13},{9,1},{13,5},{2,10},{6,14},... | collective-permute-start | bytes 6152 | tf_op jit(solution)/shard_map/ppermute | solution.py:304
  153.1 1.1 collective-permute-done.4
  154.2 1.0 collective-permute-done.3
  155.9 1.3 collective-permute-start.5
  157.2 4.2 %collective-permute-done.5 = f32[4,256]{1,0:T(4,128)S(1)} collective-permute-done((f32[4,256]{1,0:T(4,128)S(1)}, f32[4,256]{1,0:T(4,128)S(1)}, u32[]{:S(2)}, u32[]{:S(2)}) %collective-permute-start.5) | collective-permute-done | bytes 4128 | tf_op jit(solution)/shard_map/ppermute | solution.py:309
  (28 shorter events, 6.1 us)
Async XLA Ops:
  7.2 5.4 %copy-start = (f32[2,256]{1,0:T(2,128)S(1)}, f32[2,256]{1,0:T(2,128)}, u32[]{:S(2)}) copy-start(f32[2,256]{1,0:T(2,128)} %param.8) | copy-start | bytes 6148
  7.2 58.7 %all-gather.2.cloned.1.call-start = ((), (), s32[]{:S(2)}) async-start(), calls=%async_computation | async-start | bytes 8650752 | tf_op jit(solution)/shard_map/all_gather | solution.py:280
  66.8 28.2 %collective-permute-start = (f32[256,256]{1,0:T(8,128)S(1)}, f32[256,256]{1,0:T(8,128)S(1)}, u32[]{:S(2)}, u32[]{:S(2)}) collective-permute-start(f32[256,256]{1,0:T(8,128)S(1)} %slice_bitcast_fusion), channel_id=1, source_target_pairs={{0,64},{1,65},{2,66},{3,67},{4,68},{5,69},{6,70},{7,71},{8,72},{9,... | collective-permute-start | bytes 786440 | tf_op jit(solution)/shard_map/ppermute | solution.py:287
  100.5 14.0 %collective-permute-start.1 = (f32[2,256,256]{2,1,0:T(8,128)}, f32[2,256,256]{2,1,0:T(8,128)S(1)}, u32[]{:S(2)}, u32[]{:S(2)}) collective-permute-start(f32[2,256,256]{2,1,0:T(8,128)} %edge_step.1), channel_id=1, source_target_pairs={{0,64},{64,0},{1,65},{65,1},{2,66},{66,2},{3,67},{67,3},{4,68},{68... | collective-permute-start | bytes 1572872 | tf_op jit(solution)/shard_map/ppermute | solution.py:292
  114.5 0.8 copy-start.1
  146.0 7.1 %collective-permute-start.2 = (f32[2,256]{1,0:T(2,128)S(1)}, f32[2,256]{1,0:T(2,128)S(1)}, u32[]{:S(2)}, u32[]{:S(2)}) collective-permute-start(f32[2,256]{1,0:T(2,128)S(1)} %concatenate.16), channel_id=1, source_target_pairs={{0,12},{4,0},{8,4},{12,8},{1,13},{5,1},{9,5},{13,9},{2,14},{6,2},{... | collective-permute-start | bytes 6152 | tf_op jit(solution)/shard_map/ppermute | solution.py:304
  149.3 4.9 %collective-permute-start.4 = (f32[2,256]{1,0:T(2,128)S(1)}, f32[2,256]{1,0:T(2,128)S(1)}, u32[]{:S(2)}, u32[]{:S(2)}) collective-permute-start(f32[2,256]{1,0:T(2,128)S(1)} %concatenate.18), channel_id=1, source_target_pairs={{0,4},{4,8},{8,12},{12,0},{1,5},{5,9},{9,13},{13,1},{2,6},{6,10},{... | collective-permute-start | bytes 6152 | tf_op jit(solution)/shard_map/ppermute | solution.py:304
  150.0 5.2 %collective-permute-start.3 = (f32[2,256]{1,0:T(2,128)S(1)}, f32[2,256]{1,0:T(2,128)S(1)}, u32[]{:S(2)}, u32[]{:S(2)}) collective-permute-start(f32[2,256]{1,0:T(2,128)S(1)} %concatenate.17), channel_id=1, source_target_pairs={{0,8},{4,12},{8,0},{12,4},{1,9},{5,13},{9,1},{13,5},{2,10},{6,14},... | collective-permute-start | bytes 6152 | tf_op jit(solution)/shard_map/ppermute | solution.py:304
  155.9 5.5 %collective-permute-start.5 = (f32[4,256]{1,0:T(4,128)S(1)}, f32[4,256]{1,0:T(4,128)S(1)}, u32[]{:S(2)}, u32[]{:S(2)}) collective-permute-start(f32[4,256]{1,0:T(4,128)S(1)} %get-tuple-element.10), channel_id=1, source_target_pairs={{64,0},{65,1},{66,2},{67,3},{68,4},{69,5},{70,6},{71,7},{72,8},{73... | collective-permute-start | bytes 12296 | tf_op jit(solution)/shard_map/ppermute | solution.py:309
Sparse Core Ops, SparseCore 0:
  11.4 54.3 all-gather.1

commit v2 on v1

v2 whole, which is shorter than its diff:
```python
import functools
import jax
import jax.numpy as jnp
from jax import lax
from jax.experimental import pallas as pl
from jax.experimental.pallas import tpu as pltpu
from jax.sharding import Mesh
from jax.sharding import PartitionSpec as P

energy_floor = -0.2
energy_spacing = 0.0125
broadening = 0.3
W = 256
f32 = jnp.float32
b16 = jnp.bfloat16
VMEM_BYTES = 32 * 2**20


def dot_nt(left, right):
    return lax.dot_general(left, right, (((1,), (1,)), ((), ())), preferred_element_type=f32)


def dot_nn(left, right):
    return lax.dot_general(left, right, (((1,), (0,)), ((), ())), preferred_element_type=f32)


def split(value):
    high = value.astype(b16)
    return high, (value - high.astype(f32)).astype(b16)


def dot3(left, right, dot=dot_nt):
    return dot(left[0], right[0]) + (dot(left[1], right[0]) + dot(left[0], right[1]))


def cdot3(left, right, dot=dot_nt):
    (lr, li), (rr, ri) = left, right
    first = dot3(split(lr), split(rr), dot)
    second = dot3(split(li), split(ri), dot)
    summed = dot3(split(lr + li), split(rr + ri), dot)
    return first - second, summed - first - second


def eye_mask():
    rows = lax.broadcasted_iota(jnp.int32, (W, W), 0)
    columns = lax.broadcasted_iota(jnp.int32, (W, W), 1)
    return rows == columns


def diagonal_row(value):
    return jnp.sum(jnp.where(eye_mask(), value, 0.0), axis=0, keepdims=True)


def diagonal_and_rest(energy, onsite, sr, si):
    br = -(onsite + sr)
    bi = -si
    dr = energy + diagonal_row(br)
    di = broadening + diagonal_row(bi)
    scale = 1.0 / (dr * dr + di * di)
    dr, di = dr * scale, -di * scale
    mask = eye_mask()
    br = jnp.where(mask, 0.0, br)
    bi = jnp.where(mask, 0.0, bi)
    return br, bi, dr, di, br * dr - bi * di, br * di + bi * dr


def chain_step(energy, onsite, lead, sr, si):
    _, _, dr, di, fr, fi = diagonal_and_rest(energy, onsite, sr, si)
    frs, fis, leads = split(fr), split(fi), split(lead)
    pr, pi = dot3(leads, frs), dot3(leads, fis)
    prh, pih = pr.astype(b16), pi.astype(b16)
    qr = dot_nt(prh, frs[0]) - dot_nt(pih, fis[0])
    qi = dot_nt(prh, fis[0]) + dot_nt(pih, frs[0])
    x = lead - pr
    xr, xi = x * dr + pi * di, x * di - pi * dr
    return cdot3((xr, xi), (lead + qr, qi))


def spectral_row(energy, onsite, sr, si):
    br, bi, dr, di, fr, fi = diagonal_and_rest(energy, onsite, sr, si)
    frh, fih, brh, bih = (v.astype(b16) for v in (fr, fi, br, bi))
    yr = br - (dot_nt(frh, brh) - dot_nt(fih, bih))
    yi = bi - (dot_nt(frh, bih) + dot_nt(fih, brh))
    tr = jnp.sum(fr * yr - fi * yi, axis=1, keepdims=True)
    ti = jnp.sum(fr * yi + fi * yr, axis=1, keepdims=True)
    tr = diagonal_row(jnp.broadcast_to(tr, (W, W)))
    ti = diagonal_row(jnp.broadcast_to(ti, (W, W)))
    return -2.0 * (di + (dr * dr - di * di) * ti + 2.0 * dr * di * tr)


def crossing_row(energy, onsite, s0, s1, r0, r1):
    br, bi, dr, di, fr, fi = diagonal_and_rest(energy, onsite, s0 + r0, s1 + r1)
    f2r, f2i = cdot3((fr, fi), (fr, fi), dot_nn)
    f3r, f3i = cdot3((f2r, f2i), (fr, fi), dot_nn)
    one = jnp.where(eye_mask(), 1.0, 0.0)
    kr, ki = one - fr + f2r - f3r, -fi + f2i - f3i
    dcol_r = jnp.where(eye_mask(), dr, 0.0)
    dcol_i = jnp.where(eye_mask(), di, 0.0)
    dcol_r = jnp.sum(dcol_r, axis=1, keepdims=True)
    dcol_i = jnp.sum(dcol_i, axis=1, keepdims=True)
    gr, gi = dcol_r * kr - dcol_i * ki, dcol_r * ki + dcol_i * kr
    left, right = split(-2.0 * s1), split(-2.0 * r1)
    grs, gis = split(gr), split(gi)
    ar, ai = dot3(left, grs, dot_nn), dot3(left, gis, dot_nn)
    cr, ci = dot3(grs, right, dot_nt), dot3(gis, right, dot_nt)
    return jnp.sum(ar * cr + ai * ci, axis=0, keepdims=True)


H2 = W // 2


def here(name):
    return lax.axis_index(name)


def on_task():
    x = here("x")
    return ((x == 0) | (x == 3)) == (here("core") == 0)


def is_outer():
    return (here("x") < 2) == (here("half") == 0)


def pack(sr, si, extra=0.0):
    rows = lax.broadcasted_iota(jnp.int32, (H2, H2), 0)
    columns = lax.broadcasted_iota(jnp.int32, (H2, H2), 1)

    def folded(value):
        low = value[H2:, H2:]
        fold = jnp.where(rows <= columns, value[:H2, :H2], low)
        diagonal = jnp.sum(jnp.where(rows == columns, low, 0.0), axis=0, keepdims=True)
        return jnp.concatenate([value[:H2, H2:], fold], axis=1), diagonal

    top, diagonal_top = folded(sr)
    bottom, diagonal_bottom = folded(si)
    row = jnp.broadcast_to(jnp.concatenate([diagonal_top, diagonal_bottom], axis=1), (8, W))
    last = jnp.where(lax.broadcasted_iota(jnp.int32, (8, W), 0) == 0, row, extra)
    return jnp.concatenate([top, bottom, last], axis=0)


def unpack(packed):
    rows = lax.broadcasted_iota(jnp.int32, (H2, H2), 0)
    columns = lax.broadcasted_iota(jnp.int32, (H2, H2), 1)

    def unfolded(value, diagonal):
        corner, fold = value[:, :H2], value[:, H2:]
        turned = fold.T
        first = jnp.where(rows <= columns, fold, turned)
        last = jnp.where(rows > columns, fold, jnp.where(rows < columns, turned, diagonal))
        top = jnp.concatenate([first, corner], axis=1)
        return jnp.concatenate([top, jnp.concatenate([corner.T, last], axis=1)], axis=0)

    return (
        unfolded(packed[:H2], packed[2 * H2 : 2 * H2 + 1, :H2]),
        unfolded(packed[H2 : 2 * H2], packed[2 * H2 : 2 * H2 + 1, H2:]),
    )


def prepare_kernel(pattern, onsite, coupling, both, mine):
    tiles = lax.broadcasted_iota(jnp.int32, (1, W), 1) // 64
    both[0] = onsite[...]
    for p in range(4):
        row = jnp.zeros((1, W), f32)
        for q in range(4):
            row = jnp.where(tiles == q, pattern[p, q].astype(f32), row)
        part = pl.ds(64 * p, 64)
        both[1, part, :] = coupling[part, :] * row
    mine[...] = both[here("core")]


def energy_of(index):
    return energy_floor + energy_spacing * index[here("y")].astype(f32)


STEPS = ((0, 3), (3, 7), (7, 8), (8, 16))
OUTWARD = ((1, 4), (4, 8), (8, 16))


def kept_at(t):
    part = next(k for k, (first, stop) in enumerate(STEPS) if first <= t < stop)
    return part, t - STEPS[part][0]


def sweep_kernel(part, *refs):
    first, stop = STEPS[part]
    count = stop - first
    refs = list(refs)
    index = refs.pop(0)
    start = refs.pop(0)
    both, own_mine, own_sent, near_mine, near_sent = (refs.pop(0) for _ in range(5))
    bridge = refs.pop(0) if part > 1 else None
    wire_h, wire_m, store, last = (refs.pop(0) for _ in range(4))
    hbuf, mbuf, sbuf, in_sem, out_sem = refs
    half, y, core = here("half"), here("y"), here("core")
    energy = energy_of(index)

    def start_from(chunk, column, kind, target, sem):
        away = lax.rem(column - y + 4, 4)
        own_row = core == (0 if chunk in (0, 3) else 1)

        @pl.when(own_row & (away == 0))
        def _():
            pltpu.make_async_copy(both.at[kind], target, sem).start()

        for here_too, own, near in ((core == kind, own_mine, near_mine), (core != kind, own_sent, near_sent)):

            @pl.when(own_row & (away != 0) & here_too)
            def _():
                pltpu.make_async_copy(own.at[jnp.maximum(away - 1, 0)], target, sem).start()

            @pl.when(~own_row & here_too)
            def _():
                pltpu.make_async_copy(near.at[away], target, sem).start()

    @pl.when(on_task() & (is_outer() if part < 3 else ~is_outer()))
    def _():
        for n in range(count):
            t = first + n
            start_from(t // 4, jnp.where(half == 0, t % 4, 3 - t % 4), 0, hbuf.at[n], in_sem.at[n, 0])
            if t % 4 < 3:
                start_from(t // 4, jnp.where(half == 0, t % 4, 2 - t % 4), 1, mbuf.at[n], in_sem.at[n, 1])
            else:

                @pl.when(half == 0)
                def _():
                    start_from(t // 4, 3, 1, mbuf.at[n], in_sem.at[n, 1])

                @pl.when(half != 0)
                def _():
                    if t % 8 == 7:
                        pltpu.make_async_copy(bridge, mbuf.at[n], in_sem.at[n, 1]).start()
                    else:
                        start_from(t // 4 + 1, 3, 1, mbuf.at[n], in_sem.at[n, 1])

        if part == 0:
            sbuf[0, 0] = jnp.zeros((W, W), f32)
            sbuf[0, 1] = jnp.where(eye_mask(), -0.5 * start[pl.ds(half, 1), :], 0.0)
        elif part < 3:
            sbuf[0] = start[...]
        else:
            sbuf[0, 0], sbuf[0, 1] = unpack(start[...])

        def kept(n):
            return (
                pltpu.make_async_copy(hbuf.at[n], wire_h.at[n], out_sem.at[n, 0]),
                pltpu.make_async_copy(mbuf.at[n], wire_m.at[n], out_sem.at[n, 1]),
                pltpu.make_async_copy(sbuf.at[n], store.at[n], out_sem.at[n, 2]),
            )

        def one(n, unused):
            pltpu.make_async_copy(wire_h.at[n], hbuf.at[n], in_sem.at[n, 0]).wait()
            pltpu.make_async_copy(wire_m.at[n], mbuf.at[n], in_sem.at[n, 1]).wait()
            for copy in kept(n):
                copy.start()
            m = mbuf[n]
            lead = jnp.where(half == 0, m.T, m)
            nr, ni = chain_step(energy, hbuf[n], lead, sbuf[n, 0], sbuf[n, 1])
            sbuf[n + 1, 0] = nr
            sbuf[n + 1, 1] = ni
            return 0

        lax.fori_loop(0, count, one, 0)
        if part > 1:
            last[...] = pack(sbuf[count, 0], sbuf[count, 1])
        else:
            last[...] = sbuf[count]
        for n in range(count):
            for copy in kept(n):
                copy.wait()


def middle_kernel(index, arrived, wire_h, wire_m, store, carried, crossing, spectrum, hbuf, mbuf, sbuf, in_sem):
    half = here("half")
    energy = energy_of(index)
    crossing[...] = jnp.zeros((8, W), f32)

    @pl.when(on_task() & ~is_outer())
    def _():
        copies = (
            pltpu.make_async_copy(wire_h.at[kept_at(15)[1]], hbuf, in_sem.at[0]),
            pltpu.make_async_copy(wire_m.at[kept_at(14)[1]], mbuf, in_sem.at[1]),
            pltpu.make_async_copy(store.at[kept_at(15)[1]], sbuf, in_sem.at[2]),
        )
        for copy in copies:
            copy.start()
        sr, si = unpack(arrived[...])
        for copy in copies:
            copy.wait()

        @pl.when(half != 0)
        def _():
            row = crossing_row(energy, hbuf[...], sr, si, sbuf[0], sbuf[1])
            crossing[...] = jnp.broadcast_to(jnp.sum(row, axis=1, keepdims=True), (8, W))

        spectrum[...] = spectral_row(energy, hbuf[...], sbuf[0] + sr, sbuf[1] + si)
        m = mbuf[...]
        lead = jnp.where(half == 0, m, m.T)
        nr, ni = chain_step(energy, hbuf[...], lead, sr, si)
        carried[0] = nr
        carried[1] = ni


def outward_kernel(leg, places, *refs):
    first, stop = OUTWARD[leg]
    count = stop - first
    refs = list(refs)
    index = refs.pop(0)
    start = refs.pop(0)
    earlier = refs.pop(0)
    totals = [refs.pop(0) for _ in range(2)] if leg else None
    links = [refs.pop(0) for _ in range(2)] if leg == 1 else None
    kept = {place: refs.pop(0) for place in places}
    outs = [refs.pop(0) for _ in range(4 if leg == 2 else 2)]
    hbuf, mbuf, sbuf, carried, spectra, in_sem = refs
    half, x, y = here("half"), here("x"), here("y")
    energy = energy_of(index)

    @pl.when(on_task() & (is_outer() if leg == 2 else ~is_outer()))
    def _():
        for n in range(count):
            t = first + n
            k, at_n = kept_at(15 - t)
            pltpu.make_async_copy(kept[0, k].at[at_n], hbuf.at[n], in_sem.at[n, 0]).start()
            pltpu.make_async_copy(kept[2, k].at[at_n], sbuf.at[n], in_sem.at[n, 2]).start()
            if t == 7:
                for side in range(2):

                    @pl.when(half == side)
                    def _():
                        pltpu.make_async_copy(links[side], mbuf.at[n], in_sem.at[n, 1]).start()

            elif t < 15:
                k, at_n = kept_at(14 - t)
                pltpu.make_async_copy(kept[1, k].at[at_n], mbuf.at[n], in_sem.at[n, 1]).start()
        if leg == 2:
            carried[0], carried[1] = unpack(start[...])
        else:
            carried[...] = start[...]
        if leg == 0:
            spectra[pl.ds(jnp.where(half == 0, 15, 0), 1)] = earlier[...][None]
        elif leg == 1:
            spectra[...] = earlier[...]

        def landed(n, link=True):
            pltpu.make_async_copy(hbuf.at[n], hbuf.at[n], in_sem.at[n, 0]).wait()
            pltpu.make_async_copy(sbuf.at[n], sbuf.at[n], in_sem.at[n, 2]).wait()
            if link:
                pltpu.make_async_copy(mbuf.at[n], mbuf.at[n], in_sem.at[n, 1]).wait()

        def spectrum(n):
            row = spectral_row(energy, hbuf[n], sbuf[n, 0] + carried[0], sbuf[n, 1] + carried[1])
            spectra[pl.ds(jnp.where(half == 0, 15 - first - n, first + n), 1)] = row[None]

        def one(n, unused):
            landed(n)
            spectrum(n)
            m = mbuf[n]
            lead = jnp.where(half == 0, m, m.T)
            nr, ni = chain_step(energy, hbuf[n], lead, carried[0], carried[1])
            carried[0] = nr
            carried[1] = ni
            return 0

        lax.fori_loop(0, count - (leg == 2), one, 0)
        if leg == 2:
            landed(count - 1, False)
            spectrum(count - 1)
        elif leg == 1:
            outs[0][...] = pack(carried[0], carried[1], totals[0][...] + totals[1][...])
            outs[1][...] = spectra[...]
        else:
            outs[0][...] = carried[...]
            outs[1][...] = spectra[...]

    if leg == 2:

        @pl.when(on_task())
        def _():
            @pl.when(~is_outer())
            def _():
                spectra[...] = earlier[...]

            outer_total = start[pl.ds(2 * H2, 8), :]
            total = jnp.where(is_outer(), outer_total, totals[0][...] + totals[1][...])
            partner = x + 1 - 2 * lax.rem(x, 2)
            for shift in range(4):
                column = lax.rem(y + shift, 4)
                outs[shift][pl.ds(0, 1), :] = spectra[4 * x + column]
                outs[shift][pl.ds(1, 1), :] = spectra[4 * partner + column]
                outs[shift][pl.ds(2, 6), :] = total[2:8]


def deal_kernel(*refs):
    pieces, outs, stack = refs[:4], refs[4:6], refs[6]
    y = here("y")
    for shift in range(4):
        stack[shift] = pieces[shift][...]
    for e in range(4):
        shift = lax.rem(y - e + 4, 4)
        for row in range(2):
            outs[row][pl.ds(e, 1), :] = stack[shift, pl.ds(row, 1), :]
            outs[row][pl.ds(4 + e, 1), :] = stack[shift, pl.ds(2, 1), :]


def vmem():
    return pl.BlockSpec(memory_space=pltpu.VMEM)


def smem():
    return pl.BlockSpec(memory_space=pltpu.SMEM)


def anywhere():
    return pl.BlockSpec(memory_space=pl.ANY)


def shape(*sizes):
    return jax.ShapeDtypeStruct(sizes, f32)


def params():
    return pltpu.CompilerParams(vmem_limit_bytes=VMEM_BYTES)


def cost(steps):
    return pl.CostEstimate(flops=int(steps * 1.4e9), bytes_accessed=int(steps * 2**20), transcendentals=0)


def prepare(pattern, onsite, coupling):
    return pl.pallas_call(
        prepare_kernel,
        out_shape=(shape(2, W, W), shape(W, W)),
        in_specs=[smem(), vmem(), vmem()],
        out_specs=[vmem(), vmem()],
        name="prepare",
    )(pattern, onsite, coupling)


def sweep(part, index, start, sets, bridge=None):
    first, stop = STEPS[part]
    count = stop - first
    arrays = list(sets)
    if bridge is not None:
        arrays.append(bridge)
    outs = [shape(count, W, W), shape(count, W, W), shape(count, 2, W, W)]
    outs.append(shape(2 * H2 + 8, W) if part > 1 else shape(2, W, W))
    return pl.pallas_call(
        functools.partial(sweep_kernel, part),
        out_shape=tuple(outs),
        in_specs=[smem(), vmem()] + [anywhere()] * len(arrays),
        out_specs=[anywhere(), anywhere(), anywhere(), vmem()],
        scratch_shapes=[
            pltpu.VMEM((count, W, W), f32),
            pltpu.VMEM((count, W, W), f32),
            pltpu.VMEM((count + 1, 2, W, W), f32),
            pltpu.SemaphoreType.DMA((count, 2)),
            pltpu.SemaphoreType.DMA((count, 3)),
        ],
        name="sweep_%d" % part,
        compiler_params=params(),
        cost_estimate=cost(count),
    )(index, start, *arrays)


def middle(index, arrived, wire_h, wire_m, store):
    return pl.pallas_call(
        middle_kernel,
        out_shape=(shape(2, W, W), shape(8, W), shape(1, W)),
        in_specs=[smem(), vmem(), anywhere(), anywhere(), anywhere()],
        out_specs=[vmem()] * 3,
        scratch_shapes=[
            pltpu.VMEM((W, W), f32),
            pltpu.VMEM((W, W), f32),
            pltpu.VMEM((2, W, W), f32),
            pltpu.SemaphoreType.DMA((3,)),
        ],
        name="middle",
        compiler_params=params(),
        cost_estimate=cost(2),
    )(index, arrived, wire_h, wire_m, store)


def outward(leg, index, start, earlier, totals, links, kept):
    first, stop = OUTWARD[leg]
    count = stop - first
    places = set()
    for t in range(first, stop):
        k = kept_at(15 - t)[0]
        places |= {(0, k), (2, k)}
        if t not in (7, 15):
            places.add((1, kept_at(14 - t)[0]))
    places = sorted(places)
    arrays = [*links, *(kept[k][kind] for kind, k in places)]
    outs = {
        0: [shape(2, W, W), shape(16, 1, W)],
        1: [shape(2 * H2 + 8, W), shape(16, 1, W)],
        2: [shape(8, W)] * 4,
    }[leg]
    return pl.pallas_call(
        functools.partial(outward_kernel, leg, places),
        out_shape=tuple(outs),
        in_specs=[smem()] + [vmem()] * (2 + len(totals)) + [anywhere()] * len(arrays),
        out_specs=[vmem()] * len(outs),
        scratch_shapes=[
            pltpu.VMEM((count, W, W), f32),
            pltpu.VMEM((count, W, W), f32),
            pltpu.VMEM((count, 2, W, W), f32),
            pltpu.VMEM((2, W, W), f32),
            pltpu.VMEM((16, 1, W), f32),
            pltpu.SemaphoreType.DMA((count, 3)),
        ],
        name="outward_%d" % leg,
        compiler_params=params(),
        cost_estimate=cost(1.2 * count),
    )(index, start, earlier, *totals, *arrays)


def deal(pieces):
    return pl.pallas_call(
        deal_kernel,
        out_shape=(shape(8, W), shape(8, W)),
        in_specs=[vmem()] * 4,
        out_specs=[vmem()] * 2,
        scratch_shapes=[pltpu.VMEM((4, 8, W), f32)],
        name="deal",
    )(*pieces)


AXES = ("half", "x", "y", "core")


def at(half, x, y, core):
    return ((half * 4 + x) * 4 + y) * 2 + core


def moved(value, move, chosen=lambda half, x, y, core: True):
    pairs = []
    for half in range(2):
        for x in range(4):
            for y in range(4):
                for core in range(2):
                    if chosen(half, x, y, core):
                        pairs.append((at(half, x, y, core), at(*move(half, x, y, core))))
    return lax.ppermute(value, AXES, pairs)


def is_task(half, x, y, core):
    return (x in (0, 3)) == (core == 0)


def outer_task(half, x, y, core):
    return is_task(half, x, y, core) and (x < 2) == (half == 0)


def inner_task(half, x, y, core):
    return is_task(half, x, y, core) and (x < 2) != (half == 0)


def along_y(value, shift, chosen=lambda *place: True):
    return moved(value, lambda half, x, y, core: (half, x, (y + shift) % 4, core), chosen)


def to_partner(value, chosen=lambda *place: True):
    return moved(value, lambda half, x, y, core: (half, x ^ 1, y, core), chosen)


def to_next(value, chosen):
    return moved(value, lambda half, x, y, core: (half, 3 - x, y, core), chosen)


def to_other_half(value, chosen):
    return moved(value, lambda half, x, y, core: (1 - half, 3 - x, y, core), chosen)


def across(value):
    return moved(value, lambda half, x, y, core: (half, x, y, 1 - core), lambda *place: not is_task(*place))


def after(value, other):
    return lax.optimization_barrier((value, other))[0]


def on_device(onsite, coupling, pattern, contact_rates, energy_index):
    x, y = here("x"), here("y")
    both, mine = prepare(pattern[0], onsite[0], coupling[0])
    near = to_partner(mine)
    left, right = along_y(mine, 1), along_y(mine, -1)
    opposite = jnp.concatenate([along_y(left[:H2], 1), along_y(right[H2:], -1)], axis=0)
    own_row = jnp.stack([right, opposite, left])
    near_row = jnp.stack([near, along_y(near, -1), to_partner(opposite), along_y(near, 1)])
    own_sent, near_sent = across(own_row), across(near_row)
    sets = (both, own_row, own_sent, near_row, near_sent)
    *first, carry = sweep(0, energy_index, contact_rates, sets)

    links = here("core") == 1
    own_links = jnp.concatenate([both[1:], jnp.where(links, own_row, own_sent)], axis=0)
    near_links = jnp.where(links, near_row, near_sent)
    row_links = jnp.where(lax.rem(x, 2) == 1, own_links, near_links)
    link = after(lax.dynamic_index_in_dim(row_links, lax.rem(7 - y, 4), 0, keepdims=False), carry)
    bridge = moved(
        link,
        lambda half, x, y, core: (half if x < 2 else 1, 3 - x, y, core),
        lambda half, x, y, core: is_task(half, x, y, core) and not (half == 1 and x >= 2),
    )
    *second, carry = sweep(1, energy_index, carry, sets)
    *edge, leaving = sweep(2, energy_index, carry, sets, bridge)
    arrived = to_next(leaving, outer_task)
    *inner, leaving = sweep(3, energy_index, arrived, sets, bridge)
    kept = [first, second, edge, inner]
    arrived = to_other_half(leaving, inner_task)
    carry, total, earlier = middle(energy_index, arrived, *inner)
    sent_total = to_other_half(
        total, lambda half, x, y, core: half == 1 and inner_task(half, x, y, core)
    )
    totals = [total, sent_total]
    carry, earlier = outward(0, energy_index, carry, earlier, [], [], kept)
    leaving, earlier = outward(1, energy_index, carry, earlier, totals, [bridge, link], kept)
    arrived = to_next(leaving, inner_task)
    pieces = outward(2, energy_index, arrived, earlier, totals, [], kept)

    pieces = [pieces[0]] + [along_y(pieces[shift], shift, is_task) for shift in (1, 2, 3)]
    own, other = deal(pieces)
    result = jnp.where(on_task(), own, to_partner(other, is_task))
    return result[:4][None], result[4:, 0]


def solution(mesh):
    fine = Mesh(mesh.devices.reshape(2, 4, 4, 2, 2), ("half", "x", "y", "plane", "core"))
    slab = ("half", "x", "y")
    part = ("plane", "core")
    return jax.shard_map(
        on_device,
        mesh=fine,
        in_specs=(P(slab), P(slab), P(slab), P(), P(part)),
        out_specs=(P(slab, part, None), P(part)),
        check_vma=False,
    )
```

time: 171 us -> 139 us (0.81)
  starting transfers between devices: 9.6 us -> 33 us
  Pallas kernels: 52.8 us -> 32.9 us
  between operations: 14.2 us -> 0.96 us
  local copies, waits for them, and re-layouts: 14.2 us -> 3.17 us
  waiting for transfers between devices: 73.1 us -> 64.6 us
  other arithmetic: 4.98 us -> 3.03 us
    all_gather x1 -> x0, waiting for transfers between devices: 52.7 us -> none  [on_device(): lax.all_gather(jnp.where(core == 0, onsite[0], masked), ('x', 'y', 'core'...]
    ppermute x6 -> x19, waiting for transfers between devices: 20.3 us -> 64.6 us  [moved(): return lax.ppermute(value, AXES, pairs)]
    ppermute x6 -> x19, starting transfers between devices: 9.56 us -> 33 us  [moved(): return lax.ppermute(value, AXES, pairs)]
    pallas_call x3 -> x10, Pallas kernels: 52.8 us -> 32.9 us  [the longest x4 15.1 us: sweep(): pl.pallas_call(functools.partial(sweep_kernel, part), out_shape=tuple(out...]
    concatenate x4 -> x1, local copies, waits for them, and re-layouts: 2.6 us -> 0.01 us  [on_device(): jnp.concatenate([along_y(left[:H2], 1), along_y(right[H2:], -1)], axis=0)]
    dynamic_slice x4 -> x0, local copies, waits for them, and re-layouts: 2.51 us -> none  [the longest x1 0.69 us: on_device(): lax.dynamic_slice(spectra[:, 0], (4 * x, 0), (4, W))]
    squeeze x3 -> x0, local copies, waits for them, and re-layouts: 2.3 us -> none  [the longest x1 0.97 us: on_device(): bridge = jnp.where(half == 0, wire[15, 1], bridge)]
    unnamed x7 -> x21, local copies, waits for them, and re-layouts: 2.98 us -> 1.2 us
  transfers between devices with their start and end apart: 7 -> 19, of which waited for: 5 -> 10; matrix products, arithmetic and copies ran while one was open for 4% -> 1% of each run, Pallas kernels for 13% -> 5%
where the time goes in v2:
time: 139 us; the launch traced here: 138 us
  waiting for transfers between devices  64.6 us (46%)
  starting transfers between devices  33 us (24%)
  Pallas kernels  32.9 us (24%)
  local copies, waits for them, and re-layouts  3.17 us (2%)
  other arithmetic  3.03 us (2%)
    ppermute x19, waiting for transfers between devices, moved(): return lax.ppermute(value, AXES, pairs)  64.6 us
    ppermute x19, starting transfers between devices, moved(): return lax.ppermute(value, AXES, pairs)  33 us
    pallas_call x4, Pallas kernels, sweep(): pl.pallas_call(functools.partial(sweep_kernel, part), out_shape=tuple(out...  15.1 us
    pallas_call x3, Pallas kernels, outward(): pl.pallas_call(functools.partial(outward_kernel, leg, places), out_shape=...  14 us
  transfers between devices with their start and end apart: 19, of which 10 were waited for; matrix products, arithmetic and copies ran while one was open for 1% of the time, Pallas kernels for 5%

profile of v2, /device:TPU:64, one launch (start us, length us, event | category | flops | bytes accessed | tf_op | source)
XLA Modules:
  0.0 137.7 jit_solution(7435365185016404940)
XLA Ops:
  0.6 2.0 %prepare.1 = (f32[2,256,256]{2,1,0:T(8,128)}, f32[256,256]{1,0:T(8,128)}) custom-call(s32[4,4]{1,0:T(4,128)} %bitcast.26, f32[256,256]{1,0:T(8,128)} %bitcast.20, f32[256,256]{1,0:T(8,128)} %bitcast.21), custom_call_target="tpu_custom_call" | custom-call | tf_op jit(solution)/shard_map/prepare/pallas_call | solution.py:431
  2.6 1.6 %collective-permute-start.1 = (f32[256,256]{1,0:T(8,128)}, f32[256,256]{1,0:T(8,128)S(1)}, u32[]{:S(2)}, u32[]{:S(2)}) collective-permute-start(f32[256,256]{1,0:T(8,128)} %get-tuple-element.34), channel_id=1, source_target_pairs={{0,4},{1,5},{4,8},{5,9},{8,12},{9,13},{12,0},{13,1},{16,20},{17,21... | collective-permute-start | bytes 786440 | tf_op jit(solution)/shard_map/ppermute | solution.py:545
  4.2 1.7 %collective-permute-start = (f32[256,256]{1,0:T(8,128)}, f32[256,256]{1,0:T(8,128)S(1)}, u32[]{:S(2)}, u32[]{:S(2)}) collective-permute-start(f32[256,256]{1,0:T(8,128)} %get-tuple-element.34), channel_id=1, source_target_pairs={{0,12},{1,13},{4,0},{5,1},{8,4},{9,5},{12,8},{13,9},{16,28},{17,29... | collective-permute-start | bytes 786440 | tf_op jit(solution)/shard_map/ppermute | solution.py:545
  5.8 1.5 %collective-permute-start.5 = (f32[256,256]{1,0:T(8,128)}, f32[256,256]{1,0:T(8,128)S(1)}, u32[]{:S(2)}, u32[]{:S(2)}) collective-permute-start(f32[256,256]{1,0:T(8,128)} %get-tuple-element.34), channel_id=1, source_target_pairs={{0,16},{1,17},{4,20},{5,21},{8,24},{9,25},{12,28},{13,29},{16,0},{... | collective-permute-start | bytes 786440 | tf_op jit(solution)/shard_map/ppermute | solution.py:545
  7.3 4.8 %collective-permute-done.1 = f32[256,256]{1,0:T(8,128)S(1)} collective-permute-done((f32[256,256]{1,0:T(8,128)}, f32[256,256]{1,0:T(8,128)S(1)}, u32[]{:S(2)}, u32[]{:S(2)}) %collective-permute-start.1) | collective-permute-done | bytes 262176 | tf_op jit(solution)/shard_map/ppermute | solution.py:545
  12.5 3.0 %collective-permute-start.3 = (f32[128,256]{1,0:T(8,128)S(1)}, f32[128,256]{1,0:T(8,128)S(1)}, u32[]{:S(2)}, u32[]{:S(2)}) collective-permute-start(f32[128,256]{1,0:T(8,128)S(1)} %slice.21), channel_id=1, source_target_pairs={{0,12},{1,13},{4,0},{5,1},{8,4},{9,5},{12,8},{13,9},{16,28},{17,29... | collective-permute-start | bytes 393224 | tf_op jit(solution)/shard_map/ppermute | solution.py:545
  15.5 3.2 %collective-permute-start.6 = (f32[256,256]{1,0:T(8,128)S(1)}, f32[256,256]{1,0:T(8,128)S(1)}, u32[]{:S(2)}, u32[]{:S(2)}) collective-permute-start(f32[256,256]{1,0:T(8,128)S(1)} %collective-permute-done.5), channel_id=1, source_target_pairs={{0,12},{1,13},{4,0},{5,1},{8,4},{9,5},{12,8},{13,9},{16,28},{17,29... | collective-permute-start | bytes 786440 | tf_op jit(solution)/shard_map/ppermute | solution.py:545
  19.1 1.6 %collective-permute-start.7 = (f32[256,256]{1,0:T(8,128)S(1)}, f32[256,256]{1,0:T(8,128)S(1)}, u32[]{:S(2)}, u32[]{:S(2)}) collective-permute-start(f32[256,256]{1,0:T(8,128)S(1)} %constant_dynamic-update-slice_fusion), channel_id=1, source_target_pairs={{0,16},{1,17},{4,20},{5,21},{8,24},{9,25},{12,28},{13,29},{16,0},{... | collective-permute-start | bytes 786440 | tf_op jit(solution)/shard_map/ppermute | solution.py:545
  22.0 2.0 %collective-permute-done.8 = f32[256,256]{1,0:T(8,128)S(1)} collective-permute-done((f32[256,256]{1,0:T(8,128)S(1)}, f32[256,256]{1,0:T(8,128)S(1)}, u32[]{:S(2)}, u32[]{:S(2)}) %collective-permute-start.8) | collective-permute-done | bytes 262176 | tf_op jit(solution)/shard_map/ppermute | solution.py:545
  24.0 1.5 %collective-permute-done.7 = f32[256,256]{1,0:T(8,128)S(1)} collective-permute-done((f32[256,256]{1,0:T(8,128)S(1)}, f32[256,256]{1,0:T(8,128)S(1)}, u32[]{:S(2)}, u32[]{:S(2)}) %collective-permute-start.7) | collective-permute-done | bytes 262176 | tf_op jit(solution)/shard_map/ppermute | solution.py:545
  28.8 1.5 %collective-permute-done.9.refs_6_ = f32[4,256,256]{2,1,0:T(8,128)} collective-permute-done((f32[4,256,256]{2,1,0:T(8,128)S(1)}, f32[4,256,256]{2,1,0:T(8,128)}, u32[]{:S(2)}, u32[]{:S(2)}) %collective-permute-start.9) | collective-permute-done | bytes 1048608 | tf_op jit(solution)/shard_map/ppermute | solution.py:545
  30.3 4.9 %sweep_0.1 = (f32[3,256,256]{2,1,0:T(8,128)S(1)}, f32[3,256,256]{2,1,0:T(8,128)S(1)}, f32[3,2,256,256]{3,2,1,0:T(8,128)S(1)}, f32[2,256,256]{2,1,0:T(8,128)S(1)}) custom-call(s32[4]{0:T(128)S(1)} %copy-done.3, f32[2,256]{1,0:T(2,128)S(1)} %copy-done.2, f32[2,256,256]{2,1,0:T(8,128)S(1)} %copy-done, f32[3,256,256]{2,1,0:T(8,128)S(1)} %pad_maximum_fusion.1.refs_3_, ...), custom_call_target="tpu_custom_call" | custom-call | flops 4200000000 | bytes 3145728 | tf_op jit(solution)/shard_map/sweep_0/pallas_call | solution.py:448
  37.6 6.2 %sweep_1.1 = (f32[4,256,256]{2,1,0:T(8,128)S(1)}, f32[4,256,256]{2,1,0:T(8,128)S(1)}, f32[4,2,256,256]{3,2,1,0:T(8,128)S(1)}, f32[2,256,256]{2,1,0:T(8,128)S(1)}) custom-call(s32[4]{0:T(128)S(1)} %copy-done.3, f32[2,256,256]{2,1,0:T(8,128)S(1)} %get-tuple-element.35.refs_1_, f32[2,256,256]{2,1,0:T(8,128)S(1)} %copy-done, ...), custom_call_target="tpu_custom_call" | custom-call | flops 5600000000 | bytes 4194304 | tf_op jit(solution)/shard_map/sweep_1/pallas_call | solution.py:448
  43.8 2.9 %sweep_2.1 = (f32[1,256,256]{2,1,0:T(8,128)S(1)}, f32[1,256,256]{2,1,0:T(8,128)}, f32[1,2,256,256]{3,2,1,0:T(8,128)S(1)}, f32[264,256]{1,0:T(8,128)S(1)}) custom-call(s32[4]{0:T(128)S(1)} %copy-done.3, f32[2,256,256]{2,1,0:T(8,128)S(1)} %get-tuple-element.36.refs_1_, f32[2,256,256]{2,1,0:T(8,128)S(1)} %copy-done, ...), custom_call_target="tpu_custom_call" | custom-call | flops 1400000000 | bytes 1048576 | tf_op jit(solution)/shard_map/sweep_2/pallas_call | solution.py:448
  46.7 1.3 collective-permute-start.11
  48.0 3.9 %collective-permute-done.11.refs_1_ = f32[264,256]{1,0:T(8,128)S(1)} collective-permute-done((f32[264,256]{1,0:T(8,128)S(1)}, f32[264,256]{1,0:T(8,128)S(1)}, u32[]{:S(2)}, u32[]{:S(2)}) %collective-permute-start.11) | collective-permute-done | bytes 270368 | tf_op jit(solution)/shard_map/ppermute | solution.py:545
  57.7 45.6 %collective-permute-done.14.refs_1_ = f32[264,256]{1,0:T(8,128)S(1)} collective-permute-done((f32[264,256]{1,0:T(8,128)S(1)}, f32[264,256]{1,0:T(8,128)S(1)}, u32[]{:S(2)}, u32[]{:S(2)}) %collective-permute-start.14) | collective-permute-done | bytes 270368 | tf_op jit(solution)/shard_map/ppermute | solution.py:545
  103.2 12.6 %outward_2.1 = (f32[8,256]{1,0:T(8,128)S(1)}, f32[8,256]{1,0:T(8,128)S(1)}, f32[8,256]{1,0:T(8,128)S(1)}, f32[8,256]{1,0:T(8,128)S(1)}) custom-call(s32[4]{0:T(128)S(1)} %copy-done.3, f32[264,256]{1,0:T(8,128)S(1)} %collective-permute-done.14.refs_1_, f32[16,1,256]{2,1,0:T(1,128)S(1)} %get-tuple-element.49.refs_2_, f32[8,256]{1,0:T(8,128)S(1)} %get-tuple-element.47.refs_3_, ...), custom_call_target="tpu_custom_call" | custom-call | flops 13440000000 | bytes 10066329 | tf_op jit(solution)/shard_map/outward_2/pallas_call | solution.py:500
  116.5 3.4 %collective-permute-start.15 = (f32[8,256]{1,0:T(8,128)S(1)}, f32[8,256]{1,0:T(8,128)S(1)}, u32[]{:S(2)}, u32[]{:S(2)}) collective-permute-start(f32[8,256]{1,0:T(8,128)S(1)} %get-tuple-element.59), channel_id=1, source_target_pairs={{0,4},{4,8},{8,12},{12,0},{17,21},{21,25},{25,29},{29,17},{33,37},... | collective-permute-start | bytes 24584 | tf_op jit(solution)/shard_map/ppermute | solution.py:545
  119.9 5.6 %collective-permute-start.16 = (f32[8,256]{1,0:T(8,128)S(1)}, f32[8,256]{1,0:T(8,128)S(1)}, u32[]{:S(2)}, u32[]{:S(2)}) collective-permute-start(f32[8,256]{1,0:T(8,128)S(1)} %get-tuple-element.60), channel_id=1, source_target_pairs={{0,8},{4,12},{8,0},{12,4},{17,25},{21,29},{25,17},{29,21},{33,41},... | collective-permute-start | bytes 24584 | tf_op jit(solution)/shard_map/ppermute | solution.py:545
  125.4 2.0 %collective-permute-start.17 = (f32[8,256]{1,0:T(8,128)S(1)}, f32[8,256]{1,0:T(8,128)S(1)}, u32[]{:S(2)}, u32[]{:S(2)}) collective-permute-start(f32[8,256]{1,0:T(8,128)S(1)} %get-tuple-element.61), channel_id=1, source_target_pairs={{0,12},{4,0},{8,4},{12,8},{17,29},{21,17},{25,21},{29,25},{33,45},... | collective-permute-start | bytes 24584 | tf_op jit(solution)/shard_map/ppermute | solution.py:545
  127.5 3.5 %collective-permute-done.17.refs_3_ = f32[8,256]{1,0:T(8,128)S(1)} collective-permute-done((f32[8,256]{1,0:T(8,128)S(1)}, f32[8,256]{1,0:T(8,128)S(1)}, u32[]{:S(2)}, u32[]{:S(2)}) %collective-permute-start.17) | collective-permute-done | bytes 8224 | tf_op jit(solution)/shard_map/ppermute | solution.py:545
  131.6 1.4 deal.1
  134.2 1.5 %collective-permute-done.18 = f32[8,256]{1,0:T(8,128)S(1)} collective-permute-done((f32[8,256]{1,0:T(8,128)}, f32[8,256]{1,0:T(8,128)S(1)}, u32[]{:S(2)}, u32[]{:S(2)}) %collective-permute-start.18) | collective-permute-done | bytes 8224 | tf_op jit(solution)/shard_map/ppermute | solution.py:545
  (56 shorter events, 17.7 us)
Async XLA Ops:
  2.6 9.5 %collective-permute-start.1 = (f32[256,256]{1,0:T(8,128)}, f32[256,256]{1,0:T(8,128)S(1)}, u32[]{:S(2)}, u32[]{:S(2)}) collective-permute-start(f32[256,256]{1,0:T(8,128)} %get-tuple-element.34), channel_id=1, source_target_pairs={{0,4},{1,5},{4,8},{5,9},{8,12},{9,13},{12,0},{13,1},{16,20},{17,21... | collective-permute-start | bytes 786440 | tf_op jit(solution)/shard_map/ppermute | solution.py:545
  4.2 8.3 %collective-permute-start = (f32[256,256]{1,0:T(8,128)}, f32[256,256]{1,0:T(8,128)S(1)}, u32[]{:S(2)}, u32[]{:S(2)}) collective-permute-start(f32[256,256]{1,0:T(8,128)} %get-tuple-element.34), channel_id=1, source_target_pairs={{0,12},{1,13},{4,0},{5,1},{8,4},{9,5},{12,8},{13,9},{16,28},{17,29... | collective-permute-start | bytes 786440 | tf_op jit(solution)/shard_map/ppermute | solution.py:545
  5.8 9.7 %collective-permute-start.5 = (f32[256,256]{1,0:T(8,128)}, f32[256,256]{1,0:T(8,128)S(1)}, u32[]{:S(2)}, u32[]{:S(2)}) collective-permute-start(f32[256,256]{1,0:T(8,128)} %get-tuple-element.34), channel_id=1, source_target_pairs={{0,16},{1,17},{4,20},{5,21},{8,24},{9,25},{12,28},{13,29},{16,0},{... | collective-permute-start | bytes 786440 | tf_op jit(solution)/shard_map/ppermute | solution.py:545
  12.1 6.8 %collective-permute-start.2 = (f32[128,256]{1,0:T(8,128)S(1)}, f32[128,256]{1,0:T(8,128)S(1)}, u32[]{:S(2)}, u32[]{:S(2)}) collective-permute-start(f32[128,256]{1,0:T(8,128)S(1)} %slice.20), channel_id=1, source_target_pairs={{0,4},{1,5},{4,8},{5,9},{8,12},{9,13},{12,0},{13,1},{16,20},{17,21... | collective-permute-start | bytes 393224 | tf_op jit(solution)/shard_map/ppermute | solution.py:545
  12.5 13.0 %copy-start.4 = (f32[256,256]{1,0:T(8,128)}, f32[256,256]{1,0:T(8,128)S(1)}, u32[]{:S(2)}) copy-start(f32[256,256]{1,0:T(8,128)S(1)} %collective-permute-done) | copy-start | bytes 786436
  12.5 14.4 %copy-start = (f32[2,256,256]{2,1,0:T(8,128)S(1)}, f32[2,256,256]{2,1,0:T(8,128)}, u32[]{:S(2)}) copy-start(f32[2,256,256]{2,1,0:T(8,128)} %get-tuple-element.33.refs_2_) | copy-start | bytes 1572868
  12.5 6.5 %collective-permute-start.3 = (f32[128,256]{1,0:T(8,128)S(1)}, f32[128,256]{1,0:T(8,128)S(1)}, u32[]{:S(2)}, u32[]{:S(2)}) collective-permute-start(f32[128,256]{1,0:T(8,128)S(1)} %slice.21), channel_id=1, source_target_pairs={{0,12},{1,13},{4,0},{5,1},{8,4},{9,5},{12,8},{13,9},{16,28},{17,29... | collective-permute-start | bytes 393224 | tf_op jit(solution)/shard_map/ppermute | solution.py:545
  15.5 8.5 %collective-permute-start.8 = (f32[256,256]{1,0:T(8,128)S(1)}, f32[256,256]{1,0:T(8,128)S(1)}, u32[]{:S(2)}, u32[]{:S(2)}) collective-permute-start(f32[256,256]{1,0:T(8,128)S(1)} %collective-permute-done.5), channel_id=1, source_target_pairs={{0,4},{1,5},{4,8},{5,9},{8,12},{9,13},{12,0},{13,1},{16,20},{17,21... | collective-permute-start | bytes 786440 | tf_op jit(solution)/shard_map/ppermute | solution.py:545
  15.5 8.5 %collective-permute-start.6 = (f32[256,256]{1,0:T(8,128)S(1)}, f32[256,256]{1,0:T(8,128)S(1)}, u32[]{:S(2)}, u32[]{:S(2)}) collective-permute-start(f32[256,256]{1,0:T(8,128)S(1)} %collective-permute-done.5), channel_id=1, source_target_pairs={{0,12},{1,13},{4,0},{5,1},{8,4},{9,5},{12,8},{13,9},{16,28},{17,29... | collective-permute-start | bytes 786440 | tf_op jit(solution)/shard_map/ppermute | solution.py:545
  19.1 6.5 %copy-start.5 = (f32[256,256]{1,0:T(8,128)}, f32[256,256]{1,0:T(8,128)S(1)}, u32[]{:S(2)}) copy-start(f32[256,256]{1,0:T(8,128)S(1)} %constant_dynamic-update-slice_fusion) | copy-start | bytes 786436
  19.1 6.5 %collective-permute-start.7 = (f32[256,256]{1,0:T(8,128)S(1)}, f32[256,256]{1,0:T(8,128)S(1)}, u32[]{:S(2)}, u32[]{:S(2)}) collective-permute-start(f32[256,256]{1,0:T(8,128)S(1)} %constant_dynamic-update-slice_fusion), channel_id=1, source_target_pairs={{0,16},{1,17},{4,20},{5,21},{8,24},{9,25},{12,28},{13,29},{16,0},{... | collective-permute-start | bytes 786440 | tf_op jit(solution)/shard_map/ppermute | solution.py:545
  20.7 7.0 %collective-permute-start.4 = (f32[3,256,256]{2,1,0:T(8,128)S(1)}, f32[3,256,256]{2,1,0:T(8,128)S(1)}, u32[]{:S(2)}, u32[]{:S(2)}) collective-permute-start(f32[3,256,256]{2,1,0:T(8,128)S(1)} %pad_maximum_fusion.1.refs_3_), channel_id=1, source_target_pairs={{1,0},{5,4},{9,8},{13,12},{16,17},{20,21},{24,25},{28,29},{32,33},... | collective-permute-start | bytes 2359304 | tf_op jit(solution)/shard_map/ppermute | solution.py:545
  25.5 4.8 %copy-start.3 = (s32[4]{0:T(128)S(1)}, s32[4]{0:T(128)}, u32[]{:S(2)}) copy-start(s32[4]{0:T(128)} %refs_0_.13) | copy-start | bytes 52
  25.6 4.7 %collective-permute-start.9 = (f32[4,256,256]{2,1,0:T(8,128)S(1)}, f32[4,256,256]{2,1,0:T(8,128)}, u32[]{:S(2)}, u32[]{:S(2)}) collective-permute-start(f32[4,256,256]{2,1,0:T(8,128)S(1)} %pad_maximum_fusion.refs_5_), channel_id=1, source_target_pairs={{1,0},{5,4},{9,8},{13,12},{16,17},{20,21},{24,25},{28,29},{32,33},... | collective-permute-start | bytes 3145736 | tf_op jit(solution)/shard_map/ppermute | solution.py:545
  28.8 6.4 %copy-start.6 = (f32[1,256,256]{2,1,0:T(8,128)S(1)}, f32[1,256,256]{2,1,0:T(8,128)}, u32[]{:S(2)}) copy-start(f32[1,256,256]{2,1,0:T(8,128)} %slice.17) | copy-start | bytes 786436
  36.2 7.5 %collective-permute-start.10 = (f32[256,256]{1,0:T(8,128)S(1)}, f32[256,256]{1,0:T(8,128)S(1)}, u32[]{:S(2)}, u32[]{:S(2)}) collective-permute-start(f32[256,256]{1,0:T(8,128)S(1)} %fusion.2.refs_6_), channel_id=1, source_target_pairs={{0,48},{4,52},{8,56},{12,60},{17,33},{21,37},{25,41},{29,45},{33,8... | collective-permute-start | bytes 786440 | tf_op jit(solution)/shard_map/ppermute | solution.py:545
  46.7 5.3 %collective-permute-start.11 = (f32[264,256]{1,0:T(8,128)S(1)}, f32[264,256]{1,0:T(8,128)S(1)}, u32[]{:S(2)}, u32[]{:S(2)}) collective-permute-start(f32[264,256]{1,0:T(8,128)S(1)} %get-tuple-element.38), channel_id=1, source_target_pairs={{0,48},{4,52},{8,56},{12,60},{17,33},{21,37},{25,41},{29,45},{97,8... | collective-permute-start | bytes 811016 | tf_op jit(solution)/shard_map/ppermute | solution.py:545
  53.1 0.7 collective-permute-start.12
  54.4 1.3 collective-permute-start.13
  56.4 46.9 %collective-permute-start.14 = (f32[264,256]{1,0:T(8,128)S(1)}, f32[264,256]{1,0:T(8,128)S(1)}, u32[]{:S(2)}, u32[]{:S(2)}) collective-permute-start(f32[264,256]{1,0:T(8,128)S(1)} %get-tuple-element.48), channel_id=1, source_target_pairs={{33,17},{37,21},{41,25},{45,29},{48,0},{52,4},{56,8},{60,12},{64,1... | collective-permute-start | bytes 811016 | tf_op jit(solution)/shard_map/ppermute | solution.py:545
  116.5 11.0 %collective-permute-start.15 = (f32[8,256]{1,0:T(8,128)S(1)}, f32[8,256]{1,0:T(8,128)S(1)}, u32[]{:S(2)}, u32[]{:S(2)}) collective-permute-start(f32[8,256]{1,0:T(8,128)S(1)} %get-tuple-element.59), channel_id=1, source_target_pairs={{0,4},{4,8},{8,12},{12,0},{17,21},{21,25},{25,29},{29,17},{33,37},... | collective-permute-start | bytes 24584 | tf_op jit(solution)/shard_map/ppermute | solution.py:545
  119.9 7.6 %collective-permute-start.16 = (f32[8,256]{1,0:T(8,128)S(1)}, f32[8,256]{1,0:T(8,128)S(1)}, u32[]{:S(2)}, u32[]{:S(2)}) collective-permute-start(f32[8,256]{1,0:T(8,128)S(1)} %get-tuple-element.60), channel_id=1, source_target_pairs={{0,8},{4,12},{8,0},{12,4},{17,25},{21,29},{25,17},{29,21},{33,41},... | collective-permute-start | bytes 24584 | tf_op jit(solution)/shard_map/ppermute | solution.py:545
  125.4 5.5 %collective-permute-start.17 = (f32[8,256]{1,0:T(8,128)S(1)}, f32[8,256]{1,0:T(8,128)S(1)}, u32[]{:S(2)}, u32[]{:S(2)}) collective-permute-start(f32[8,256]{1,0:T(8,128)S(1)} %get-tuple-element.61), channel_id=1, source_target_pairs={{0,12},{4,0},{8,4},{12,8},{17,29},{21,17},{25,21},{29,25},{33,45},... | collective-permute-start | bytes 24584 | tf_op jit(solution)/shard_map/ppermute | solution.py:545
  132.9 2.8 %collective-permute-start.18 = (f32[8,256]{1,0:T(8,128)}, f32[8,256]{1,0:T(8,128)S(1)}, u32[]{:S(2)}, u32[]{:S(2)}) collective-permute-start(f32[8,256]{1,0:T(8,128)} %get-tuple-element.63), channel_id=1, source_target_pairs={{0,16},{4,20},{8,24},{12,28},{17,1},{21,5},{25,9},{29,13},{33,49},... | collective-permute-start | bytes 24584 | tf_op jit(solution)/shard_map/ppermute | solution.py:545
  (5 other events, 13.0 us)

commit v3 on v2

--- a/solution.py
+++ b/solution.py
@@ -66,11 +66,13 @@
 
 def chain_step(energy, onsite, lead, sr, si):
     _, _, dr, di, fr, fi = diagonal_and_rest(energy, onsite, sr, si)
-    frs, fis, leads = split(fr), split(fi), split(lead)
-    pr, pi = dot3(leads, frs), dot3(leads, fis)
+    frh, fih = fr.astype(b16), fi.astype(b16)
+    leads = jnp.concatenate(split(lead), axis=0)
+    pr, pi = dot_nt(leads, frh), dot_nt(leads, fih)
+    pr, pi = pr[:W] + pr[W:], pi[:W] + pi[W:]
     prh, pih = pr.astype(b16), pi.astype(b16)
-    qr = dot_nt(prh, frs[0]) - dot_nt(pih, fis[0])
-    qi = dot_nt(prh, fis[0]) + dot_nt(pih, frs[0])
+    qr = dot_nt(prh, frh) - dot_nt(pih, fih)
+    qi = dot_nt(prh, fih) + dot_nt(pih, frh)
     x = lead - pr
     xr, xi = x * dr + pi * di, x * di - pi * dr
     return cdot3((xr, xi), (lead + qr, qi))
@@ -110,6 +112,8 @@
 
 
 def here(name):
+    if name == "x":
+        return 2 * lax.axis_index("pair") + lax.axis_index("row")
     return lax.axis_index(name)
 
 
@@ -174,7 +178,7 @@
 
 
 STEPS = ((0, 3), (3, 7), (7, 8), (8, 16))
-OUTWARD = ((1, 4), (4, 8), (8, 16))
+OUTWARD = ((1, 5), (5, 8), (8, 16))
 
 
 def kept_at(t):
@@ -191,13 +195,16 @@
     both, own_mine, own_sent, near_mine, near_sent = (refs.pop(0) for _ in range(5))
     bridge = refs.pop(0) if part > 1 else None
     wire_h, wire_m, store, last = (refs.pop(0) for _ in range(4))
+    link, link_sem = (refs.pop(0), refs.pop()) if part == 0 else (None, None)
     hbuf, mbuf, sbuf, in_sem, out_sem = refs
     half, y, core = here("half"), here("y"), here("core")
     energy = energy_of(index)
 
     def start_from(chunk, column, kind, target, sem):
+        start_row(core == (0 if chunk in (0, 3) else 1), column, kind, target, sem)
+
+    def start_row(own_row, column, kind, target, sem):
         away = lax.rem(column - y + 4, 4)
-        own_row = core == (0 if chunk in (0, 3) else 1)
 
         @pl.when(own_row & (away == 0))
         def _():
@@ -212,6 +219,11 @@
             @pl.when(~own_row & here_too)
             def _():
                 pltpu.make_async_copy(near.at[away], target, sem).start()
+
+    if part == 0:
+        @pl.when(on_task())
+        def _():
+            start_row(lax.rem(here("x"), 2) == 1, 3, 1, link, link_sem.at[0])
 
     @pl.when(on_task() & (is_outer() if part < 3 else ~is_outer()))
     def _():
@@ -268,6 +280,12 @@
         for n in range(count):
             for copy in kept(n):
                 copy.wait()
+
+    if part == 0:
+
+        @pl.when(on_task())
+        def _():
+            pltpu.make_async_copy(both.at[1], link, link_sem.at[0]).wait()
 
 
 def middle_kernel(index, arrived, wire_h, wire_m, store, carried, crossing, spectrum, hbuf, mbuf, sbuf, in_sem):
@@ -311,9 +329,9 @@
     totals = [refs.pop(0) for _ in range(2)] if leg else None
     links = [refs.pop(0) for _ in range(2)] if leg == 1 else None
     kept = {place: refs.pop(0) for place in places}
-    outs = [refs.pop(0) for _ in range(4 if leg == 2 else 2)]
+    outs = [refs.pop(0) for _ in range(1 if leg == 2 else 2)]
     hbuf, mbuf, sbuf, carried, spectra, in_sem = refs
-    half, x, y = here("half"), here("x"), here("y")
+    half = here("half")
     energy = energy_of(index)
 
     @pl.when(on_task() & (is_outer() if leg == 2 else ~is_outer()))
@@ -383,24 +401,17 @@
 
             outer_total = start[pl.ds(2 * H2, 8), :]
             total = jnp.where(is_outer(), outer_total, totals[0][...] + totals[1][...])
-            partner = x + 1 - 2 * lax.rem(x, 2)
-            for shift in range(4):
-                column = lax.rem(y + shift, 4)
-                outs[shift][pl.ds(0, 1), :] = spectra[4 * x + column]
-                outs[shift][pl.ds(1, 1), :] = spectra[4 * partner + column]
-                outs[shift][pl.ds(2, 6), :] = total[2:8]
-
-
-def deal_kernel(*refs):
-    pieces, outs, stack = refs[:4], refs[4:6], refs[6]
-    y = here("y")
-    for shift in range(4):
-        stack[shift] = pieces[shift][...]
+            base = 8 * lax.axis_index("pair")
+            for place in range(8):
+                outs[0][place, pl.ds(0, 1), :] = spectra[base + place]
+                outs[0][place, pl.ds(1, 7), :] = total[1:8]
+
+
+def deal_kernel(pieces, spectral, totals):
+    row = jnp.where(lax.axis_index("pair") == 0, here("core"), 1 - here("core"))
     for e in range(4):
-        shift = lax.rem(y - e + 4, 4)
-        for row in range(2):
-            outs[row][pl.ds(e, 1), :] = stack[shift, pl.ds(row, 1), :]
-            outs[row][pl.ds(4 + e, 1), :] = stack[shift, pl.ds(2, 1), :]
+        spectral[pl.ds(e, 1), :] = pieces[4 * row + e, pl.ds(0, 1), :]
+        totals[e] = jnp.max(pieces[4 * row + e, pl.ds(1, 1), :])
 
 
 def vmem():
@@ -445,18 +456,24 @@
         arrays.append(bridge)
     outs = [shape(count, W, W), shape(count, W, W), shape(count, 2, W, W)]
     outs.append(shape(2 * H2 + 8, W) if part > 1 else shape(2, W, W))
+    specs = [anywhere(), anywhere(), anywhere(), vmem()]
+    scratch = [
+        pltpu.VMEM((count, W, W), f32),
+        pltpu.VMEM((count, W, W), f32),
+        pltpu.VMEM((count + 1, 2, W, W), f32),
+        pltpu.SemaphoreType.DMA((count, 2)),
+        pltpu.SemaphoreType.DMA((count, 3)),
+    ]
+    if part == 0:
+        outs.append(shape(W, W))
+        specs.append(anywhere())
+        scratch.append(pltpu.SemaphoreType.DMA((1,)))
     return pl.pallas_call(
         functools.partial(sweep_kernel, part),
         out_shape=tuple(outs),
         in_specs=[smem(), vmem()] + [anywhere()] * len(arrays),
-        out_specs=[anywhere(), anywhere(), anywhere(), vmem()],
-        scratch_shapes=[
-            pltpu.VMEM((count, W, W), f32),
-            pltpu.VMEM((count, W, W), f32),
-            pltpu.VMEM((count + 1, 2, W, W), f32),
-            pltpu.SemaphoreType.DMA((count, 2)),
-            pltpu.SemaphoreType.DMA((count, 3)),
-        ],
+        out_specs=specs,
+        scratch_shapes=scratch,
         name="sweep_%d" % part,
         compiler_params=params(),
         cost_estimate=cost(count),
@@ -495,7 +512,7 @@
     outs = {
         0: [shape(2, W, W), shape(16, 1, W)],
         1: [shape(2 * H2 + 8, W), shape(16, 1, W)],
-        2: [shape(8, W)] * 4,
+        2: [shape(8, 8, W)],
     }[leg]
     return pl.pallas_call(
         functools.partial(outward_kernel, leg, places),
@@ -519,15 +536,14 @@
 def deal(pieces):
     return pl.pallas_call(
         deal_kernel,
-        out_shape=(shape(8, W), shape(8, W)),
-        in_specs=[vmem()] * 4,
-        out_specs=[vmem()] * 2,
-        scratch_shapes=[pltpu.VMEM((4, 8, W), f32)],
+        out_shape=(shape(4, W), shape(4)),
+        in_specs=[vmem()],
+        out_specs=[vmem(), smem()],
         name="deal",
-    )(*pieces)
-
-
-AXES = ("half", "x", "y", "core")
+    )(pieces)
+
+
+AXES = ("half", "pair", "row", "y", "core")
 
 
 def at(half, x, y, core):
@@ -577,12 +593,7 @@
     return moved(value, lambda half, x, y, core: (half, x, y, 1 - core), lambda *place: not is_task(*place))
 
 
-def after(value, other):
-    return lax.optimization_barrier((value, other))[0]
-
-
 def on_device(onsite, coupling, pattern, contact_rates, energy_index):
-    x, y = here("x"), here("y")
     both, mine = prepare(pattern[0], onsite[0], coupling[0])
     near = to_partner(mine)
     left, right = along_y(mine, 1), along_y(mine, -1)
@@ -591,13 +602,7 @@
     near_row = jnp.stack([near, along_y(near, -1), to_partner(opposite), along_y(near, 1)])
     own_sent, near_sent = across(own_row), across(near_row)
     sets = (both, own_row, own_sent, near_row, near_sent)
-    *first, carry = sweep(0, energy_index, contact_rates, sets)
-
-    links = here("core") == 1
-    own_links = jnp.concatenate([both[1:], jnp.where(links, own_row, own_sent)], axis=0)
-    near_links = jnp.where(links, near_row, near_sent)
-    row_links = jnp.where(lax.rem(x, 2) == 1, own_links, near_links)
-    link = after(lax.dynamic_index_in_dim(row_links, lax.rem(7 - y, 4), 0, keepdims=False), carry)
+    *first, carry, link = sweep(0, energy_index, contact_rates, sets)
     bridge = moved(
         link,
         lambda half, x, y, core: (half if x < 2 else 1, 3 - x, y, core),
@@ -617,17 +622,15 @@
     carry, earlier = outward(0, energy_index, carry, earlier, [], [], kept)
     leaving, earlier = outward(1, energy_index, carry, earlier, totals, [bridge, link], kept)
     arrived = to_next(leaving, inner_task)
-    pieces = outward(2, energy_index, arrived, earlier, totals, [], kept)
-
-    pieces = [pieces[0]] + [along_y(pieces[shift], shift, is_task) for shift in (1, 2, 3)]
-    own, other = deal(pieces)
-    result = jnp.where(on_task(), own, to_partner(other, is_task))
-    return result[:4][None], result[4:, 0]
+    (pieces,) = outward(2, energy_index, arrived, earlier, totals, [], kept)
+    pieces = lax.all_to_all(pieces, ("row", "y"), 0, 0)
+    spectral, totals = deal(pieces)
+    return spectral[None], totals
 
 
 def solution(mesh):
-    fine = Mesh(mesh.devices.reshape(2, 4, 4, 2, 2), ("half", "x", "y", "plane", "core"))
-    slab = ("half", "x", "y")
+    fine = Mesh(mesh.devices.reshape(2, 2, 2, 4, 2, 2), ("half", "pair", "row", "y", "plane", "core"))
+    slab = ("half", "pair", "row", "y")
     part = ("plane", "core")
     return jax.shard_map(
         on_device,

time: 139 us -> 126 us (0.906)
  blocking collectives: 0 us -> 11.2 us
  starting transfers between devices: 33 us -> 21.8 us
  waiting for transfers between devices: 64.6 us -> 59.4 us
  local copies, waits for them, and re-layouts: 3.17 us -> 0.06 us
  other arithmetic: 3.03 us -> 0.13 us
  Pallas kernels: 32.9 us -> 30.6 us
    all_to_all x0 -> x1, blocking collectives: none -> 11.2 us  [on_device(): pieces = lax.all_to_all(pieces, ('row', 'y'), 0, 0)]
    ppermute x19 -> x15, starting transfers between devices: 33 us -> 21.8 us  [moved(): return lax.ppermute(value, AXES, pairs)]
    ppermute x19 -> x15, waiting for transfers between devices: 64.6 us -> 59.4 us  [moved(): return lax.ppermute(value, AXES, pairs)]
    select_n x2 -> x0, other arithmetic: 1.86 us -> none  [the longest x1 1.16 us: on_device(): jnp.where(links, own_row, own_sent)]
    pallas_call x4, Pallas kernels: 15.1 us -> 13.4 us  [sweep(): pl.pallas_call(functools.partial(sweep_kernel, part), out_shape=tuple(out...]
  transfers between devices with their start and end apart: 19 -> 15, of which waited for: 10 -> 8; matrix products, arithmetic and copies ran while one was open for 1% -> 0% of each run, Pallas kernels for 5% -> 5%
where the time goes in v3:
time: 126 us; the launch traced here: 124 us
  waiting for transfers between devices  59.4 us (47%)
  Pallas kernels  30.6 us (24%)
  starting transfers between devices  21.8 us (17%)
  blocking collectives  11.2 us (9%)
    ppermute x15, waiting for transfers between devices, moved(): return lax.ppermute(value, AXES, pairs)  59.4 us
    ppermute x15, starting transfers between devices, moved(): return lax.ppermute(value, AXES, pairs)  21.8 us
    pallas_call x4, Pallas kernels, sweep(): pl.pallas_call(functools.partial(sweep_kernel, part), out_shape=tuple(out...  13.4 us
    pallas_call x3, Pallas kernels, outward(): pl.pallas_call(functools.partial(outward_kernel, leg, places), out_shape=...  13.2 us
    all_to_all x1, blocking collectives, on_device(): pieces = lax.all_to_all(pieces, ('row', 'y'), 0, 0)  11.2 us
  transfers between devices with their start and end apart: 15, of which 8 were waited for; matrix products, arithmetic and copies ran while one was open for 0% of the time, Pallas kernels for 5%

profile of v3, /device:TPU:64, one launch (start us, length us, event | category | flops | bytes accessed | tf_op | source)
XLA Modules:
  0.0 124.2 jit_solution(15577294607945317955)
XLA Ops:
  0.6 2.0 %prepare.1 = (f32[2,256,256]{2,1,0:T(8,128)}, f32[256,256]{1,0:T(8,128)}) custom-call(s32[4,4]{1,0:T(4,128)} %bitcast.20, f32[256,256]{1,0:T(8,128)} %bitcast.14, f32[256,256]{1,0:T(8,128)} %bitcast.15), custom_call_target="tpu_custom_call" | custom-call | tf_op jit(solution)/shard_map/prepare/pallas_call | solution.py:442
  2.6 1.6 %collective-permute-start.1 = (f32[256,256]{1,0:T(8,128)}, f32[256,256]{1,0:T(8,128)S(1)}, u32[]{:S(2)}, u32[]{:S(2)}) collective-permute-start(f32[256,256]{1,0:T(8,128)} %get-tuple-element.30), channel_id=1, source_target_pairs={{0,4},{1,5},{4,8},{5,9},{8,12},{9,13},{12,0},{13,1},{16,20},{17,21... | collective-permute-start | bytes 786440 | tf_op jit(solution)/shard_map/ppermute | solution.py:561
  4.2 1.7 %collective-permute-start = (f32[256,256]{1,0:T(8,128)}, f32[256,256]{1,0:T(8,128)S(1)}, u32[]{:S(2)}, u32[]{:S(2)}) collective-permute-start(f32[256,256]{1,0:T(8,128)} %get-tuple-element.30), channel_id=1, source_target_pairs={{0,12},{1,13},{4,0},{5,1},{8,4},{9,5},{12,8},{13,9},{16,28},{17,29... | collective-permute-start | bytes 786440 | tf_op jit(solution)/shard_map/ppermute | solution.py:561
  5.8 1.5 %collective-permute-start.5 = (f32[256,256]{1,0:T(8,128)}, f32[256,256]{1,0:T(8,128)S(1)}, u32[]{:S(2)}, u32[]{:S(2)}) collective-permute-start(f32[256,256]{1,0:T(8,128)} %get-tuple-element.30), channel_id=1, source_target_pairs={{0,16},{1,17},{4,20},{5,21},{8,24},{9,25},{12,28},{13,29},{16,0},{... | collective-permute-start | bytes 786440 | tf_op jit(solution)/shard_map/ppermute | solution.py:561
  7.3 4.8 %collective-permute-done.1 = f32[256,256]{1,0:T(8,128)S(1)} collective-permute-done((f32[256,256]{1,0:T(8,128)}, f32[256,256]{1,0:T(8,128)S(1)}, u32[]{:S(2)}, u32[]{:S(2)}) %collective-permute-start.1) | collective-permute-done | bytes 262176 | tf_op jit(solution)/shard_map/ppermute | solution.py:561
  12.6 3.0 %collective-permute-start.3 = (f32[128,256]{1,0:T(8,128)S(1)}, f32[128,256]{1,0:T(8,128)S(1)}, u32[]{:S(2)}, u32[]{:S(2)}) collective-permute-start(f32[128,256]{1,0:T(8,128)S(1)} %slice.9), channel_id=1, source_target_pairs={{0,12},{1,13},{4,0},{5,1},{8,4},{9,5},{12,8},{13,9},{16,28},{17,29... | collective-permute-start | bytes 393224 | tf_op jit(solution)/shard_map/ppermute | solution.py:561
  15.6 3.2 %collective-permute-start.6 = (f32[256,256]{1,0:T(8,128)S(1)}, f32[256,256]{1,0:T(8,128)S(1)}, u32[]{:S(2)}, u32[]{:S(2)}) collective-permute-start(f32[256,256]{1,0:T(8,128)S(1)} %collective-permute-done.5), channel_id=1, source_target_pairs={{0,12},{1,13},{4,0},{5,1},{8,4},{9,5},{12,8},{13,9},{16,28},{17,29... | collective-permute-start | bytes 786440 | tf_op jit(solution)/shard_map/ppermute | solution.py:561
  19.1 1.6 %collective-permute-start.7 = (f32[256,256]{1,0:T(8,128)S(1)}, f32[256,256]{1,0:T(8,128)S(1)}, u32[]{:S(2)}, u32[]{:S(2)}) collective-permute-start(f32[256,256]{1,0:T(8,128)S(1)} %constant_dynamic-update-slice_fusion), channel_id=1, source_target_pairs={{0,16},{1,17},{4,20},{5,21},{8,24},{9,25},{12,28},{13,29},{16,0},{... | collective-permute-start | bytes 786440 | tf_op jit(solution)/shard_map/ppermute | solution.py:561
  20.7 3.4 %collective-permute-done.8 = f32[256,256]{1,0:T(8,128)S(1)} collective-permute-done((f32[256,256]{1,0:T(8,128)S(1)}, f32[256,256]{1,0:T(8,128)S(1)}, u32[]{:S(2)}, u32[]{:S(2)}) %collective-permute-start.8) | collective-permute-done | bytes 262176 | tf_op jit(solution)/shard_map/ppermute | solution.py:561
  24.0 1.5 %collective-permute-done.7 = f32[256,256]{1,0:T(8,128)S(1)} collective-permute-done((f32[256,256]{1,0:T(8,128)S(1)}, f32[256,256]{1,0:T(8,128)S(1)}, u32[]{:S(2)}, u32[]{:S(2)}) %collective-permute-start.7) | collective-permute-done | bytes 262176 | tf_op jit(solution)/shard_map/ppermute | solution.py:561
  25.6 1.3 %collective-permute-start.9 = (f32[4,256,256]{2,1,0:T(8,128)S(1)}, f32[4,256,256]{2,1,0:T(8,128)S(1)}, u32[]{:S(2)}, u32[]{:S(2)}) collective-permute-start(f32[4,256,256]{2,1,0:T(8,128)S(1)} %pad_maximum_fusion.refs_5_), channel_id=1, source_target_pairs={{1,0},{5,4},{9,8},{13,12},{16,17},{20,21},{24,25},{28,29},{32,33},... | collective-permute-start | bytes 3145736 | tf_op jit(solution)/shard_map/ppermute | solution.py:561
  27.0 1.3 %collective-permute-start.4 = (f32[3,256,256]{2,1,0:T(8,128)S(1)}, f32[3,256,256]{2,1,0:T(8,128)S(1)}, u32[]{:S(2)}, u32[]{:S(2)}) collective-permute-start(f32[3,256,256]{2,1,0:T(8,128)S(1)} %pad_maximum_fusion.1.refs_3_), channel_id=1, source_target_pairs={{1,0},{5,4},{9,8},{13,12},{16,17},{20,21},{24,25},{28,29},{32,33},... | collective-permute-start | bytes 2359304 | tf_op jit(solution)/shard_map/ppermute | solution.py:561
  28.3 3.0 %collective-permute-done.4.refs_4_ = f32[3,256,256]{2,1,0:T(8,128)S(1)} collective-permute-done((f32[3,256,256]{2,1,0:T(8,128)S(1)}, f32[3,256,256]{2,1,0:T(8,128)S(1)}, u32[]{:S(2)}, u32[]{:S(2)}) %collective-permute-start.4) | collective-permute-done | bytes 786464 | tf_op jit(solution)/shard_map/ppermute | solution.py:561
  31.3 4.6 %sweep_0.1 = (f32[3,256,256]{2,1,0:T(8,128)S(1)}, f32[3,256,256]{2,1,0:T(8,128)S(1)}, f32[3,2,256,256]{3,2,1,0:T(8,128)S(1)}, f32[2,256,256]{2,1,0:T(8,128)S(1)}, f32[256,256]{1,0:T(8,128)S(1)}) custom-call(s32[4]{0:T(128)S(1)} %copy-done.2, f32[2,256]{1,0:T(2,128)S(1)} %copy-done.1, f32[2,256,256]{2,1,0:T(8,128)S(1)} %copy-done, ...), custom_call_target="tpu_custom_call" | custom-call | flops 4200000000 | bytes 3145728 | tf_op jit(solution)/shard_map/sweep_0/pallas_call | solution.py:471
  35.9 1.3 %collective-permute-start.10 = (f32[256,256]{1,0:T(8,128)S(1)}, f32[256,256]{1,0:T(8,128)S(1)}, u32[]{:S(2)}, u32[]{:S(2)}) collective-permute-start(f32[256,256]{1,0:T(8,128)S(1)} %get-tuple-element.33.refs_6_), channel_id=1, source_target_pairs={{0,48},{4,52},{8,56},{12,60},{17,33},{21,37},{25,41},{29,45},{33,8... | collective-permute-start | bytes 786440 | tf_op jit(solution)/shard_map/ppermute | solution.py:561
  37.2 5.8 %sweep_1.1 = (f32[4,256,256]{2,1,0:T(8,128)S(1)}, f32[4,256,256]{2,1,0:T(8,128)S(1)}, f32[4,2,256,256]{3,2,1,0:T(8,128)S(1)}, f32[2,256,256]{2,1,0:T(8,128)S(1)}) custom-call(s32[4]{0:T(128)S(1)} %copy-done.2, f32[2,256,256]{2,1,0:T(8,128)S(1)} %get-tuple-element.31.refs_1_, f32[2,256,256]{2,1,0:T(8,128)S(1)} %copy-done, ...), custom_call_target="tpu_custom_call" | custom-call | flops 5600000000 | bytes 4194304 | tf_op jit(solution)/shard_map/sweep_1/pallas_call | solution.py:471
  43.0 1.9 %sweep_2.1 = (f32[1,256,256]{2,1,0:T(8,128)S(1)}, f32[1,256,256]{2,1,0:T(8,128)}, f32[1,2,256,256]{3,2,1,0:T(8,128)S(1)}, f32[264,256]{1,0:T(8,128)S(1)}) custom-call(s32[4]{0:T(128)S(1)} %copy-done.2, f32[2,256,256]{2,1,0:T(8,128)S(1)} %get-tuple-element.32.refs_1_, f32[2,256,256]{2,1,0:T(8,128)S(1)} %copy-done, ...), custom_call_target="tpu_custom_call" | custom-call | flops 1400000000 | bytes 1048576 | tf_op jit(solution)/shard_map/sweep_2/pallas_call | solution.py:471
  44.9 2.4 %collective-permute-start.11 = (f32[264,256]{1,0:T(8,128)S(1)}, f32[264,256]{1,0:T(8,128)S(1)}, u32[]{:S(2)}, u32[]{:S(2)}) collective-permute-start(f32[264,256]{1,0:T(8,128)S(1)} %get-tuple-element.34), channel_id=1, source_target_pairs={{0,48},{4,52},{8,56},{12,60},{17,33},{21,37},{25,41},{29,45},{97,8... | collective-permute-start | bytes 811016 | tf_op jit(solution)/shard_map/ppermute | solution.py:561
  47.3 3.9 %collective-permute-done.11.refs_1_ = f32[264,256]{1,0:T(8,128)S(1)} collective-permute-done((f32[264,256]{1,0:T(8,128)S(1)}, f32[264,256]{1,0:T(8,128)S(1)}, u32[]{:S(2)}, u32[]{:S(2)}) %collective-permute-start.11) | collective-permute-done | bytes 270368 | tf_op jit(solution)/shard_map/ppermute | solution.py:561
  55.7 1.3 %collective-permute-start.14 = (f32[264,256]{1,0:T(8,128)S(1)}, f32[264,256]{1,0:T(8,128)S(1)}, u32[]{:S(2)}, u32[]{:S(2)}) collective-permute-start(f32[264,256]{1,0:T(8,128)S(1)} %get-tuple-element.44), channel_id=1, source_target_pairs={{33,17},{37,21},{41,25},{45,29},{48,0},{52,4},{56,8},{60,12},{64,1... | collective-permute-start | bytes 811016 | tf_op jit(solution)/shard_map/ppermute | solution.py:561
  57.0 42.5 %collective-permute-done.14.refs_1_ = f32[264,256]{1,0:T(8,128)S(1)} collective-permute-done((f32[264,256]{1,0:T(8,128)S(1)}, f32[264,256]{1,0:T(8,128)S(1)}, u32[]{:S(2)}, u32[]{:S(2)}) %collective-permute-start.14) | collective-permute-done | bytes 270368 | tf_op jit(solution)/shard_map/ppermute | solution.py:561
  99.5 11.9 %outward_2.1 = f32[8,8,256]{2,1,0:T(8,128)S(1)} custom-call(s32[4]{0:T(128)S(1)} %copy-done.2, f32[264,256]{1,0:T(8,128)S(1)} %collective-permute-done.14.refs_1_, f32[16,1,256]{2,1,0:T(1,128)S(1)} %get-tuple-element.45.refs_2_, f32[8,256]{1,0:T(8,128)S(1)} %get-tuple-element.43.refs_3_, f32[8,256]{1,0:T(8,128)S(1)} %collective-permute-done.13.refs_4_, ...), custom_call_target="tpu_custom_call" | custom-call | flops 13440000000 | bytes 10066329 | tf_op jit(solution)/shard_map/outward_2/pallas_call | solution.py:517
  111.4 11.2 %all_to_all.5.pieces = f32[8,8,256]{2,1,0:T(8,128)} all-to-all(f32[8,8,256]{2,1,0:T(8,128)S(1)} %outward_2.1), channel_id=1, replica_groups=mesh['half'=2,'pair'=2,'row'=2,'y'=4,'plane'=2,'core'=2] {'row','y'}, dimensions={0} | all-to-all | bytes 131072 | tf_op jit(solution)/shard_map/all_to_all | solution.py:626
  122.6 1.5 %deal.1 = (f32[4,256]{1,0:T(4,128)}, f32[4]{0:T(128)}) custom-call(f32[8,8,256]{2,1,0:T(8,128)} %all_to_all.5.pieces), custom_call_target="tpu_custom_call" | custom-call | tf_op jit(solution)/shard_map/deal/pallas_call | solution.py:537
  (29 shorter events, 5.2 us)
Async XLA Ops:
  2.6 9.5 %collective-permute-start.1 = (f32[256,256]{1,0:T(8,128)}, f32[256,256]{1,0:T(8,128)S(1)}, u32[]{:S(2)}, u32[]{:S(2)}) collective-permute-start(f32[256,256]{1,0:T(8,128)} %get-tuple-element.30), channel_id=1, source_target_pairs={{0,4},{1,5},{4,8},{5,9},{8,12},{9,13},{12,0},{13,1},{16,20},{17,21... | collective-permute-start | bytes 786440 | tf_op jit(solution)/shard_map/ppermute | solution.py:561
  4.2 8.3 %collective-permute-start = (f32[256,256]{1,0:T(8,128)}, f32[256,256]{1,0:T(8,128)S(1)}, u32[]{:S(2)}, u32[]{:S(2)}) collective-permute-start(f32[256,256]{1,0:T(8,128)} %get-tuple-element.30), channel_id=1, source_target_pairs={{0,12},{1,13},{4,0},{5,1},{8,4},{9,5},{12,8},{13,9},{16,28},{17,29... | collective-permute-start | bytes 786440 | tf_op jit(solution)/shard_map/ppermute | solution.py:561
  5.8 9.7 %collective-permute-start.5 = (f32[256,256]{1,0:T(8,128)}, f32[256,256]{1,0:T(8,128)S(1)}, u32[]{:S(2)}, u32[]{:S(2)}) collective-permute-start(f32[256,256]{1,0:T(8,128)} %get-tuple-element.30), channel_id=1, source_target_pairs={{0,16},{1,17},{4,20},{5,21},{8,24},{9,25},{12,28},{13,29},{16,0},{... | collective-permute-start | bytes 786440 | tf_op jit(solution)/shard_map/ppermute | solution.py:561
  12.1 6.8 %collective-permute-start.2 = (f32[128,256]{1,0:T(8,128)S(1)}, f32[128,256]{1,0:T(8,128)S(1)}, u32[]{:S(2)}, u32[]{:S(2)}) collective-permute-start(f32[128,256]{1,0:T(8,128)S(1)} %slice.8), channel_id=1, source_target_pairs={{0,4},{1,5},{4,8},{5,9},{8,12},{9,13},{12,0},{13,1},{16,20},{17,21... | collective-permute-start | bytes 393224 | tf_op jit(solution)/shard_map/ppermute | solution.py:561
  12.5 18.8 %copy-start = (f32[2,256,256]{2,1,0:T(8,128)S(1)}, f32[2,256,256]{2,1,0:T(8,128)}, u32[]{:S(2)}) copy-start(f32[2,256,256]{2,1,0:T(8,128)} %get-tuple-element.29.refs_2_) | copy-start | bytes 1572868
  12.5 18.8 %copy-start.1 = (f32[2,256]{1,0:T(2,128)S(1)}, f32[2,256]{1,0:T(2,128)}, u32[]{:S(2)}) copy-start(f32[2,256]{1,0:T(2,128)} %refs_1_.1) | copy-start | bytes 6148
  12.6 18.8 %copy-start.2 = (s32[4]{0:T(128)S(1)}, s32[4]{0:T(128)}, u32[]{:S(2)}) copy-start(s32[4]{0:T(128)} %refs_0_.13) | copy-start | bytes 52
  12.6 6.5 %collective-permute-start.3 = (f32[128,256]{1,0:T(8,128)S(1)}, f32[128,256]{1,0:T(8,128)S(1)}, u32[]{:S(2)}, u32[]{:S(2)}) collective-permute-start(f32[128,256]{1,0:T(8,128)S(1)} %slice.9), channel_id=1, source_target_pairs={{0,12},{1,13},{4,0},{5,1},{8,4},{9,5},{12,8},{13,9},{16,28},{17,29... | collective-permute-start | bytes 393224 | tf_op jit(solution)/shard_map/ppermute | solution.py:561
  15.6 8.4 %collective-permute-start.8 = (f32[256,256]{1,0:T(8,128)S(1)}, f32[256,256]{1,0:T(8,128)S(1)}, u32[]{:S(2)}, u32[]{:S(2)}) collective-permute-start(f32[256,256]{1,0:T(8,128)S(1)} %collective-permute-done.5), channel_id=1, source_target_pairs={{0,4},{1,5},{4,8},{5,9},{8,12},{9,13},{12,0},{13,1},{16,20},{17,21... | collective-permute-start | bytes 786440 | tf_op jit(solution)/shard_map/ppermute | solution.py:561
  15.6 8.4 %collective-permute-start.6 = (f32[256,256]{1,0:T(8,128)S(1)}, f32[256,256]{1,0:T(8,128)S(1)}, u32[]{:S(2)}, u32[]{:S(2)}) collective-permute-start(f32[256,256]{1,0:T(8,128)S(1)} %collective-permute-done.5), channel_id=1, source_target_pairs={{0,12},{1,13},{4,0},{5,1},{8,4},{9,5},{12,8},{13,9},{16,28},{17,29... | collective-permute-start | bytes 786440 | tf_op jit(solution)/shard_map/ppermute | solution.py:561
  19.1 6.5 %collective-permute-start.7 = (f32[256,256]{1,0:T(8,128)S(1)}, f32[256,256]{1,0:T(8,128)S(1)}, u32[]{:S(2)}, u32[]{:S(2)}) collective-permute-start(f32[256,256]{1,0:T(8,128)S(1)} %constant_dynamic-update-slice_fusion), channel_id=1, source_target_pairs={{0,16},{1,17},{4,20},{5,21},{8,24},{9,25},{12,28},{13,29},{16,0},{... | collective-permute-start | bytes 786440 | tf_op jit(solution)/shard_map/ppermute | solution.py:561
  25.6 5.7 %collective-permute-start.9 = (f32[4,256,256]{2,1,0:T(8,128)S(1)}, f32[4,256,256]{2,1,0:T(8,128)S(1)}, u32[]{:S(2)}, u32[]{:S(2)}) collective-permute-start(f32[4,256,256]{2,1,0:T(8,128)S(1)} %pad_maximum_fusion.refs_5_), channel_id=1, source_target_pairs={{1,0},{5,4},{9,8},{13,12},{16,17},{20,21},{24,25},{28,29},{32,33},... | collective-permute-start | bytes 3145736 | tf_op jit(solution)/shard_map/ppermute | solution.py:561
  27.0 4.3 %collective-permute-start.4 = (f32[3,256,256]{2,1,0:T(8,128)S(1)}, f32[3,256,256]{2,1,0:T(8,128)S(1)}, u32[]{:S(2)}, u32[]{:S(2)}) collective-permute-start(f32[3,256,256]{2,1,0:T(8,128)S(1)} %pad_maximum_fusion.1.refs_3_), channel_id=1, source_target_pairs={{1,0},{5,4},{9,8},{13,12},{16,17},{20,21},{24,25},{28,29},{32,33},... | collective-permute-start | bytes 2359304 | tf_op jit(solution)/shard_map/ppermute | solution.py:561
  35.9 7.1 %collective-permute-start.10 = (f32[256,256]{1,0:T(8,128)S(1)}, f32[256,256]{1,0:T(8,128)S(1)}, u32[]{:S(2)}, u32[]{:S(2)}) collective-permute-start(f32[256,256]{1,0:T(8,128)S(1)} %get-tuple-element.33.refs_6_), channel_id=1, source_target_pairs={{0,48},{4,52},{8,56},{12,60},{17,33},{21,37},{25,41},{29,45},{33,8... | collective-permute-start | bytes 786440 | tf_op jit(solution)/shard_map/ppermute | solution.py:561
  44.9 6.3 %collective-permute-start.11 = (f32[264,256]{1,0:T(8,128)S(1)}, f32[264,256]{1,0:T(8,128)S(1)}, u32[]{:S(2)}, u32[]{:S(2)}) collective-permute-start(f32[264,256]{1,0:T(8,128)S(1)} %get-tuple-element.34), channel_id=1, source_target_pairs={{0,48},{4,52},{8,56},{12,60},{17,33},{21,37},{25,41},{29,45},{97,8... | collective-permute-start | bytes 811016 | tf_op jit(solution)/shard_map/ppermute | solution.py:561
  52.4 0.7 collective-permute-start.12
  53.7 1.4 %collective-permute-start.13 = (f32[8,256]{1,0:T(8,128)S(1)}, f32[8,256]{1,0:T(8,128)S(1)}, u32[]{:S(2)}, u32[]{:S(2)}) collective-permute-start(f32[8,256]{1,0:T(8,128)S(1)} %get-tuple-element.43.refs_3_), channel_id=1, source_target_pairs={{64,48},{68,52},{72,56},{76,60},{81,33},{85,37},{89,41},{93,45},{6... | collective-permute-start | bytes 24584 | tf_op jit(solution)/shard_map/ppermute | solution.py:561
  55.7 43.8 %collective-permute-start.14 = (f32[264,256]{1,0:T(8,128)S(1)}, f32[264,256]{1,0:T(8,128)S(1)}, u32[]{:S(2)}, u32[]{:S(2)}) collective-permute-start(f32[264,256]{1,0:T(8,128)S(1)} %get-tuple-element.44), channel_id=1, source_target_pairs={{33,17},{37,21},{41,25},{45,29},{48,0},{52,4},{56,8},{60,12},{64,1... | collective-permute-start | bytes 811016 | tf_op jit(solution)/shard_map/ppermute | solution.py:561

commit v4 on v3

--- a/solution.py
+++ b/solution.py
@@ -177,7 +177,7 @@
     return energy_floor + energy_spacing * index[here("y")].astype(f32)
 
 
-STEPS = ((0, 3), (3, 7), (7, 8), (8, 16))
+STEPS = ((0, 2), (2, 7), (7, 8), (8, 16))
 OUTWARD = ((1, 5), (5, 8), (8, 16))
 
 
@@ -192,7 +192,7 @@
     refs = list(refs)
     index = refs.pop(0)
     start = refs.pop(0)
-    both, own_mine, own_sent, near_mine, near_sent = (refs.pop(0) for _ in range(5))
+    both, own_onsite, own_links, near_mine, near_sent = (refs.pop(0) for _ in range(5))
     bridge = refs.pop(0) if part > 1 else None
     wire_h, wire_m, store, last = (refs.pop(0) for _ in range(4))
     link, link_sem = (refs.pop(0), refs.pop()) if part == 0 else (None, None)
@@ -210,11 +210,12 @@
         def _():
             pltpu.make_async_copy(both.at[kind], target, sem).start()
 
-        for here_too, own, near in ((core == kind, own_mine, near_mine), (core != kind, own_sent, near_sent)):
-
-            @pl.when(own_row & (away != 0) & here_too)
-            def _():
-                pltpu.make_async_copy(own.at[jnp.maximum(away - 1, 0)], target, sem).start()
+        @pl.when(own_row & (away != 0))
+        def _():
+            source = (own_onsite, own_links)[kind].at[jnp.maximum(away - 1, 0)]
+            pltpu.make_async_copy(source, target, sem).start()
+
+        for here_too, near in ((core == kind, near_mine), (core != kind, near_sent)):
 
             @pl.when(~own_row & here_too)
             def _():
@@ -601,7 +602,10 @@
     own_row = jnp.stack([right, opposite, left])
     near_row = jnp.stack([near, along_y(near, -1), to_partner(opposite), along_y(near, 1)])
     own_sent, near_sent = across(own_row), across(near_row)
-    sets = (both, own_row, own_sent, near_row, near_sent)
+    brings_onsite = here("core") == 0
+    own_onsite = jnp.where(brings_onsite, own_row, own_sent)
+    own_links = jnp.where(brings_onsite, own_sent, own_row)
+    sets = (both, own_onsite, own_links, near_row, near_sent)
     *first, carry, link = sweep(0, energy_index, contact_rates, sets)
     bridge = moved(
         link,

time: 126 us -> 124 us (0.984)
  waiting for transfers between devices: 59.4 us -> 55.2 us
  other arithmetic: 0.13 us -> 2.28 us
    ppermute x15, waiting for transfers between devices: 59.4 us -> 55.2 us  [moved(): return lax.ppermute(value, AXES, pairs)]
    select_n x0 -> x1, other arithmetic: none -> 1.26 us  [on_device(): own_links = jnp.where(brings_onsite, own_sent, own_row)]
  transfers between devices with their start and end apart: 15 -> 15, of which waited for: 8 -> 7; matrix products, arithmetic and copies ran while one was open for 0% -> 2% of each run, Pallas kernels for 5% -> 6%
where the time goes in v4:
time: 124 us; the launch traced here: 122 us
  waiting for transfers between devices  55.2 us (45%)
  Pallas kernels  30.5 us (25%)
  starting transfers between devices  21.7 us (18%)
  blocking collectives  11.2 us (9%)
  other arithmetic  2.28 us (2%)
    ppermute x15, waiting for transfers between devices, moved(): return lax.ppermute(value, AXES, pairs)  55.2 us
    ppermute x15, starting transfers between devices, moved(): return lax.ppermute(value, AXES, pairs)  21.7 us
    pallas_call x3, Pallas kernels, outward(): pl.pallas_call(functools.partial(outward_kernel, leg, places), out_shape=...  13.2 us
    pallas_call x4, Pallas kernels, sweep(): pl.pallas_call(functools.partial(sweep_kernel, part), out_shape=tuple(out...  13.1 us
    all_to_all x1, blocking collectives, on_device(): pieces = lax.all_to_all(pieces, ('row', 'y'), 0, 0)  11.2 us
  transfers between devices with their start and end apart: 15, of which 7 were waited for; matrix products, arithmetic and copies ran while one was open for 2% of the time, Pallas kernels for 6%

profile of v4, /device:TPU:64, one launch (start us, length us, event | category | flops | bytes accessed | tf_op | source)
XLA Modules:
  0.0 122.0 jit_solution(9608946038094467182)
XLA Ops:
  0.6 2.0 %prepare.1 = (f32[2,256,256]{2,1,0:T(8,128)}, f32[256,256]{1,0:T(8,128)}) custom-call(s32[4,4]{1,0:T(4,128)} %bitcast.23, f32[256,256]{1,0:T(8,128)} %bitcast.17, f32[256,256]{1,0:T(8,128)} %bitcast.18), custom_call_target="tpu_custom_call" | custom-call | tf_op jit(solution)/shard_map/prepare/pallas_call | solution.py:443
  2.6 1.6 %collective-permute-start.1 = (f32[256,256]{1,0:T(8,128)}, f32[256,256]{1,0:T(8,128)S(1)}, u32[]{:S(2)}, u32[]{:S(2)}) collective-permute-start(f32[256,256]{1,0:T(8,128)} %get-tuple-element.30), channel_id=1, source_target_pairs={{0,4},{1,5},{4,8},{5,9},{8,12},{9,13},{12,0},{13,1},{16,20},{17,21... | collective-permute-start | bytes 786440 | tf_op jit(solution)/shard_map/ppermute | solution.py:562
  4.2 1.7 %collective-permute-start = (f32[256,256]{1,0:T(8,128)}, f32[256,256]{1,0:T(8,128)S(1)}, u32[]{:S(2)}, u32[]{:S(2)}) collective-permute-start(f32[256,256]{1,0:T(8,128)} %get-tuple-element.30), channel_id=1, source_target_pairs={{0,12},{1,13},{4,0},{5,1},{8,4},{9,5},{12,8},{13,9},{16,28},{17,29... | collective-permute-start | bytes 786440 | tf_op jit(solution)/shard_map/ppermute | solution.py:562
  5.8 1.5 %collective-permute-start.5 = (f32[256,256]{1,0:T(8,128)}, f32[256,256]{1,0:T(8,128)S(1)}, u32[]{:S(2)}, u32[]{:S(2)}) collective-permute-start(f32[256,256]{1,0:T(8,128)} %get-tuple-element.30), channel_id=1, source_target_pairs={{0,16},{1,17},{4,20},{5,21},{8,24},{9,25},{12,28},{13,29},{16,0},{... | collective-permute-start | bytes 786440 | tf_op jit(solution)/shard_map/ppermute | solution.py:562
  7.3 4.8 %collective-permute-done.1 = f32[256,256]{1,0:T(8,128)S(1)} collective-permute-done((f32[256,256]{1,0:T(8,128)}, f32[256,256]{1,0:T(8,128)S(1)}, u32[]{:S(2)}, u32[]{:S(2)}) %collective-permute-start.1) | collective-permute-done | bytes 262176 | tf_op jit(solution)/shard_map/ppermute | solution.py:562
  12.5 3.0 %collective-permute-start.3 = (f32[128,256]{1,0:T(8,128)S(1)}, f32[128,256]{1,0:T(8,128)S(1)}, u32[]{:S(2)}, u32[]{:S(2)}) collective-permute-start(f32[128,256]{1,0:T(8,128)S(1)} %slice.9), channel_id=1, source_target_pairs={{0,12},{1,13},{4,0},{5,1},{8,4},{9,5},{12,8},{13,9},{16,28},{17,29... | collective-permute-start | bytes 393224 | tf_op jit(solution)/shard_map/ppermute | solution.py:562
  15.5 3.2 %collective-permute-start.6 = (f32[256,256]{1,0:T(8,128)S(1)}, f32[256,256]{1,0:T(8,128)S(1)}, u32[]{:S(2)}, u32[]{:S(2)}) collective-permute-start(f32[256,256]{1,0:T(8,128)S(1)} %collective-permute-done.5), channel_id=1, source_target_pairs={{0,12},{1,13},{4,0},{5,1},{8,4},{9,5},{12,8},{13,9},{16,28},{17,29... | collective-permute-start | bytes 786440 | tf_op jit(solution)/shard_map/ppermute | solution.py:562
  19.0 1.6 %collective-permute-start.7 = (f32[256,256]{1,0:T(8,128)S(1)}, f32[256,256]{1,0:T(8,128)S(1)}, u32[]{:S(2)}, u32[]{:S(2)}) collective-permute-start(f32[256,256]{1,0:T(8,128)S(1)} %constant_dynamic-update-slice_fusion), channel_id=1, source_target_pairs={{0,16},{1,17},{4,20},{5,21},{8,24},{9,25},{12,28},{13,29},{16,0},{... | collective-permute-start | bytes 786440 | tf_op jit(solution)/shard_map/ppermute | solution.py:562
  21.6 1.3 %collective-permute-start.4 = (f32[3,256,256]{2,1,0:T(8,128)}, f32[3,256,256]{2,1,0:T(8,128)}, u32[]{:S(2)}, u32[]{:S(2)}) collective-permute-start(f32[3,256,256]{2,1,0:T(8,128)} %pad_maximum_fusion.1), channel_id=1, source_target_pairs={{1,0},{5,4},{9,8},{13,12},{16,17},{20,21},{24,25},{28,29},{32,33},... | collective-permute-start | bytes 2359304 | tf_op jit(solution)/shard_map/ppermute | solution.py:562
  24.0 1.5 %collective-permute-done.7 = f32[256,256]{1,0:T(8,128)S(1)} collective-permute-done((f32[256,256]{1,0:T(8,128)S(1)}, f32[256,256]{1,0:T(8,128)S(1)}, u32[]{:S(2)}, u32[]{:S(2)}) %collective-permute-start.7) | collective-permute-done | bytes 262176 | tf_op jit(solution)/shard_map/ppermute | solution.py:562
  25.6 1.4 %collective-permute-start.9 = (f32[4,256,256]{2,1,0:T(8,128)S(1)}, f32[4,256,256]{2,1,0:T(8,128)S(1)}, u32[]{:S(2)}, u32[]{:S(2)}) collective-permute-start(f32[4,256,256]{2,1,0:T(8,128)S(1)} %pad_maximum_fusion.refs_5_), channel_id=1, source_target_pairs={{1,0},{5,4},{9,8},{13,12},{16,17},{20,21},{24,25},{28,29},{32,33},... | collective-permute-start | bytes 3145736 | tf_op jit(solution)/shard_map/ppermute | solution.py:562
  27.1 1.3 %broadcast_select_fusion = (f32[3,256,256]{2,1,0:T(8,128)S(1)}, f32[3,256,256]{2,1,0:T(8,128)S(1)}) fusion(f32[3,256,256]{2,1,0:T(8,128)} %collective-permute-done.4, pred[]{:T(512)S(6)} %eq.3, f32[1,256,256]{2,1,0:T(8,128)S(1)} %bitcast.12, f32[1,256,256]{2,1,0:T(8,128)S(1)} %bitcast.16, f32[1,256,256]{2,1,0:T(8,128)S(1)} %bitcast.14), kind=kLoop, calls=%fused_computation.2 | loop fusion | flops 786432 | bytes 3145729 | tf_op jit(solution)/shard_map/jit(_where)/select_n | solution.py:607
  28.3 2.0 %collective-permute-done.9.refs_6_ = f32[4,256,256]{2,1,0:T(8,128)S(1)} collective-permute-done((f32[4,256,256]{2,1,0:T(8,128)S(1)}, f32[4,256,256]{2,1,0:T(8,128)S(1)}, u32[]{:S(2)}, u32[]{:S(2)}) %collective-permute-start.9) | collective-permute-done | bytes 1048608 | tf_op jit(solution)/shard_map/ppermute | solution.py:562
  30.3 3.3 %sweep_0.1 = (f32[2,256,256]{2,1,0:T(8,128)S(1)}, f32[2,256,256]{2,1,0:T(8,128)S(1)}, f32[2,2,256,256]{3,2,1,0:T(8,128)S(1)}, f32[2,256,256]{2,1,0:T(8,128)S(1)}, f32[256,256]{1,0:T(8,128)S(1)}) custom-call(s32[4]{0:T(128)S(1)} %copy-done.2, f32[2,256]{1,0:T(2,128)S(1)} %copy-done.1, f32[2,256,256]{2,1,0:T(8,128)S(1)} %copy-done, ...), custom_call_target="tpu_custom_call" | custom-call | flops 2800000000 | bytes 2097152 | tf_op jit(solution)/shard_map/sweep_0/pallas_call | solution.py:472
  33.6 2.1 %collective-permute-start.10 = (f32[256,256]{1,0:T(8,128)S(1)}, f32[256,256]{1,0:T(8,128)S(1)}, u32[]{:S(2)}, u32[]{:S(2)}) collective-permute-start(f32[256,256]{1,0:T(8,128)S(1)} %get-tuple-element.33.refs_6_), channel_id=1, source_target_pairs={{0,48},{4,52},{8,56},{12,60},{17,33},{21,37},{25,41},{29,45},{33,8... | collective-permute-start | bytes 786440 | tf_op jit(solution)/shard_map/ppermute | solution.py:562
  35.7 7.0 %sweep_1.1 = (f32[5,256,256]{2,1,0:T(8,128)S(1)}, f32[5,256,256]{2,1,0:T(8,128)S(1)}, f32[5,2,256,256]{3,2,1,0:T(8,128)S(1)}, f32[2,256,256]{2,1,0:T(8,128)S(1)}) custom-call(s32[4]{0:T(128)S(1)} %copy-done.2, f32[2,256,256]{2,1,0:T(8,128)S(1)} %get-tuple-element.31.refs_1_, f32[2,256,256]{2,1,0:T(8,128)S(1)} %copy-done, ...), custom_call_target="tpu_custom_call" | custom-call | flops 7000000000 | bytes 5242880 | tf_op jit(solution)/shard_map/sweep_1/pallas_call | solution.py:472
  42.8 1.9 %sweep_2.1 = (f32[1,256,256]{2,1,0:T(8,128)S(1)}, f32[1,256,256]{2,1,0:T(8,128)}, f32[1,2,256,256]{3,2,1,0:T(8,128)S(1)}, f32[264,256]{1,0:T(8,128)S(1)}) custom-call(s32[4]{0:T(128)S(1)} %copy-done.2, f32[2,256,256]{2,1,0:T(8,128)S(1)} %get-tuple-element.32.refs_1_, f32[2,256,256]{2,1,0:T(8,128)S(1)} %copy-done, ...), custom_call_target="tpu_custom_call" | custom-call | flops 1400000000 | bytes 1048576 | tf_op jit(solution)/shard_map/sweep_2/pallas_call | solution.py:472
  44.6 1.3 %collective-permute-start.11 = (f32[264,256]{1,0:T(8,128)S(1)}, f32[264,256]{1,0:T(8,128)S(1)}, u32[]{:S(2)}, u32[]{:S(2)}) collective-permute-start(f32[264,256]{1,0:T(8,128)S(1)} %get-tuple-element.34), channel_id=1, source_target_pairs={{0,48},{4,52},{8,56},{12,60},{17,33},{21,37},{25,41},{29,45},{97,8... | collective-permute-start | bytes 811016 | tf_op jit(solution)/shard_map/ppermute | solution.py:562
  46.0 3.9 %collective-permute-done.11.refs_1_ = f32[264,256]{1,0:T(8,128)S(1)} collective-permute-done((f32[264,256]{1,0:T(8,128)S(1)}, f32[264,256]{1,0:T(8,128)S(1)}, u32[]{:S(2)}, u32[]{:S(2)}) %collective-permute-start.11) | collective-permute-done | bytes 270368 | tf_op jit(solution)/shard_map/ppermute | solution.py:562
  54.4 1.3 %collective-permute-start.14 = (f32[264,256]{1,0:T(8,128)S(1)}, f32[264,256]{1,0:T(8,128)S(1)}, u32[]{:S(2)}, u32[]{:S(2)}) collective-permute-start(f32[264,256]{1,0:T(8,128)S(1)} %get-tuple-element.44), channel_id=1, source_target_pairs={{33,17},{37,21},{41,25},{45,29},{48,0},{52,4},{56,8},{60,12},{64,1... | collective-permute-start | bytes 811016 | tf_op jit(solution)/shard_map/ppermute | solution.py:562
  55.7 41.6 %collective-permute-done.14.refs_1_ = f32[264,256]{1,0:T(8,128)S(1)} collective-permute-done((f32[264,256]{1,0:T(8,128)S(1)}, f32[264,256]{1,0:T(8,128)S(1)}, u32[]{:S(2)}, u32[]{:S(2)}) %collective-permute-start.14) | collective-permute-done | bytes 270368 | tf_op jit(solution)/shard_map/ppermute | solution.py:562
  97.3 11.9 %outward_2.1 = f32[8,8,256]{2,1,0:T(8,128)S(1)} custom-call(s32[4]{0:T(128)S(1)} %copy-done.2, f32[264,256]{1,0:T(8,128)S(1)} %collective-permute-done.14.refs_1_, f32[16,1,256]{2,1,0:T(1,128)S(1)} %get-tuple-element.45.refs_2_, f32[8,256]{1,0:T(8,128)S(1)} %get-tuple-element.43.refs_3_, f32[8,256]{1,0:T(8,128)S(1)} %collective-permute-done.13.refs_4_, ...), custom_call_target="tpu_custom_call" | custom-call | flops 13440000000 | bytes 10066329 | tf_op jit(solution)/shard_map/outward_2/pallas_call | solution.py:518
  109.2 11.2 %all_to_all.5.pieces = f32[8,8,256]{2,1,0:T(8,128)} all-to-all(f32[8,8,256]{2,1,0:T(8,128)S(1)} %outward_2.1), channel_id=1, replica_groups=mesh['half'=2,'pair'=2,'row'=2,'y'=4,'plane'=2,'core'=2] {'row','y'}, dimensions={0} | all-to-all | bytes 131072 | tf_op jit(solution)/shard_map/all_to_all | solution.py:630
  120.4 1.5 %deal.1 = (f32[4,256]{1,0:T(4,128)}, f32[4]{0:T(128)}) custom-call(f32[8,8,256]{2,1,0:T(8,128)} %all_to_all.5.pieces), custom_call_target="tpu_custom_call" | custom-call | tf_op jit(solution)/shard_map/deal/pallas_call | solution.py:538
  (30 shorter events, 7.3 us)
Async XLA Ops:
  2.6 9.5 %collective-permute-start.1 = (f32[256,256]{1,0:T(8,128)}, f32[256,256]{1,0:T(8,128)S(1)}, u32[]{:S(2)}, u32[]{:S(2)}) collective-permute-start(f32[256,256]{1,0:T(8,128)} %get-tuple-element.30), channel_id=1, source_target_pairs={{0,4},{1,5},{4,8},{5,9},{8,12},{9,13},{12,0},{13,1},{16,20},{17,21... | collective-permute-start | bytes 786440 | tf_op jit(solution)/shard_map/ppermute | solution.py:562
  4.2 8.3 %collective-permute-start = (f32[256,256]{1,0:T(8,128)}, f32[256,256]{1,0:T(8,128)S(1)}, u32[]{:S(2)}, u32[]{:S(2)}) collective-permute-start(f32[256,256]{1,0:T(8,128)} %get-tuple-element.30), channel_id=1, source_target_pairs={{0,12},{1,13},{4,0},{5,1},{8,4},{9,5},{12,8},{13,9},{16,28},{17,29... | collective-permute-start | bytes 786440 | tf_op jit(solution)/shard_map/ppermute | solution.py:562
  5.8 9.7 %collective-permute-start.5 = (f32[256,256]{1,0:T(8,128)}, f32[256,256]{1,0:T(8,128)S(1)}, u32[]{:S(2)}, u32[]{:S(2)}) collective-permute-start(f32[256,256]{1,0:T(8,128)} %get-tuple-element.30), channel_id=1, source_target_pairs={{0,16},{1,17},{4,20},{5,21},{8,24},{9,25},{12,28},{13,29},{16,0},{... | collective-permute-start | bytes 786440 | tf_op jit(solution)/shard_map/ppermute | solution.py:562
  12.1 6.8 %collective-permute-start.2 = (f32[128,256]{1,0:T(8,128)S(1)}, f32[128,256]{1,0:T(8,128)S(1)}, u32[]{:S(2)}, u32[]{:S(2)}) collective-permute-start(f32[128,256]{1,0:T(8,128)S(1)} %slice.8), channel_id=1, source_target_pairs={{0,4},{1,5},{4,8},{5,9},{8,12},{9,13},{12,0},{13,1},{16,20},{17,21... | collective-permute-start | bytes 393224 | tf_op jit(solution)/shard_map/ppermute | solution.py:562
  12.5 6.5 %collective-permute-start.3 = (f32[128,256]{1,0:T(8,128)S(1)}, f32[128,256]{1,0:T(8,128)S(1)}, u32[]{:S(2)}, u32[]{:S(2)}) collective-permute-start(f32[128,256]{1,0:T(8,128)S(1)} %slice.9), channel_id=1, source_target_pairs={{0,12},{1,13},{4,0},{5,1},{8,4},{9,5},{12,8},{13,9},{16,28},{17,29... | collective-permute-start | bytes 393224 | tf_op jit(solution)/shard_map/ppermute | solution.py:562
  15.5 8.5 %collective-permute-start.8 = (f32[256,256]{1,0:T(8,128)S(1)}, f32[256,256]{1,0:T(8,128)S(1)}, u32[]{:S(2)}, u32[]{:S(2)}) collective-permute-start(f32[256,256]{1,0:T(8,128)S(1)} %collective-permute-done.5), channel_id=1, source_target_pairs={{0,4},{1,5},{4,8},{5,9},{8,12},{9,13},{12,0},{13,1},{16,20},{17,21... | collective-permute-start | bytes 786440 | tf_op jit(solution)/shard_map/ppermute | solution.py:562
  15.5 8.5 %collective-permute-start.6 = (f32[256,256]{1,0:T(8,128)S(1)}, f32[256,256]{1,0:T(8,128)S(1)}, u32[]{:S(2)}, u32[]{:S(2)}) collective-permute-start(f32[256,256]{1,0:T(8,128)S(1)} %collective-permute-done.5), channel_id=1, source_target_pairs={{0,12},{1,13},{4,0},{5,1},{8,4},{9,5},{12,8},{13,9},{16,28},{17,29... | collective-permute-start | bytes 786440 | tf_op jit(solution)/shard_map/ppermute | solution.py:562
  19.0 6.5 %collective-permute-start.7 = (f32[256,256]{1,0:T(8,128)S(1)}, f32[256,256]{1,0:T(8,128)S(1)}, u32[]{:S(2)}, u32[]{:S(2)}) collective-permute-start(f32[256,256]{1,0:T(8,128)S(1)} %constant_dynamic-update-slice_fusion), channel_id=1, source_target_pairs={{0,16},{1,17},{4,20},{5,21},{8,24},{9,25},{12,28},{13,29},{16,0},{... | collective-permute-start | bytes 786440 | tf_op jit(solution)/shard_map/ppermute | solution.py:562
  21.6 5.5 %collective-permute-start.4 = (f32[3,256,256]{2,1,0:T(8,128)}, f32[3,256,256]{2,1,0:T(8,128)}, u32[]{:S(2)}, u32[]{:S(2)}) collective-permute-start(f32[3,256,256]{2,1,0:T(8,128)} %pad_maximum_fusion.1), channel_id=1, source_target_pairs={{1,0},{5,4},{9,8},{13,12},{16,17},{20,21},{24,25},{28,29},{32,33},... | collective-permute-start | bytes 2359304 | tf_op jit(solution)/shard_map/ppermute | solution.py:562
  25.6 4.7 %copy-start = (f32[2,256,256]{2,1,0:T(8,128)S(1)}, f32[2,256,256]{2,1,0:T(8,128)}, u32[]{:S(2)}) copy-start(f32[2,256,256]{2,1,0:T(8,128)} %get-tuple-element.29.refs_2_) | copy-start | bytes 1572868
  25.6 4.7 %copy-start.1 = (f32[2,256]{1,0:T(2,128)S(1)}, f32[2,256]{1,0:T(2,128)}, u32[]{:S(2)}) copy-start(f32[2,256]{1,0:T(2,128)} %refs_1_.1) | copy-start | bytes 6148
  25.6 4.7 %copy-start.2 = (s32[4]{0:T(128)S(1)}, s32[4]{0:T(128)}, u32[]{:S(2)}) copy-start(s32[4]{0:T(128)} %refs_0_.13) | copy-start | bytes 52
  25.6 4.7 %collective-permute-start.9 = (f32[4,256,256]{2,1,0:T(8,128)S(1)}, f32[4,256,256]{2,1,0:T(8,128)S(1)}, u32[]{:S(2)}, u32[]{:S(2)}) collective-permute-start(f32[4,256,256]{2,1,0:T(8,128)S(1)} %pad_maximum_fusion.refs_5_), channel_id=1, source_target_pairs={{1,0},{5,4},{9,8},{13,12},{16,17},{20,21},{24,25},{28,29},{32,33},... | collective-permute-start | bytes 3145736 | tf_op jit(solution)/shard_map/ppermute | solution.py:562
  33.6 9.2 %collective-permute-start.10 = (f32[256,256]{1,0:T(8,128)S(1)}, f32[256,256]{1,0:T(8,128)S(1)}, u32[]{:S(2)}, u32[]{:S(2)}) collective-permute-start(f32[256,256]{1,0:T(8,128)S(1)} %get-tuple-element.33.refs_6_), channel_id=1, source_target_pairs={{0,48},{4,52},{8,56},{12,60},{17,33},{21,37},{25,41},{29,45},{33,8... | collective-permute-start | bytes 786440 | tf_op jit(solution)/shard_map/ppermute | solution.py:562
  44.6 5.3 %collective-permute-start.11 = (f32[264,256]{1,0:T(8,128)S(1)}, f32[264,256]{1,0:T(8,128)S(1)}, u32[]{:S(2)}, u32[]{:S(2)}) collective-permute-start(f32[264,256]{1,0:T(8,128)S(1)} %get-tuple-element.34), channel_id=1, source_target_pairs={{0,48},{4,52},{8,56},{12,60},{17,33},{21,37},{25,41},{29,45},{97,8... | collective-permute-start | bytes 811016 | tf_op jit(solution)/shard_map/ppermute | solution.py:562
  50.8 0.7 collective-permute-start.12
  52.4 1.4 %collective-permute-start.13 = (f32[8,256]{1,0:T(8,128)S(1)}, f32[8,256]{1,0:T(8,128)S(1)}, u32[]{:S(2)}, u32[]{:S(2)}) collective-permute-start(f32[8,256]{1,0:T(8,128)S(1)} %get-tuple-element.43.refs_3_), channel_id=1, source_target_pairs={{64,48},{68,52},{72,56},{76,60},{81,33},{85,37},{89,41},{93,45},{6... | collective-permute-start | bytes 24584 | tf_op jit(solution)/shard_map/ppermute | solution.py:562
  54.4 42.9 %collective-permute-start.14 = (f32[264,256]{1,0:T(8,128)S(1)}, f32[264,256]{1,0:T(8,128)S(1)}, u32[]{:S(2)}, u32[]{:S(2)}) collective-permute-start(f32[264,256]{1,0:T(8,128)S(1)} %get-tuple-element.44), channel_id=1, source_target_pairs={{33,17},{37,21},{41,25},{45,29},{48,0},{52,4},{56,8},{60,12},{64,1... | collective-permute-start | bytes 811016 | tf_op jit(solution)/shard_map/ppermute | solution.py:562

commit v5 on v4

--- a/solution.py
+++ b/solution.py
@@ -177,7 +177,7 @@
     return energy_floor + energy_spacing * index[here("y")].astype(f32)
 
 
-STEPS = ((0, 2), (2, 7), (7, 8), (8, 16))
+STEPS = ((0, 7), (7, 8), (8, 16))
 OUTWARD = ((1, 5), (5, 8), (8, 16))
 
 
@@ -193,18 +193,15 @@
     index = refs.pop(0)
     start = refs.pop(0)
     both, own_onsite, own_links, near_mine, near_sent = (refs.pop(0) for _ in range(5))
-    bridge = refs.pop(0) if part > 1 else None
+    bridge = refs.pop(0) if part else None
     wire_h, wire_m, store, last = (refs.pop(0) for _ in range(4))
-    link, link_sem = (refs.pop(0), refs.pop()) if part == 0 else (None, None)
     hbuf, mbuf, sbuf, in_sem, out_sem = refs
     half, y, core = here("half"), here("y"), here("core")
     energy = energy_of(index)
 
     def start_from(chunk, column, kind, target, sem):
-        start_row(core == (0 if chunk in (0, 3) else 1), column, kind, target, sem)
-
-    def start_row(own_row, column, kind, target, sem):
         away = lax.rem(column - y + 4, 4)
+        own_row = core == (0 if chunk in (0, 3) else 1)
 
         @pl.when(own_row & (away == 0))
         def _():
@@ -221,12 +218,7 @@
             def _():
                 pltpu.make_async_copy(near.at[away], target, sem).start()
 
-    if part == 0:
-        @pl.when(on_task())
-        def _():
-            start_row(lax.rem(here("x"), 2) == 1, 3, 1, link, link_sem.at[0])
-
-    @pl.when(on_task() & (is_outer() if part < 3 else ~is_outer()))
+    @pl.when(on_task() & (is_outer() if part < 2 else ~is_outer()))
     def _():
         for n in range(count):
             t = first + n
@@ -249,7 +241,7 @@
         if part == 0:
             sbuf[0, 0] = jnp.zeros((W, W), f32)
             sbuf[0, 1] = jnp.where(eye_mask(), -0.5 * start[pl.ds(half, 1), :], 0.0)
-        elif part < 3:
+        elif part == 1:
             sbuf[0] = start[...]
         else:
             sbuf[0, 0], sbuf[0, 1] = unpack(start[...])
@@ -274,19 +266,13 @@
             return 0
 
         lax.fori_loop(0, count, one, 0)
-        if part > 1:
+        if part:
             last[...] = pack(sbuf[count, 0], sbuf[count, 1])
         else:
             last[...] = sbuf[count]
         for n in range(count):
             for copy in kept(n):
                 copy.wait()
-
-    if part == 0:
-
-        @pl.when(on_task())
-        def _():
-            pltpu.make_async_copy(both.at[1], link, link_sem.at[0]).wait()
 
 
 def middle_kernel(index, arrived, wire_h, wire_m, store, carried, crossing, spectrum, hbuf, mbuf, sbuf, in_sem):
@@ -328,7 +314,7 @@
     start = refs.pop(0)
     earlier = refs.pop(0)
     totals = [refs.pop(0) for _ in range(2)] if leg else None
-    links = [refs.pop(0) for _ in range(2)] if leg == 1 else None
+    links = [refs.pop(0) for _ in range(3)] if leg == 1 else None
     kept = {place: refs.pop(0) for place in places}
     outs = [refs.pop(0) for _ in range(1 if leg == 2 else 2)]
     hbuf, mbuf, sbuf, carried, spectra, in_sem = refs
@@ -343,11 +329,17 @@
             pltpu.make_async_copy(kept[0, k].at[at_n], hbuf.at[n], in_sem.at[n, 0]).start()
             pltpu.make_async_copy(kept[2, k].at[at_n], sbuf.at[n], in_sem.at[n, 2]).start()
             if t == 7:
-                for side in range(2):
-
-                    @pl.when(half == side)
+                away = lax.rem(7 - here("y"), 4)
+                upper, brings = half != 0, here("core") != 0
+                for wanted, source in (
+                    (~upper, links[0]),
+                    (upper & brings, links[1]),
+                    (upper & ~brings, links[2].at[away]),
+                ):
+
+                    @pl.when(wanted)
                     def _():
-                        pltpu.make_async_copy(links[side], mbuf.at[n], in_sem.at[n, 1]).start()
+                        pltpu.make_async_copy(source, mbuf.at[n], in_sem.at[n, 1]).start()
 
             elif t < 15:
                 k, at_n = kept_at(14 - t)
@@ -456,7 +448,7 @@
     if bridge is not None:
         arrays.append(bridge)
     outs = [shape(count, W, W), shape(count, W, W), shape(count, 2, W, W)]
-    outs.append(shape(2 * H2 + 8, W) if part > 1 else shape(2, W, W))
+    outs.append(shape(2 * H2 + 8, W) if part else shape(2, W, W))
     specs = [anywhere(), anywhere(), anywhere(), vmem()]
     scratch = [
         pltpu.VMEM((count, W, W), f32),
@@ -465,10 +457,6 @@
         pltpu.SemaphoreType.DMA((count, 2)),
         pltpu.SemaphoreType.DMA((count, 3)),
     ]
-    if part == 0:
-        outs.append(shape(W, W))
-        specs.append(anywhere())
-        scratch.append(pltpu.SemaphoreType.DMA((1,)))
     return pl.pallas_call(
         functools.partial(sweep_kernel, part),
         out_shape=tuple(outs),
@@ -606,17 +594,19 @@
     own_onsite = jnp.where(brings_onsite, own_row, own_sent)
     own_links = jnp.where(brings_onsite, own_sent, own_row)
     sets = (both, own_onsite, own_links, near_row, near_sent)
-    *first, carry, link = sweep(0, energy_index, contact_rates, sets)
+    x, y = here("x"), here("y")
+    row_links = jnp.where(lax.rem(x, 2) == 1, jnp.concatenate([mine[None], own_row], axis=0), near_row)
+    link = lax.dynamic_index_in_dim(row_links, lax.rem(7 - y, 4), 0, keepdims=False)
     bridge = moved(
         link,
-        lambda half, x, y, core: (half if x < 2 else 1, 3 - x, y, core),
-        lambda half, x, y, core: is_task(half, x, y, core) and not (half == 1 and x >= 2),
+        lambda half, x, y, core: (half if x < 2 else 1, 3 - x, y, 0 if x in (0, 3) else 1),
+        lambda half, x, y, core: core == 1 and not (half == 1 and x >= 2),
     )
-    *second, carry = sweep(1, energy_index, carry, sets)
-    *edge, leaving = sweep(2, energy_index, carry, sets, bridge)
+    *first, carry = sweep(0, energy_index, contact_rates, sets)
+    *edge, leaving = sweep(1, energy_index, carry, sets, bridge)
     arrived = to_next(leaving, outer_task)
-    *inner, leaving = sweep(3, energy_index, arrived, sets, bridge)
-    kept = [first, second, edge, inner]
+    *inner, leaving = sweep(2, energy_index, arrived, sets, bridge)
+    kept = [first, edge, inner]
     arrived = to_other_half(leaving, inner_task)
     carry, total, earlier = middle(energy_index, arrived, *inner)
     sent_total = to_other_half(
@@ -624,7 +614,7 @@
     )
     totals = [total, sent_total]
     carry, earlier = outward(0, energy_index, carry, earlier, [], [], kept)
-    leaving, earlier = outward(1, energy_index, carry, earlier, totals, [bridge, link], kept)
+    leaving, earlier = outward(1, energy_index, carry, earlier, totals, [bridge, link, near_sent], kept)
     arrived = to_next(leaving, inner_task)
     (pieces,) = outward(2, energy_index, arrived, earlier, totals, [], kept)
     pieces = lax.all_to_all(pieces, ("row", "y"), 0, 0)

time: 124 us -> 121 us (0.976)
  starting transfers between devices: 21.7 us -> 20.2 us
  waiting for transfers between devices: 55.2 us -> 53.9 us
    ppermute x15, starting transfers between devices: 21.7 us -> 20.2 us  [moved(): return lax.ppermute(value, AXES, pairs)]
    ppermute x15, waiting for transfers between devices: 55.2 us -> 53.9 us  [moved(): return lax.ppermute(value, AXES, pairs)]
    pallas_call x4 -> x3, Pallas kernels: 13.1 us -> 12.4 us  [sweep(): pl.pallas_call(functools.partial(sweep_kernel, part), out_shape=tuple(out...]
  transfers between devices with their start and end apart: 15 -> 15, of which waited for: 7 -> 8; matrix products, arithmetic and copies ran while one was open for 2% -> 2% of each run, Pallas kernels for 6% -> 9%
where the time goes in v5:
time: 121 us; the launch traced here: 119 us
  waiting for transfers between devices  53.9 us (45%)
  Pallas kernels  29.9 us (25%)
  starting transfers between devices  20.2 us (17%)
  blocking collectives  11.2 us (9%)
  other arithmetic  2.39 us (2%)
    ppermute x15, waiting for transfers between devices, moved(): return lax.ppermute(value, AXES, pairs)  53.9 us
    ppermute x15, starting transfers between devices, moved(): return lax.ppermute(value, AXES, pairs)  20.2 us
    pallas_call x3, Pallas kernels, outward(): pl.pallas_call(functools.partial(outward_kernel, leg, places), out_shape=...  13.2 us
    pallas_call x3, Pallas kernels, sweep(): pl.pallas_call(functools.partial(sweep_kernel, part), out_shape=tuple(out...  12.4 us
    all_to_all x1, blocking collectives, on_device(): pieces = lax.all_to_all(pieces, ('row', 'y'), 0, 0)  11.2 us
  transfers between devices with their start and end apart: 15, of which 8 were waited for; matrix products, arithmetic and copies ran while one was open for 2% of the time, Pallas kernels for 9%

profile of v5, /device:TPU:64, one launch (start us, length us, event | category | flops | bytes accessed | tf_op | source)
XLA Modules:
  0.0 118.8 jit_solution(3419523158906974617)
XLA Ops:
  0.6 2.0 %prepare.1 = (f32[2,256,256]{2,1,0:T(8,128)}, f32[256,256]{1,0:T(8,128)}) custom-call(s32[4,4]{1,0:T(4,128)} %bitcast.30, f32[256,256]{1,0:T(8,128)} %bitcast.23, f32[256,256]{1,0:T(8,128)} %bitcast.24), custom_call_target="tpu_custom_call" | custom-call | tf_op jit(solution)/shard_map/prepare/pallas_call | solution.py:435
  2.6 1.6 %collective-permute-start.1 = (f32[256,256]{1,0:T(8,128)}, f32[256,256]{1,0:T(8,128)S(1)}, u32[]{:S(2)}, u32[]{:S(2)}) collective-permute-start(f32[256,256]{1,0:T(8,128)} %get-tuple-element.25), channel_id=1, source_target_pairs={{0,4},{1,5},{4,8},{5,9},{8,12},{9,13},{12,0},{13,1},{16,20},{17,21... | collective-permute-start | bytes 786440 | tf_op jit(solution)/shard_map/ppermute | solution.py:550
  4.2 1.7 %collective-permute-start = (f32[256,256]{1,0:T(8,128)}, f32[256,256]{1,0:T(8,128)S(1)}, u32[]{:S(2)}, u32[]{:S(2)}) collective-permute-start(f32[256,256]{1,0:T(8,128)} %get-tuple-element.25), channel_id=1, source_target_pairs={{0,12},{1,13},{4,0},{5,1},{8,4},{9,5},{12,8},{13,9},{16,28},{17,29... | collective-permute-start | bytes 786440 | tf_op jit(solution)/shard_map/ppermute | solution.py:550
  5.8 1.5 %collective-permute-start.5 = (f32[256,256]{1,0:T(8,128)}, f32[256,256]{1,0:T(8,128)S(1)}, u32[]{:S(2)}, u32[]{:S(2)}) collective-permute-start(f32[256,256]{1,0:T(8,128)} %get-tuple-element.25), channel_id=1, source_target_pairs={{0,16},{1,17},{4,20},{5,21},{8,24},{9,25},{12,28},{13,29},{16,0},{... | collective-permute-start | bytes 786440 | tf_op jit(solution)/shard_map/ppermute | solution.py:550
  7.3 4.8 %collective-permute-done.1 = f32[256,256]{1,0:T(8,128)S(1)} collective-permute-done((f32[256,256]{1,0:T(8,128)}, f32[256,256]{1,0:T(8,128)S(1)}, u32[]{:S(2)}, u32[]{:S(2)}) %collective-permute-start.1) | collective-permute-done | bytes 262176 | tf_op jit(solution)/shard_map/ppermute | solution.py:550
  12.5 3.0 %collective-permute-start.3 = (f32[128,256]{1,0:T(8,128)S(1)}, f32[128,256]{1,0:T(8,128)S(1)}, u32[]{:S(2)}, u32[]{:S(2)}) collective-permute-start(f32[128,256]{1,0:T(8,128)S(1)} %slice.9), channel_id=1, source_target_pairs={{0,12},{1,13},{4,0},{5,1},{8,4},{9,5},{12,8},{13,9},{16,28},{17,29... | collective-permute-start | bytes 393224 | tf_op jit(solution)/shard_map/ppermute | solution.py:550
  15.6 3.2 %collective-permute-start.6 = (f32[256,256]{1,0:T(8,128)S(1)}, f32[256,256]{1,0:T(8,128)S(1)}, u32[]{:S(2)}, u32[]{:S(2)}) collective-permute-start(f32[256,256]{1,0:T(8,128)S(1)} %collective-permute-done.5), channel_id=1, source_target_pairs={{0,12},{1,13},{4,0},{5,1},{8,4},{9,5},{12,8},{13,9},{16,28},{17,29... | collective-permute-start | bytes 786440 | tf_op jit(solution)/shard_map/ppermute | solution.py:550
  19.1 1.6 %collective-permute-start.7 = (f32[256,256]{1,0:T(8,128)S(1)}, f32[256,256]{1,0:T(8,128)S(1)}, u32[]{:S(2)}, u32[]{:S(2)}) collective-permute-start(f32[256,256]{1,0:T(8,128)S(1)} %constant_dynamic-update-slice_fusion), channel_id=1, source_target_pairs={{0,16},{1,17},{4,20},{5,21},{8,24},{9,25},{12,28},{13,29},{16,0},{... | collective-permute-start | bytes 786440 | tf_op jit(solution)/shard_map/ppermute | solution.py:550
  20.6 0.9 pad_maximum_fusion.1
  21.6 1.3 %collective-permute-start.4 = (f32[3,256,256]{2,1,0:T(8,128)}, f32[3,256,256]{2,1,0:T(8,128)}, u32[]{:S(2)}, u32[]{:S(2)}) collective-permute-start(f32[3,256,256]{2,1,0:T(8,128)} %pad_maximum_fusion.1), channel_id=1, source_target_pairs={{1,0},{5,4},{9,8},{13,12},{16,17},{20,21},{24,25},{28,29},{32,33},... | collective-permute-start | bytes 2359304 | tf_op jit(solution)/shard_map/ppermute | solution.py:550
  22.9 1.2 collective-permute-done.8
  24.0 1.5 %collective-permute-done.7 = f32[256,256]{1,0:T(8,128)S(1)} collective-permute-done((f32[256,256]{1,0:T(8,128)S(1)}, f32[256,256]{1,0:T(8,128)S(1)}, u32[]{:S(2)}, u32[]{:S(2)}) %collective-permute-start.7) | collective-permute-done | bytes 262176 | tf_op jit(solution)/shard_map/ppermute | solution.py:550
  25.6 1.3 %collective-permute-start.9 = (f32[4,256,256]{2,1,0:T(8,128)S(1)}, f32[4,256,256]{2,1,0:T(8,128)S(1)}, u32[]{:S(2)}, u32[]{:S(2)}) collective-permute-start(f32[4,256,256]{2,1,0:T(8,128)S(1)} %pad_maximum_fusion.refs_5_), channel_id=1, source_target_pairs={{1,0},{5,4},{9,8},{13,12},{16,17},{20,21},{24,25},{28,29},{32,33},... | collective-permute-start | bytes 3145736 | tf_op jit(solution)/shard_map/ppermute | solution.py:550
  27.9 1.3 %broadcast_select_fusion = (f32[3,256,256]{2,1,0:T(8,128)S(1)}, f32[3,256,256]{2,1,0:T(8,128)S(1)}) fusion(f32[3,256,256]{2,1,0:T(8,128)} %collective-permute-done.4, pred[]{:T(512)S(6)} %eq.6, f32[1,256,256]{2,1,0:T(8,128)S(1)} %bitcast.16, f32[1,256,256]{2,1,0:T(8,128)S(1)} %bitcast.22, f32[1,256,256]{2,1,0:T(8,128)S(1)} %bitcast.19), kind=kLoop, calls=%fused_computation.6 | loop fusion | flops 786432 | bytes 3145729 | tf_op jit(solution)/shard_map/jit(_where)/select_n | solution.py:595
  29.2 1.0 collective-permute-done.9.refs_6_.refs_7_
  30.2 9.6 %sweep_0.1 = (f32[7,256,256]{2,1,0:T(8,128)S(1)}, f32[7,256,256]{2,1,0:T(8,128)S(1)}, f32[7,2,256,256]{3,2,1,0:T(8,128)S(1)}, f32[2,256,256]{2,1,0:T(8,128)S(1)}) custom-call(s32[4]{0:T(128)S(1)} %copy-done.2, f32[2,256]{1,0:T(2,128)S(1)} %copy-done.1, f32[2,256,256]{2,1,0:T(8,128)S(1)} %copy-done, f32[3,256,256]{2,1,0:T(8,128)S(1)} %get-tuple-element.47.refs_3_, ...), custom_call_target="tpu_custom_call" | custom-call | flops 9799999488 | bytes 7340032 | tf_op jit(solution)/shard_map/sweep_0/pallas_call | solution.py:460
  39.8 1.9 %sweep_1.1 = (f32[1,256,256]{2,1,0:T(8,128)S(1)}, f32[1,256,256]{2,1,0:T(8,128)}, f32[1,2,256,256]{3,2,1,0:T(8,128)S(1)}, f32[264,256]{1,0:T(8,128)S(1)}) custom-call(s32[4]{0:T(128)S(1)} %copy-done.2, f32[2,256,256]{2,1,0:T(8,128)S(1)} %get-tuple-element.26.refs_1_, f32[2,256,256]{2,1,0:T(8,128)S(1)} %copy-done, ...), custom_call_target="tpu_custom_call" | custom-call | flops 1400000000 | bytes 1048576 | tf_op jit(solution)/shard_map/sweep_1/pallas_call | solution.py:460
  41.7 1.3 %collective-permute-start.11 = (f32[264,256]{1,0:T(8,128)S(1)}, f32[264,256]{1,0:T(8,128)S(1)}, u32[]{:S(2)}, u32[]{:S(2)}) collective-permute-start(f32[264,256]{1,0:T(8,128)S(1)} %get-tuple-element.27), channel_id=1, source_target_pairs={{0,48},{4,52},{8,56},{12,60},{17,33},{21,37},{25,41},{29,45},{97,8... | collective-permute-start | bytes 811016 | tf_op jit(solution)/shard_map/ppermute | solution.py:550
  43.0 3.9 %collective-permute-done.11.refs_1_ = f32[264,256]{1,0:T(8,128)S(1)} collective-permute-done((f32[264,256]{1,0:T(8,128)S(1)}, f32[264,256]{1,0:T(8,128)S(1)}, u32[]{:S(2)}, u32[]{:S(2)}) %collective-permute-start.11) | collective-permute-done | bytes 270368 | tf_op jit(solution)/shard_map/ppermute | solution.py:550
  51.4 1.3 %collective-permute-start.14 = (f32[264,256]{1,0:T(8,128)S(1)}, f32[264,256]{1,0:T(8,128)S(1)}, u32[]{:S(2)}, u32[]{:S(2)}) collective-permute-start(f32[264,256]{1,0:T(8,128)S(1)} %get-tuple-element.37), channel_id=1, source_target_pairs={{33,17},{37,21},{41,25},{45,29},{48,0},{52,4},{56,8},{60,12},{64,1... | collective-permute-start | bytes 811016 | tf_op jit(solution)/shard_map/ppermute | solution.py:550
  52.7 41.3 %collective-permute-done.14.refs_1_ = f32[264,256]{1,0:T(8,128)S(1)} collective-permute-done((f32[264,256]{1,0:T(8,128)S(1)}, f32[264,256]{1,0:T(8,128)S(1)}, u32[]{:S(2)}, u32[]{:S(2)}) %collective-permute-start.14) | collective-permute-done | bytes 270368 | tf_op jit(solution)/shard_map/ppermute | solution.py:550
  94.0 11.9 %outward_2.1 = f32[8,8,256]{2,1,0:T(8,128)S(1)} custom-call(s32[4]{0:T(128)S(1)} %copy-done.2, f32[264,256]{1,0:T(8,128)S(1)} %collective-permute-done.14.refs_1_, f32[16,1,256]{2,1,0:T(1,128)S(1)} %get-tuple-element.38.refs_2_, f32[8,256]{1,0:T(8,128)S(1)} %get-tuple-element.36.refs_3_, f32[8,256]{1,0:T(8,128)S(1)} %collective-permute-done.13.refs_4_, ...), custom_call_target="tpu_custom_call" | custom-call | flops 13440000000 | bytes 10066329 | tf_op jit(solution)/shard_map/outward_2/pallas_call | solution.py:506
  105.9 11.2 %all_to_all.5.pieces = f32[8,8,256]{2,1,0:T(8,128)} all-to-all(f32[8,8,256]{2,1,0:T(8,128)S(1)} %outward_2.1), channel_id=1, replica_groups=mesh['half'=2,'pair'=2,'row'=2,'y'=4,'plane'=2,'core'=2] {'row','y'}, dimensions={0} | all-to-all | bytes 131072 | tf_op jit(solution)/shard_map/all_to_all | solution.py:620
  117.1 1.5 %deal.1 = (f32[4,256]{1,0:T(4,128)}, f32[4]{0:T(128)}) custom-call(f32[8,8,256]{2,1,0:T(8,128)} %all_to_all.5.pieces), custom_call_target="tpu_custom_call" | custom-call | tf_op jit(solution)/shard_map/deal/pallas_call | solution.py:526
  (32 shorter events, 6.1 us)
Async XLA Ops:
  2.6 9.5 %collective-permute-start.1 = (f32[256,256]{1,0:T(8,128)}, f32[256,256]{1,0:T(8,128)S(1)}, u32[]{:S(2)}, u32[]{:S(2)}) collective-permute-start(f32[256,256]{1,0:T(8,128)} %get-tuple-element.25), channel_id=1, source_target_pairs={{0,4},{1,5},{4,8},{5,9},{8,12},{9,13},{12,0},{13,1},{16,20},{17,21... | collective-permute-start | bytes 786440 | tf_op jit(solution)/shard_map/ppermute | solution.py:550
  4.2 8.3 %collective-permute-start = (f32[256,256]{1,0:T(8,128)}, f32[256,256]{1,0:T(8,128)S(1)}, u32[]{:S(2)}, u32[]{:S(2)}) collective-permute-start(f32[256,256]{1,0:T(8,128)} %get-tuple-element.25), channel_id=1, source_target_pairs={{0,12},{1,13},{4,0},{5,1},{8,4},{9,5},{12,8},{13,9},{16,28},{17,29... | collective-permute-start | bytes 786440 | tf_op jit(solution)/shard_map/ppermute | solution.py:550
  5.8 9.7 %collective-permute-start.5 = (f32[256,256]{1,0:T(8,128)}, f32[256,256]{1,0:T(8,128)S(1)}, u32[]{:S(2)}, u32[]{:S(2)}) collective-permute-start(f32[256,256]{1,0:T(8,128)} %get-tuple-element.25), channel_id=1, source_target_pairs={{0,16},{1,17},{4,20},{5,21},{8,24},{9,25},{12,28},{13,29},{16,0},{... | collective-permute-start | bytes 786440 | tf_op jit(solution)/shard_map/ppermute | solution.py:550
  12.1 6.8 %collective-permute-start.2 = (f32[128,256]{1,0:T(8,128)S(1)}, f32[128,256]{1,0:T(8,128)S(1)}, u32[]{:S(2)}, u32[]{:S(2)}) collective-permute-start(f32[128,256]{1,0:T(8,128)S(1)} %slice.8), channel_id=1, source_target_pairs={{0,4},{1,5},{4,8},{5,9},{8,12},{9,13},{12,0},{13,1},{16,20},{17,21... | collective-permute-start | bytes 393224 | tf_op jit(solution)/shard_map/ppermute | solution.py:550
  12.5 14.4 %copy-start.3 = (f32[256,256]{1,0:T(8,128)S(1)}, f32[256,256]{1,0:T(8,128)}, u32[]{:S(2)}) copy-start(f32[256,256]{1,0:T(8,128)} %get-tuple-element.25) | copy-start | bytes 786436
  12.5 6.5 %collective-permute-start.3 = (f32[128,256]{1,0:T(8,128)S(1)}, f32[128,256]{1,0:T(8,128)S(1)}, u32[]{:S(2)}, u32[]{:S(2)}) collective-permute-start(f32[128,256]{1,0:T(8,128)S(1)} %slice.9), channel_id=1, source_target_pairs={{0,12},{1,13},{4,0},{5,1},{8,4},{9,5},{12,8},{13,9},{16,28},{17,29... | collective-permute-start | bytes 393224 | tf_op jit(solution)/shard_map/ppermute | solution.py:550
  15.5 8.5 %collective-permute-start.8 = (f32[256,256]{1,0:T(8,128)S(1)}, f32[256,256]{1,0:T(8,128)S(1)}, u32[]{:S(2)}, u32[]{:S(2)}) collective-permute-start(f32[256,256]{1,0:T(8,128)S(1)} %collective-permute-done.5), channel_id=1, source_target_pairs={{0,4},{1,5},{4,8},{5,9},{8,12},{9,13},{12,0},{13,1},{16,20},{17,21... | collective-permute-start | bytes 786440 | tf_op jit(solution)/shard_map/ppermute | solution.py:550
  15.6 8.5 %collective-permute-start.6 = (f32[256,256]{1,0:T(8,128)S(1)}, f32[256,256]{1,0:T(8,128)S(1)}, u32[]{:S(2)}, u32[]{:S(2)}) collective-permute-start(f32[256,256]{1,0:T(8,128)S(1)} %collective-permute-done.5), channel_id=1, source_target_pairs={{0,12},{1,13},{4,0},{5,1},{8,4},{9,5},{12,8},{13,9},{16,28},{17,29... | collective-permute-start | bytes 786440 | tf_op jit(solution)/shard_map/ppermute | solution.py:550
  19.1 6.5 %collective-permute-start.7 = (f32[256,256]{1,0:T(8,128)S(1)}, f32[256,256]{1,0:T(8,128)S(1)}, u32[]{:S(2)}, u32[]{:S(2)}) collective-permute-start(f32[256,256]{1,0:T(8,128)S(1)} %constant_dynamic-update-slice_fusion), channel_id=1, source_target_pairs={{0,16},{1,17},{4,20},{5,21},{8,24},{9,25},{12,28},{13,29},{16,0},{... | collective-permute-start | bytes 786440 | tf_op jit(solution)/shard_map/ppermute | solution.py:550
  21.6 6.3 %collective-permute-start.4 = (f32[3,256,256]{2,1,0:T(8,128)}, f32[3,256,256]{2,1,0:T(8,128)}, u32[]{:S(2)}, u32[]{:S(2)}) collective-permute-start(f32[3,256,256]{2,1,0:T(8,128)} %pad_maximum_fusion.1), channel_id=1, source_target_pairs={{1,0},{5,4},{9,8},{13,12},{16,17},{20,21},{24,25},{28,29},{32,33},... | collective-permute-start | bytes 2359304 | tf_op jit(solution)/shard_map/ppermute | solution.py:550
  25.6 4.6 %collective-permute-start.9 = (f32[4,256,256]{2,1,0:T(8,128)S(1)}, f32[4,256,256]{2,1,0:T(8,128)S(1)}, u32[]{:S(2)}, u32[]{:S(2)}) collective-permute-start(f32[4,256,256]{2,1,0:T(8,128)S(1)} %pad_maximum_fusion.refs_5_), channel_id=1, source_target_pairs={{1,0},{5,4},{9,8},{13,12},{16,17},{20,21},{24,25},{28,29},{32,33},... | collective-permute-start | bytes 3145736 | tf_op jit(solution)/shard_map/ppermute | solution.py:550
  26.9 3.2 %copy-start = (f32[2,256,256]{2,1,0:T(8,128)S(1)}, f32[2,256,256]{2,1,0:T(8,128)}, u32[]{:S(2)}) copy-start(f32[2,256,256]{2,1,0:T(8,128)} %get-tuple-element.24.refs_2_) | copy-start | bytes 1572868
  26.9 3.2 %copy-start.1 = (f32[2,256]{1,0:T(2,128)S(1)}, f32[2,256]{1,0:T(2,128)}, u32[]{:S(2)}) copy-start(f32[2,256]{1,0:T(2,128)} %refs_1_.1) | copy-start | bytes 6148
  26.9 3.2 %copy-start.2 = (s32[4]{0:T(128)S(1)}, s32[4]{0:T(128)}, u32[]{:S(2)}) copy-start(s32[4]{0:T(128)} %refs_0_.11) | copy-start | bytes 52
  27.1 12.7 %collective-permute-start.10 = (f32[256,256]{1,0:T(8,128)S(1)}, f32[256,256]{1,0:T(8,128)S(1)}, u32[]{:S(2)}, u32[]{:S(2)}) collective-permute-start(f32[256,256]{1,0:T(8,128)S(1)} %fusion.4.refs_6_), channel_id=1, source_target_pairs={{1,48},{5,52},{9,56},{13,60},{17,33},{21,37},{25,41},{29,45},{33,8... | collective-permute-start | bytes 786440 | tf_op jit(solution)/shard_map/ppermute | solution.py:550
  41.7 5.3 %collective-permute-start.11 = (f32[264,256]{1,0:T(8,128)S(1)}, f32[264,256]{1,0:T(8,128)S(1)}, u32[]{:S(2)}, u32[]{:S(2)}) collective-permute-start(f32[264,256]{1,0:T(8,128)S(1)} %get-tuple-element.27), channel_id=1, source_target_pairs={{0,48},{4,52},{8,56},{12,60},{17,33},{21,37},{25,41},{29,45},{97,8... | collective-permute-start | bytes 811016 | tf_op jit(solution)/shard_map/ppermute | solution.py:550
  47.9 0.7 collective-permute-start.12
  49.4 1.4 %collective-permute-start.13 = (f32[8,256]{1,0:T(8,128)S(1)}, f32[8,256]{1,0:T(8,128)S(1)}, u32[]{:S(2)}, u32[]{:S(2)}) collective-permute-start(f32[8,256]{1,0:T(8,128)S(1)} %get-tuple-element.36.refs_3_), channel_id=1, source_target_pairs={{64,48},{68,52},{72,56},{76,60},{81,33},{85,37},{89,41},{93,45},{6... | collective-permute-start | bytes 24584 | tf_op jit(solution)/shard_map/ppermute | solution.py:550
  51.4 42.6 %collective-permute-start.14 = (f32[264,256]{1,0:T(8,128)S(1)}, f32[264,256]{1,0:T(8,128)S(1)}, u32[]{:S(2)}, u32[]{:S(2)}) collective-permute-start(f32[264,256]{1,0:T(8,128)S(1)} %get-tuple-element.37), channel_id=1, source_target_pairs={{33,17},{37,21},{41,25},{45,29},{48,0},{52,4},{56,8},{60,12},{64,1... | collective-permute-start | bytes 811016 | tf_op jit(solution)/shard_map/ppermute | solution.py:550

commit v6 on v5

--- a/solution.py
+++ b/solution.py
@@ -275,7 +275,7 @@
                 copy.wait()
 
 
-def middle_kernel(index, arrived, wire_h, wire_m, store, carried, crossing, spectrum, hbuf, mbuf, sbuf, in_sem):
+def middle_kernel(index, arrived, wire_h, wire_m, store, carried, crossing, hbuf, mbuf, sbuf, in_sem):
     half = here("half")
     energy = energy_of(index)
     crossing[...] = jnp.zeros((8, W), f32)
@@ -298,7 +298,6 @@
             row = crossing_row(energy, hbuf[...], sr, si, sbuf[0], sbuf[1])
             crossing[...] = jnp.broadcast_to(jnp.sum(row, axis=1, keepdims=True), (8, W))
 
-        spectrum[...] = spectral_row(energy, hbuf[...], sbuf[0] + sr, sbuf[1] + si)
         m = mbuf[...]
         lead = jnp.where(half == 0, m, m.T)
         nr, ni = chain_step(energy, hbuf[...], lead, sr, si)
@@ -306,28 +305,25 @@
         carried[1] = ni
 
 
-def outward_kernel(leg, places, *refs):
+def inner_kernel(leg, places, *refs):
     first, stop = OUTWARD[leg]
     count = stop - first
     refs = list(refs)
     index = refs.pop(0)
     start = refs.pop(0)
-    earlier = refs.pop(0)
     totals = [refs.pop(0) for _ in range(2)] if leg else None
-    links = [refs.pop(0) for _ in range(3)] if leg == 1 else None
+    links = [refs.pop(0) for _ in range(3)] if leg else None
     kept = {place: refs.pop(0) for place in places}
-    outs = [refs.pop(0) for _ in range(1 if leg == 2 else 2)]
-    hbuf, mbuf, sbuf, carried, spectra, in_sem = refs
+    leaving, entered, hbuf, mbuf, carried, in_sem, out_sem = refs
     half = here("half")
     energy = energy_of(index)
 
-    @pl.when(on_task() & (is_outer() if leg == 2 else ~is_outer()))
+    @pl.when(on_task() & ~is_outer())
     def _():
         for n in range(count):
             t = first + n
             k, at_n = kept_at(15 - t)
             pltpu.make_async_copy(kept[0, k].at[at_n], hbuf.at[n], in_sem.at[n, 0]).start()
-            pltpu.make_async_copy(kept[2, k].at[at_n], sbuf.at[n], in_sem.at[n, 2]).start()
             if t == 7:
                 away = lax.rem(7 - here("y"), 4)
                 upper, brings = half != 0, here("core") != 0
@@ -341,31 +337,67 @@
                     def _():
                         pltpu.make_async_copy(source, mbuf.at[n], in_sem.at[n, 1]).start()
 
-            elif t < 15:
+            else:
                 k, at_n = kept_at(14 - t)
                 pltpu.make_async_copy(kept[1, k].at[at_n], mbuf.at[n], in_sem.at[n, 1]).start()
-        if leg == 2:
-            carried[0], carried[1] = unpack(start[...])
+        carried[0] = start[...]
+
+        def one(n, unused):
+            pltpu.make_async_copy(hbuf.at[n], hbuf.at[n], in_sem.at[n, 0]).wait()
+            pltpu.make_async_copy(mbuf.at[n], mbuf.at[n], in_sem.at[n, 1]).wait()
+            pltpu.make_async_copy(carried.at[n], entered.at[n], out_sem.at[n]).start()
+            m = mbuf[n]
+            lead = jnp.where(half == 0, m, m.T)
+            nr, ni = chain_step(energy, hbuf[n], lead, carried[n, 0], carried[n, 1])
+            carried[n + 1, 0] = nr
+            carried[n + 1, 1] = ni
+            return 0
+
+        lax.fori_loop(0, count, one, 0)
+        if leg:
+            leaving[...] = pack(carried[count, 0], carried[count, 1], totals[0][...] + totals[1][...])
         else:
-            carried[...] = start[...]
-        if leg == 0:
-            spectra[pl.ds(jnp.where(half == 0, 15, 0), 1)] = earlier[...][None]
-        elif leg == 1:
-            spectra[...] = earlier[...]
-
-        def landed(n, link=True):
-            pltpu.make_async_copy(hbuf.at[n], hbuf.at[n], in_sem.at[n, 0]).wait()
-            pltpu.make_async_copy(sbuf.at[n], sbuf.at[n], in_sem.at[n, 2]).wait()
-            if link:
-                pltpu.make_async_copy(mbuf.at[n], mbuf.at[n], in_sem.at[n, 1]).wait()
-
-        def spectrum(n):
-            row = spectral_row(energy, hbuf[n], sbuf[n, 0] + carried[0], sbuf[n, 1] + carried[1])
-            spectra[pl.ds(jnp.where(half == 0, 15 - first - n, first + n), 1)] = row[None]
+            leaving[...] = carried[count]
+        for n in range(count):
+            pltpu.make_async_copy(carried.at[n], entered.at[n], out_sem.at[n]).wait()
+
+
+def last_kernel(places, *refs):
+    first, stop = OUTWARD[2]
+    count = stop - first
+    refs = list(refs)
+    index, start, middle_start, own_total, sent_total = (refs.pop(0) for _ in range(5))
+    entered = [refs.pop(0) for _ in range(2)]
+    kept = {place: refs.pop(0) for place in places}
+    out, hbuf, mbuf, sbuf, rbuf, spectra, in_sem = refs
+    half = here("half")
+    energy = energy_of(index)
+
+    def landed(n, kinds):
+        for kind in kinds:
+            buffer = (hbuf, mbuf, sbuf, rbuf)[kind].at[n]
+            pltpu.make_async_copy(buffer, buffer, in_sem.at[n, kind]).wait()
+
+    def spectrum(n, t, rr, ri):
+        row = spectral_row(energy, hbuf[n], sbuf[n, 0] + rr, sbuf[n, 1] + ri)
+        spectra[pl.ds(jnp.where(half == 0, 15 - t, t), 1)] = row[None]
+
+    @pl.when(on_task() & is_outer())
+    def _():
+        for n in range(count):
+            t = first + n
+            k, at_n = kept_at(15 - t)
+            pltpu.make_async_copy(kept[0, k].at[at_n], hbuf.at[n], in_sem.at[n, 0]).start()
+            pltpu.make_async_copy(kept[2, k].at[at_n], sbuf.at[n], in_sem.at[n, 2]).start()
+            if t < 15:
+                k, at_n = kept_at(14 - t)
+                pltpu.make_async_copy(kept[1, k].at[at_n], mbuf.at[n], in_sem.at[n, 1]).start()
+        carried = rbuf.at[0]
+        carried[0], carried[1] = unpack(start[...])
 
         def one(n, unused):
-            landed(n)
-            spectrum(n)
+            landed(n, (0, 1, 2))
+            spectrum(n, first + n, carried[0], carried[1])
             m = mbuf[n]
             lead = jnp.where(half == 0, m, m.T)
             nr, ni = chain_step(energy, hbuf[n], lead, carried[0], carried[1])
@@ -373,31 +405,39 @@
             carried[1] = ni
             return 0
 
-        lax.fori_loop(0, count - (leg == 2), one, 0)
-        if leg == 2:
-            landed(count - 1, False)
-            spectrum(count - 1)
-        elif leg == 1:
-            outs[0][...] = pack(carried[0], carried[1], totals[0][...] + totals[1][...])
-            outs[1][...] = spectra[...]
-        else:
-            outs[0][...] = carried[...]
-            outs[1][...] = spectra[...]
-
-    if leg == 2:
-
-        @pl.when(on_task())
-        def _():
-            @pl.when(~is_outer())
-            def _():
-                spectra[...] = earlier[...]
-
-            outer_total = start[pl.ds(2 * H2, 8), :]
-            total = jnp.where(is_outer(), outer_total, totals[0][...] + totals[1][...])
-            base = 8 * lax.axis_index("pair")
-            for place in range(8):
-                outs[0][place, pl.ds(0, 1), :] = spectra[base + place]
-                outs[0][place, pl.ds(1, 7), :] = total[1:8]
+        lax.fori_loop(0, count - 1, one, 0)
+        landed(count - 1, (0, 2))
+        spectrum(count - 1, stop - 1, carried[0], carried[1])
+
+    @pl.when(on_task() & ~is_outer())
+    def _():
+        for t in range(8):
+            k, at_n = kept_at(15 - t)
+            pltpu.make_async_copy(kept[0, k].at[at_n], hbuf.at[t], in_sem.at[t, 0]).start()
+            pltpu.make_async_copy(kept[2, k].at[at_n], sbuf.at[t], in_sem.at[t, 2]).start()
+            if t:
+                leg = 0 if t < OUTWARD[1][0] else 1
+                source = entered[leg].at[t - OUTWARD[leg][0]]
+                pltpu.make_async_copy(source, rbuf.at[t], in_sem.at[t, 3]).start()
+        rbuf[0, 0], rbuf[0, 1] = unpack(middle_start[...])
+        landed(0, (0, 2))
+        spectrum(0, 0, rbuf[0, 0], rbuf[0, 1])
+
+        def one(t, unused):
+            landed(t, (0, 2, 3))
+            spectrum(t, t, rbuf[t, 0], rbuf[t, 1])
+            return 0
+
+        lax.fori_loop(1, 8, one, 0)
+
+    @pl.when(on_task())
+    def _():
+        outer_total = start[pl.ds(2 * H2, 8), :]
+        total = jnp.where(is_outer(), outer_total, own_total[...] + sent_total[...])
+        base = 8 * lax.axis_index("pair")
+        for place in range(8):
+            out[place, pl.ds(0, 1), :] = spectra[base + place]
+            out[place, pl.ds(1, 7), :] = total[1:8]
 
 
 def deal_kernel(pieces, spectral, totals):
@@ -472,9 +512,9 @@
 def middle(index, arrived, wire_h, wire_m, store):
     return pl.pallas_call(
         middle_kernel,
-        out_shape=(shape(2, W, W), shape(8, W), shape(1, W)),
+        out_shape=(shape(2, W, W), shape(8, W)),
         in_specs=[smem(), vmem(), anywhere(), anywhere(), anywhere()],
-        out_specs=[vmem()] * 3,
+        out_specs=[vmem()] * 2,
         scratch_shapes=[
             pltpu.VMEM((W, W), f32),
             pltpu.VMEM((W, W), f32),
@@ -487,39 +527,56 @@
     )(index, arrived, wire_h, wire_m, store)
 
 
-def outward(leg, index, start, earlier, totals, links, kept):
+def inner_leg(leg, index, start, totals, links, kept):
     first, stop = OUTWARD[leg]
     count = stop - first
     places = set()
     for t in range(first, stop):
-        k = kept_at(15 - t)[0]
-        places |= {(0, k), (2, k)}
-        if t not in (7, 15):
+        places.add((0, kept_at(15 - t)[0]))
+        if t != 7:
             places.add((1, kept_at(14 - t)[0]))
     places = sorted(places)
     arrays = [*links, *(kept[k][kind] for kind, k in places)]
-    outs = {
-        0: [shape(2, W, W), shape(16, 1, W)],
-        1: [shape(2 * H2 + 8, W), shape(16, 1, W)],
-        2: [shape(8, 8, W)],
-    }[leg]
     return pl.pallas_call(
-        functools.partial(outward_kernel, leg, places),
-        out_shape=tuple(outs),
-        in_specs=[smem()] + [vmem()] * (2 + len(totals)) + [anywhere()] * len(arrays),
-        out_specs=[vmem()] * len(outs),
+        functools.partial(inner_kernel, leg, places),
+        out_shape=(shape(2 * H2 + 8, W) if leg else shape(2, W, W), shape(count, 2, W, W)),
+        in_specs=[smem()] + [vmem()] * (1 + len(totals)) + [anywhere()] * len(arrays),
+        out_specs=[vmem(), anywhere()],
+        scratch_shapes=[
+            pltpu.VMEM((count, W, W), f32),
+            pltpu.VMEM((count, W, W), f32),
+            pltpu.VMEM((count + 1, 2, W, W), f32),
+            pltpu.SemaphoreType.DMA((count, 2)),
+            pltpu.SemaphoreType.DMA((count,)),
+        ],
+        name="outward_%d" % leg,
+        compiler_params=params(),
+        cost_estimate=cost(count),
+    )(index, start, *totals, *arrays)
+
+
+def last_leg(index, start, middle_start, totals, entered, kept):
+    first, stop = OUTWARD[2]
+    count = stop - first
+    places = [(kind, k) for kind in (0, 2) for k in range(3)] + [(1, 0)]
+    arrays = [*entered, *(kept[k][kind] for kind, k in places)]
+    return pl.pallas_call(
+        functools.partial(last_kernel, places),
+        out_shape=shape(8, 8, W),
+        in_specs=[smem()] + [vmem()] * 4 + [anywhere()] * len(arrays),
+        out_specs=vmem(),
         scratch_shapes=[
             pltpu.VMEM((count, W, W), f32),
             pltpu.VMEM((count, W, W), f32),
             pltpu.VMEM((count, 2, W, W), f32),
-            pltpu.VMEM((2, W, W), f32),
+            pltpu.VMEM((count, 2, W, W), f32),
             pltpu.VMEM((16, 1, W), f32),
-            pltpu.SemaphoreType.DMA((count, 3)),
+            pltpu.SemaphoreType.DMA((count, 4)),
         ],
-        name="outward_%d" % leg,
+        name="outward_2",
         compiler_params=params(),
         cost_estimate=cost(1.2 * count),
-    )(index, start, earlier, *totals, *arrays)
+    )(index, start, middle_start, *totals, *arrays)
 
 
 def deal(pieces):
@@ -607,16 +664,17 @@
     arrived = to_next(leaving, outer_task)
     *inner, leaving = sweep(2, energy_index, arrived, sets, bridge)
     kept = [first, edge, inner]
-    arrived = to_other_half(leaving, inner_task)
-    carry, total, earlier = middle(energy_index, arrived, *inner)
+    crossed = to_other_half(leaving, inner_task)
+    carry, total = middle(energy_index, crossed, *inner)
     sent_total = to_other_half(
         total, lambda half, x, y, core: half == 1 and inner_task(half, x, y, core)
     )
     totals = [total, sent_total]
-    carry, earlier = outward(0, energy_index, carry, earlier, [], [], kept)
-    leaving, earlier = outward(1, energy_index, carry, earlier, totals, [bridge, link, near_sent], kept)
+    carry, *entered = inner_leg(0, energy_index, carry, [], [], kept)
+    leaving, later = inner_leg(1, energy_index, carry, totals, [bridge, link, near_sent], kept)
+    entered.append(later)
     arrived = to_next(leaving, inner_task)
-    (pieces,) = outward(2, energy_index, arrived, earlier, totals, [], kept)
+    pieces = last_leg(energy_index, arrived, crossed, totals, entered, kept)
     pieces = lax.all_to_all(pieces, ("row", "y"), 0, 0)
     spectral, totals = deal(pieces)
     return spectral[None], totals

time: 121 us -> 118 us (0.975); the launches traced: 119 us -> 117 us
  waiting for transfers between devices: 53.9 us -> 52.5 us
    ppermute x15, waiting for transfers between devices: 53.9 us -> 52.5 us  [moved(): return lax.ppermute(value, AXES, pairs)]
where the time goes in v6:
time: 118 us; the launch traced here: 117 us
  waiting for transfers between devices  52.5 us (44%)
  Pallas kernels  29.9 us (25%)
  starting transfers between devices  20.2 us (17%)
  blocking collectives  11.2 us (9%)
  other arithmetic  2.39 us (2%)
    ppermute x15, waiting for transfers between devices, moved(): return lax.ppermute(value, AXES, pairs)  52.5 us
    ppermute x15, starting transfers between devices, moved(): return lax.ppermute(value, AXES, pairs)  20.2 us
    pallas_call x3, Pallas kernels, sweep(): pl.pallas_call(functools.partial(sweep_kernel, part), out_shape=tuple(out...  12.4 us
    pallas_call x1, Pallas kernels, last_leg(): pl.pallas_call(functools.partial(last_kernel, places), out_shape=shape(8,...  11.9 us
    all_to_all x1, blocking collectives, on_device(): pieces = lax.all_to_all(pieces, ('row', 'y'), 0, 0)  11.2 us
  transfers between devices with their start and end apart: 15, of which 8 were waited for; matrix products, arithmetic and copies ran while one was open for 2% of the time, Pallas kernels for 9%

profile of v6, /device:TPU:64, one launch (start us, length us, event | category | flops | bytes accessed | tf_op | source)
XLA Modules:
  0.0 117.4 jit_solution(12286842058699556698)
XLA Ops:
  0.6 2.0 %prepare.1 = (f32[2,256,256]{2,1,0:T(8,128)}, f32[256,256]{1,0:T(8,128)}) custom-call(s32[4,4]{1,0:T(4,128)} %bitcast.30, f32[256,256]{1,0:T(8,128)} %bitcast.23, f32[256,256]{1,0:T(8,128)} %bitcast.24), custom_call_target="tpu_custom_call" | custom-call | tf_op jit(solution)/shard_map/prepare/pallas_call | solution.py:475
  2.6 1.6 %collective-permute-start.1 = (f32[256,256]{1,0:T(8,128)}, f32[256,256]{1,0:T(8,128)S(1)}, u32[]{:S(2)}, u32[]{:S(2)}) collective-permute-start(f32[256,256]{1,0:T(8,128)} %get-tuple-element.24), channel_id=1, source_target_pairs={{0,4},{1,5},{4,8},{5,9},{8,12},{9,13},{12,0},{13,1},{16,20},{17,21... | collective-permute-start | bytes 786440 | tf_op jit(solution)/shard_map/ppermute | solution.py:607
  4.2 1.7 %collective-permute-start = (f32[256,256]{1,0:T(8,128)}, f32[256,256]{1,0:T(8,128)S(1)}, u32[]{:S(2)}, u32[]{:S(2)}) collective-permute-start(f32[256,256]{1,0:T(8,128)} %get-tuple-element.24), channel_id=1, source_target_pairs={{0,12},{1,13},{4,0},{5,1},{8,4},{9,5},{12,8},{13,9},{16,28},{17,29... | collective-permute-start | bytes 786440 | tf_op jit(solution)/shard_map/ppermute | solution.py:607
  5.8 1.5 %collective-permute-start.5 = (f32[256,256]{1,0:T(8,128)}, f32[256,256]{1,0:T(8,128)S(1)}, u32[]{:S(2)}, u32[]{:S(2)}) collective-permute-start(f32[256,256]{1,0:T(8,128)} %get-tuple-element.24), channel_id=1, source_target_pairs={{0,16},{1,17},{4,20},{5,21},{8,24},{9,25},{12,28},{13,29},{16,0},{... | collective-permute-start | bytes 786440 | tf_op jit(solution)/shard_map/ppermute | solution.py:607
  7.3 4.8 %collective-permute-done.1 = f32[256,256]{1,0:T(8,128)S(1)} collective-permute-done((f32[256,256]{1,0:T(8,128)}, f32[256,256]{1,0:T(8,128)S(1)}, u32[]{:S(2)}, u32[]{:S(2)}) %collective-permute-start.1) | collective-permute-done | bytes 262176 | tf_op jit(solution)/shard_map/ppermute | solution.py:607
  12.6 3.0 %collective-permute-start.3 = (f32[128,256]{1,0:T(8,128)S(1)}, f32[128,256]{1,0:T(8,128)S(1)}, u32[]{:S(2)}, u32[]{:S(2)}) collective-permute-start(f32[128,256]{1,0:T(8,128)S(1)} %slice.9), channel_id=1, source_target_pairs={{0,12},{1,13},{4,0},{5,1},{8,4},{9,5},{12,8},{13,9},{16,28},{17,29... | collective-permute-start | bytes 393224 | tf_op jit(solution)/shard_map/ppermute | solution.py:607
  15.6 3.2 %collective-permute-start.6 = (f32[256,256]{1,0:T(8,128)S(1)}, f32[256,256]{1,0:T(8,128)S(1)}, u32[]{:S(2)}, u32[]{:S(2)}) collective-permute-start(f32[256,256]{1,0:T(8,128)S(1)} %collective-permute-done.5), channel_id=1, source_target_pairs={{0,12},{1,13},{4,0},{5,1},{8,4},{9,5},{12,8},{13,9},{16,28},{17,29... | collective-permute-start | bytes 786440 | tf_op jit(solution)/shard_map/ppermute | solution.py:607
  19.1 1.6 %collective-permute-start.7 = (f32[256,256]{1,0:T(8,128)S(1)}, f32[256,256]{1,0:T(8,128)S(1)}, u32[]{:S(2)}, u32[]{:S(2)}) collective-permute-start(f32[256,256]{1,0:T(8,128)S(1)} %constant_dynamic-update-slice_fusion), channel_id=1, source_target_pairs={{0,16},{1,17},{4,20},{5,21},{8,24},{9,25},{12,28},{13,29},{16,0},{... | collective-permute-start | bytes 786440 | tf_op jit(solution)/shard_map/ppermute | solution.py:607
  20.6 0.9 pad_maximum_fusion.1
  21.6 1.3 %collective-permute-start.4 = (f32[3,256,256]{2,1,0:T(8,128)}, f32[3,256,256]{2,1,0:T(8,128)}, u32[]{:S(2)}, u32[]{:S(2)}) collective-permute-start(f32[3,256,256]{2,1,0:T(8,128)} %pad_maximum_fusion.1), channel_id=1, source_target_pairs={{1,0},{5,4},{9,8},{13,12},{16,17},{20,21},{24,25},{28,29},{32,33},... | collective-permute-start | bytes 2359304 | tf_op jit(solution)/shard_map/ppermute | solution.py:607
  22.9 1.1 collective-permute-done.8
  24.0 1.5 %collective-permute-done.7 = f32[256,256]{1,0:T(8,128)S(1)} collective-permute-done((f32[256,256]{1,0:T(8,128)S(1)}, f32[256,256]{1,0:T(8,128)S(1)}, u32[]{:S(2)}, u32[]{:S(2)}) %collective-permute-start.7) | collective-permute-done | bytes 262176 | tf_op jit(solution)/shard_map/ppermute | solution.py:607
  25.6 1.3 %collective-permute-start.9 = (f32[4,256,256]{2,1,0:T(8,128)S(1)}, f32[4,256,256]{2,1,0:T(8,128)S(1)}, u32[]{:S(2)}, u32[]{:S(2)}) collective-permute-start(f32[4,256,256]{2,1,0:T(8,128)S(1)} %pad_maximum_fusion.refs_5_), channel_id=1, source_target_pairs={{1,0},{5,4},{9,8},{13,12},{16,17},{20,21},{24,25},{28,29},{32,33},... | collective-permute-start | bytes 3145736 | tf_op jit(solution)/shard_map/ppermute | solution.py:607
  27.9 1.3 %broadcast_select_fusion = (f32[3,256,256]{2,1,0:T(8,128)S(1)}, f32[3,256,256]{2,1,0:T(8,128)S(1)}) fusion(f32[3,256,256]{2,1,0:T(8,128)} %collective-permute-done.4, pred[]{:T(512)S(6)} %eq.6, f32[1,256,256]{2,1,0:T(8,128)S(1)} %bitcast.16, f32[1,256,256]{2,1,0:T(8,128)S(1)} %bitcast.22, f32[1,256,256]{2,1,0:T(8,128)S(1)} %bitcast.19), kind=kLoop, calls=%fused_computation.6 | loop fusion | flops 786432 | bytes 3145729 | tf_op jit(solution)/shard_map/jit(_where)/select_n | solution.py:652
  29.2 1.0 collective-permute-done.9.refs_6_
  30.2 9.6 %sweep_0.1 = (f32[7,256,256]{2,1,0:T(8,128)S(1)}, f32[7,256,256]{2,1,0:T(8,128)S(1)}, f32[7,2,256,256]{3,2,1,0:T(8,128)S(1)}, f32[2,256,256]{2,1,0:T(8,128)S(1)}) custom-call(s32[4]{0:T(128)S(1)} %copy-done.2, f32[2,256]{1,0:T(2,128)S(1)} %copy-done.1, f32[2,256,256]{2,1,0:T(8,128)S(1)} %copy-done, f32[3,256,256]{2,1,0:T(8,128)S(1)} %get-tuple-element.45.refs_3_, ...), custom_call_target="tpu_custom_call" | custom-call | flops 9799999488 | bytes 7340032 | tf_op jit(solution)/shard_map/sweep_0/pallas_call | solution.py:500
  39.8 1.9 %sweep_1.1 = (f32[1,256,256]{2,1,0:T(8,128)S(1)}, f32[1,256,256]{2,1,0:T(8,128)}, f32[1,2,256,256]{3,2,1,0:T(8,128)S(1)}, f32[264,256]{1,0:T(8,128)S(1)}) custom-call(s32[4]{0:T(128)S(1)} %copy-done.2, f32[2,256,256]{2,1,0:T(8,128)S(1)} %get-tuple-element.25.refs_1_, f32[2,256,256]{2,1,0:T(8,128)S(1)} %copy-done, ...), custom_call_target="tpu_custom_call" | custom-call | flops 1400000000 | bytes 1048576 | tf_op jit(solution)/shard_map/sweep_1/pallas_call | solution.py:500
  41.7 1.3 %collective-permute-start.11 = (f32[264,256]{1,0:T(8,128)S(1)}, f32[264,256]{1,0:T(8,128)S(1)}, u32[]{:S(2)}, u32[]{:S(2)}) collective-permute-start(f32[264,256]{1,0:T(8,128)S(1)} %get-tuple-element.26), channel_id=1, source_target_pairs={{0,48},{4,52},{8,56},{12,60},{17,33},{21,37},{25,41},{29,45},{97,8... | collective-permute-start | bytes 811016 | tf_op jit(solution)/shard_map/ppermute | solution.py:607
  43.0 3.9 %collective-permute-done.11.refs_1_ = f32[264,256]{1,0:T(8,128)S(1)} collective-permute-done((f32[264,256]{1,0:T(8,128)S(1)}, f32[264,256]{1,0:T(8,128)S(1)}, u32[]{:S(2)}, u32[]{:S(2)}) %collective-permute-start.11) | collective-permute-done | bytes 270368 | tf_op jit(solution)/shard_map/ppermute | solution.py:607
  51.4 1.3 %collective-permute-start.14 = (f32[264,256]{1,0:T(8,128)S(1)}, f32[264,256]{1,0:T(8,128)S(1)}, u32[]{:S(2)}, u32[]{:S(2)}) collective-permute-start(f32[264,256]{1,0:T(8,128)S(1)} %get-tuple-element.34), channel_id=1, source_target_pairs={{33,17},{37,21},{41,25},{45,29},{48,0},{52,4},{56,8},{60,12},{64,1... | collective-permute-start | bytes 811016 | tf_op jit(solution)/shard_map/ppermute | solution.py:607
  52.7 39.9 %collective-permute-done.14.refs_1_ = f32[264,256]{1,0:T(8,128)S(1)} collective-permute-done((f32[264,256]{1,0:T(8,128)S(1)}, f32[264,256]{1,0:T(8,128)S(1)}, u32[]{:S(2)}, u32[]{:S(2)}) %collective-permute-start.14) | collective-permute-done | bytes 270368 | tf_op jit(solution)/shard_map/ppermute | solution.py:607
  92.6 11.9 %outward_2.1 = f32[8,8,256]{2,1,0:T(8,128)S(1)} custom-call(s32[4]{0:T(128)S(1)} %copy-done.2, f32[264,256]{1,0:T(8,128)S(1)} %collective-permute-done.14.refs_1_, f32[264,256]{1,0:T(8,128)S(1)} %collective-permute-done.12.arrived.refs_2_, f32[8,256]{1,0:T(8,128)S(1)} %get-tuple-element.33.refs_2_.refs_3_, ...), custom_call_target="tpu_custom_call" | custom-call | flops 13440000000 | bytes 10066329 | tf_op jit(solution)/shard_map/outward_2/pallas_call | solution.py:563
  104.5 11.2 %all_to_all.5.pieces = f32[8,8,256]{2,1,0:T(8,128)} all-to-all(f32[8,8,256]{2,1,0:T(8,128)S(1)} %outward_2.1), channel_id=1, replica_groups=mesh['half'=2,'pair'=2,'row'=2,'y'=4,'plane'=2,'core'=2] {'row','y'}, dimensions={0} | all-to-all | bytes 131072 | tf_op jit(solution)/shard_map/all_to_all | solution.py:678
  115.8 1.5 %deal.1 = (f32[4,256]{1,0:T(4,128)}, f32[4]{0:T(128)}) custom-call(f32[8,8,256]{2,1,0:T(8,128)} %all_to_all.5.pieces), custom_call_target="tpu_custom_call" | custom-call | tf_op jit(solution)/shard_map/deal/pallas_call | solution.py:583
  (36 shorter events, 6.1 us)
Async XLA Ops:
  2.6 9.5 %collective-permute-start.1 = (f32[256,256]{1,0:T(8,128)}, f32[256,256]{1,0:T(8,128)S(1)}, u32[]{:S(2)}, u32[]{:S(2)}) collective-permute-start(f32[256,256]{1,0:T(8,128)} %get-tuple-element.24), channel_id=1, source_target_pairs={{0,4},{1,5},{4,8},{5,9},{8,12},{9,13},{12,0},{13,1},{16,20},{17,21... | collective-permute-start | bytes 786440 | tf_op jit(solution)/shard_map/ppermute | solution.py:607
  4.2 8.3 %collective-permute-start = (f32[256,256]{1,0:T(8,128)}, f32[256,256]{1,0:T(8,128)S(1)}, u32[]{:S(2)}, u32[]{:S(2)}) collective-permute-start(f32[256,256]{1,0:T(8,128)} %get-tuple-element.24), channel_id=1, source_target_pairs={{0,12},{1,13},{4,0},{5,1},{8,4},{9,5},{12,8},{13,9},{16,28},{17,29... | collective-permute-start | bytes 786440 | tf_op jit(solution)/shard_map/ppermute | solution.py:607
  5.8 9.7 %collective-permute-start.5 = (f32[256,256]{1,0:T(8,128)}, f32[256,256]{1,0:T(8,128)S(1)}, u32[]{:S(2)}, u32[]{:S(2)}) collective-permute-start(f32[256,256]{1,0:T(8,128)} %get-tuple-element.24), channel_id=1, source_target_pairs={{0,16},{1,17},{4,20},{5,21},{8,24},{9,25},{12,28},{13,29},{16,0},{... | collective-permute-start | bytes 786440 | tf_op jit(solution)/shard_map/ppermute | solution.py:607
  12.2 6.8 %collective-permute-start.2 = (f32[128,256]{1,0:T(8,128)S(1)}, f32[128,256]{1,0:T(8,128)S(1)}, u32[]{:S(2)}, u32[]{:S(2)}) collective-permute-start(f32[128,256]{1,0:T(8,128)S(1)} %slice.8), channel_id=1, source_target_pairs={{0,4},{1,5},{4,8},{5,9},{8,12},{9,13},{12,0},{13,1},{16,20},{17,21... | collective-permute-start | bytes 393224 | tf_op jit(solution)/shard_map/ppermute | solution.py:607
  12.5 14.4 %copy-start.5 = (f32[256,256]{1,0:T(8,128)S(1)}, f32[256,256]{1,0:T(8,128)}, u32[]{:S(2)}) copy-start(f32[256,256]{1,0:T(8,128)} %get-tuple-element.24) | copy-start | bytes 786436
  12.6 6.5 %collective-permute-start.3 = (f32[128,256]{1,0:T(8,128)S(1)}, f32[128,256]{1,0:T(8,128)S(1)}, u32[]{:S(2)}, u32[]{:S(2)}) collective-permute-start(f32[128,256]{1,0:T(8,128)S(1)} %slice.9), channel_id=1, source_target_pairs={{0,12},{1,13},{4,0},{5,1},{8,4},{9,5},{12,8},{13,9},{16,28},{17,29... | collective-permute-start | bytes 393224 | tf_op jit(solution)/shard_map/ppermute | solution.py:607
  15.6 8.5 %collective-permute-start.8 = (f32[256,256]{1,0:T(8,128)S(1)}, f32[256,256]{1,0:T(8,128)S(1)}, u32[]{:S(2)}, u32[]{:S(2)}) collective-permute-start(f32[256,256]{1,0:T(8,128)S(1)} %collective-permute-done.5), channel_id=1, source_target_pairs={{0,4},{1,5},{4,8},{5,9},{8,12},{9,13},{12,0},{13,1},{16,20},{17,21... | collective-permute-start | bytes 786440 | tf_op jit(solution)/shard_map/ppermute | solution.py:607
  15.6 8.5 %collective-permute-start.6 = (f32[256,256]{1,0:T(8,128)S(1)}, f32[256,256]{1,0:T(8,128)S(1)}, u32[]{:S(2)}, u32[]{:S(2)}) collective-permute-start(f32[256,256]{1,0:T(8,128)S(1)} %collective-permute-done.5), channel_id=1, source_target_pairs={{0,12},{1,13},{4,0},{5,1},{8,4},{9,5},{12,8},{13,9},{16,28},{17,29... | collective-permute-start | bytes 786440 | tf_op jit(solution)/shard_map/ppermute | solution.py:607
  19.1 6.5 %collective-permute-start.7 = (f32[256,256]{1,0:T(8,128)S(1)}, f32[256,256]{1,0:T(8,128)S(1)}, u32[]{:S(2)}, u32[]{:S(2)}) collective-permute-start(f32[256,256]{1,0:T(8,128)S(1)} %constant_dynamic-update-slice_fusion), channel_id=1, source_target_pairs={{0,16},{1,17},{4,20},{5,21},{8,24},{9,25},{12,28},{13,29},{16,0},{... | collective-permute-start | bytes 786440 | tf_op jit(solution)/shard_map/ppermute | solution.py:607
  21.6 6.3 %collective-permute-start.4 = (f32[3,256,256]{2,1,0:T(8,128)}, f32[3,256,256]{2,1,0:T(8,128)}, u32[]{:S(2)}, u32[]{:S(2)}) collective-permute-start(f32[3,256,256]{2,1,0:T(8,128)} %pad_maximum_fusion.1), channel_id=1, source_target_pairs={{1,0},{5,4},{9,8},{13,12},{16,17},{20,21},{24,25},{28,29},{32,33},... | collective-permute-start | bytes 2359304 | tf_op jit(solution)/shard_map/ppermute | solution.py:607
  25.6 4.6 %collective-permute-start.9 = (f32[4,256,256]{2,1,0:T(8,128)S(1)}, f32[4,256,256]{2,1,0:T(8,128)S(1)}, u32[]{:S(2)}, u32[]{:S(2)}) collective-permute-start(f32[4,256,256]{2,1,0:T(8,128)S(1)} %pad_maximum_fusion.refs_5_), channel_id=1, source_target_pairs={{1,0},{5,4},{9,8},{13,12},{16,17},{20,21},{24,25},{28,29},{32,33},... | collective-permute-start | bytes 3145736 | tf_op jit(solution)/shard_map/ppermute | solution.py:607
  26.9 3.2 %copy-start = (f32[2,256,256]{2,1,0:T(8,128)S(1)}, f32[2,256,256]{2,1,0:T(8,128)}, u32[]{:S(2)}) copy-start(f32[2,256,256]{2,1,0:T(8,128)} %get-tuple-element.23.refs_2_) | copy-start | bytes 1572868
  26.9 3.2 %copy-start.1 = (f32[2,256]{1,0:T(2,128)S(1)}, f32[2,256]{1,0:T(2,128)}, u32[]{:S(2)}) copy-start(f32[2,256]{1,0:T(2,128)} %refs_1_.1) | copy-start | bytes 6148
  27.0 3.2 %copy-start.2 = (s32[4]{0:T(128)S(1)}, s32[4]{0:T(128)}, u32[]{:S(2)}) copy-start(s32[4]{0:T(128)} %refs_0_.11) | copy-start | bytes 52
  27.1 12.7 %collective-permute-start.10 = (f32[256,256]{1,0:T(8,128)S(1)}, f32[256,256]{1,0:T(8,128)S(1)}, u32[]{:S(2)}, u32[]{:S(2)}) collective-permute-start(f32[256,256]{1,0:T(8,128)S(1)} %fusion.4.refs_5_), channel_id=1, source_target_pairs={{1,48},{5,52},{9,56},{13,60},{17,33},{21,37},{25,41},{29,45},{33,8... | collective-permute-start | bytes 786440 | tf_op jit(solution)/shard_map/ppermute | solution.py:607
  39.8 1.9 %copy-start.3 = (f32[7,256,256]{2,1,0:T(8,128)}, f32[7,256,256]{2,1,0:T(8,128)S(1)}, u32[]{:S(2)}) copy-start(f32[7,256,256]{2,1,0:T(8,128)S(1)} %get-tuple-element.41.refs_13_) | copy-start | bytes 5505028
  41.7 5.3 %collective-permute-start.11 = (f32[264,256]{1,0:T(8,128)S(1)}, f32[264,256]{1,0:T(8,128)S(1)}, u32[]{:S(2)}, u32[]{:S(2)}) collective-permute-start(f32[264,256]{1,0:T(8,128)S(1)} %get-tuple-element.26), channel_id=1, source_target_pairs={{0,48},{4,52},{8,56},{12,60},{17,33},{21,37},{25,41},{29,45},{97,8... | collective-permute-start | bytes 811016 | tf_op jit(solution)/shard_map/ppermute | solution.py:607
  47.9 0.7 collective-permute-start.12
  49.4 1.4 %collective-permute-start.13 = (f32[8,256]{1,0:T(8,128)S(1)}, f32[8,256]{1,0:T(8,128)S(1)}, u32[]{:S(2)}, u32[]{:S(2)}) collective-permute-start(f32[8,256]{1,0:T(8,128)S(1)} %get-tuple-element.33.refs_2_.refs_3_), channel_id=1, source_target_pairs={{64,48},{68,52},{72,56},{76,60},{81,33},{85,37},{89,41},{93,45},{6... | collective-permute-start | bytes 24584 | tf_op jit(solution)/shard_map/ppermute | solution.py:607
  50.8 41.8 %copy-start.4 = (f32[7,256,256]{2,1,0:T(8,128)S(1)}, f32[7,256,256]{2,1,0:T(8,128)}, u32[]{:S(2)}) copy-start(f32[7,256,256]{2,1,0:T(8,128)} %copy-done.3) | copy-start | bytes 5505028
  51.4 41.2 %collective-permute-start.14 = (f32[264,256]{1,0:T(8,128)S(1)}, f32[264,256]{1,0:T(8,128)S(1)}, u32[]{:S(2)}, u32[]{:S(2)}) collective-permute-start(f32[264,256]{1,0:T(8,128)S(1)} %get-tuple-element.34), channel_id=1, source_target_pairs={{33,17},{37,21},{41,25},{45,29},{48,0},{52,4},{56,8},{60,12},{64,1... | collective-permute-start | bytes 811016 | tf_op jit(solution)/shard_map/ppermute | solution.py:607
